TPU v7x, 512 devices: a whole 4x8x8 slice. The times are simulated.
512 devices in a mesh: segment: 16 (over z_lo, x), row: 32 (over z_hi, y, core).
Axes of the slice: x: 4, y: 8, z: 8 (z_hi: 2, z_lo: 4; z = z_hi * 4 + z_lo), core: 2. Of those that a mesh axis runs over, the one named last changes fastest.
Arguments:
- input_fields: float32 [4, 32, 32, 4, 256], P(None, 'row'), may hold values from -6 to 6
- injection_order: int32 [4], replicated, may hold values from 0 to 3, each once
- dispersion: float32 [16, 768, 256], P('segment'), may hold values from -0.21875 to 0.21875
- coupling: float32 [16, 4, 32, 32], P('segment', None, 'row'), may hold values from 0.03 to 0.2
- amplifier_gain: float32 [16, 32, 32], P('segment', 'row'), may hold values from 0.4 to 1.6
- inversion: float32 [16, 32, 32], P('segment', 'row'), may hold values from 0.3 to 1
Outputs:
- tap_fields: float32 [16, 4, 32, 32, 4, 256], P('segment', None, 'row')
Inputs may be any that keep to these rules, and one draw needn't show every extreme that they name: `injection_order`: each realization enters exactly once.
All inputs are finite; a program needn't handle non-finite values.
Results may differ from a plain program's by a relative error of at most 0.00018.
Values sent between devices are 32-bit elements; how exact they have to be, the bound alone decides.
No kernel may reach another device: no remote copies, remote signals or barrier semaphores. Data moves between devices by JAX's collectives and lax.ppermute only.
A program may use at most 64 MiB of HBM per device.

v0:
```python
import jax
import jax.numpy as jnp
from jax import lax
from jax.sharding import PartitionSpec as P

STEPS = 2


saturation_power = 1.0
loss_rate = 0.2
recovery = 0.8


def padded_2(block, sides, width):
    for axis, dim in sides:
        count = lax.axis_size(axis)
        forward = [(i, i + 1) for i in range(count - 1)]
        backward = [(target, source) for source, target in forward]
        low = lax.ppermute(
            lax.slice_in_dim(block, block.shape[dim] - width, None, axis=dim), axis, forward
        )
        high = lax.ppermute(lax.slice_in_dim(block, 0, width, axis=dim), axis, backward)
        block = jnp.concatenate([low, block, high], axis=dim)
    return block


def from_behind(block, axis, distance):
    devices = range(lax.axis_size(axis))
    route = [(i - distance, i) for i in devices if i - distance in devices]
    return lax.ppermute(block, axis, route)


def kernel_of(section_matrix):
    span = section_matrix.shape[1]
    return jnp.concatenate(
        [
            section_matrix[0:span],
            section_matrix[span : 2 * span],
            section_matrix[2 * span : 3 * span],
        ],
        axis=1,
    )


def advance(extended, kernel, bonds, gain_now, inversion_now, samples):
    own_rows = extended[1:-1]
    block_width = own_rows.shape[-1]
    leading = own_rows.shape[:-1]
    mixed = jnp.dot(own_rows.reshape(-1, block_width), kernel, precision=lax.Precision.HIGHEST)
    mixed = mixed.reshape(leading + (3 * block_width,))
    before = mixed[..., :block_width]
    middle = mixed[..., block_width : 2 * block_width]
    following = mixed[..., 2 * block_width :]
    zero_block = jnp.zeros_like(before[:, :, :1])
    dispersed = (
        middle
        + jnp.concatenate([zero_block, before[:, :, :-1]], axis=2)
        + jnp.concatenate([following[:, :, 1:], zero_block], axis=2)
    )
    padded = jnp.pad(own_rows, ((0, 0), (1, 1), (0, 0), (0, 0)))
    spread = (
        bonds[0][:, :, None, None] * extended[:-2]
        + bonds[1][:, :, None, None] * extended[2:]
        + bonds[2][:, :, None, None] * padded[:, :-2]
        + bonds[3][:, :, None, None] * padded[:, 2:]
    )
    half_width = block_width // 2
    turned = jnp.concatenate([-spread[..., half_width:], spread[..., :half_width]], axis=-1)
    linear = dispersed + turned
    mean_power = jnp.sum(linear * linear, axis=(2, 3)) / samples
    factor = jnp.exp(
        0.5 * (gain_now * inversion_now / (1.0 + mean_power / saturation_power) - loss_rate)
    )
    return factor[:, :, None, None] * linear


def with_edges(current):
    return padded_2(current, (("row", 0),), 1)


def local(input_fields, injection_order, dispersion, coupling, amplifier_gain, inversion):
    segment_count = lax.axis_size("segment")
    segment_index = lax.axis_index("segment")
    realization_count = input_fields.shape[0]
    turn_count = realization_count + segment_count - 1
    samples = input_fields.shape[3] * input_fields.shape[4] // 2
    kernel = kernel_of(dispersion[0])
    bonds = coupling[0]
    gain_now = amplifier_gain[0]
    field_shape = input_fields.shape[1:]
    tap_start = jnp.zeros(input_fields.shape, jnp.float32)
    arrived_start = jnp.zeros(field_shape, jnp.float32)

    def turn_step(turn_index, carry):
        arrived, inversion_now, tap_store = carry
        position = turn_index - segment_index
        active = jnp.logical_and(position >= 0, position < realization_count)
        chosen = injection_order[jnp.clip(turn_index, 0, realization_count - 1)]
        injected = lax.dynamic_index_in_dim(input_fields, chosen, 0, keepdims=False)
        current = jnp.where(segment_index == 0, injected, arrived)
        for step_number in range(STEPS):
            current = advance(with_edges(current), kernel, bonds, gain_now, inversion_now, samples)
        mean_power = jnp.sum(current * current, axis=(2, 3)) / samples
        updated = 1.0 - recovery * (1.0 - inversion_now / (1.0 + mean_power / saturation_power))
        inversion_now = jnp.where(active, updated, inversion_now)
        write_index = jnp.clip(position, 0, realization_count - 1)
        placed = lax.dynamic_update_index_in_dim(tap_store, current, write_index, 0)
        tap_store = jnp.where(active, placed, tap_store)
        arrived = from_behind(current, "segment", 1)
        return (arrived, inversion_now, tap_store)

    carry = lax.fori_loop(0, turn_count, turn_step, (arrived_start, inversion[0], tap_start))
    return carry[2][None]


def solution(mesh):
    return jax.shard_map(
        local,
        mesh=mesh,
        in_specs=(
            P(None, "row", None, None, None),
            P(),
            P("segment", None, None),
            P("segment", None, "row", None),
            P("segment", "row", None),
            P("segment", "row", None),
        ),
        out_specs=P("segment", None, "row", None, None, None),
        check_vma=False,
    )
```

profile of v0, /device:TPU:121, one launch (start us, length us, event | category | flops | bytes accessed | tf_op | source)
XLA Modules:
  0.0 801.4 jit_solution(17469565517220254764)
XLA Ops:
  1.9 798.7 %while.20 = (s32[]{:T(128)}, f32[1,32,4,256]{3,1,2,0:T(8,128)S(1)}, f32[1,32]{1,0:T(1,128)S(1)}, f32[4,1,32,4,256]{4,3,2,0,1:T(4,128)S(1)}, f32[1,32]{1,0:T(1,12...) while((s32[]{:T(128)}, f32[1,32,4,256]{3,1,2,0:T(8,128)S(1)}, ...), condition=%wide.region_4.5_spmd, body=%wide.region_0.4_spmd.sunk | while | flops 605061632 | bytes 10883555 | solution.py:112
  5.4 9.5 %collective-permute-start.1 = (f32[1,32,4,256]{3,1,2,0:T(8,128)S(1)}, f32[1,32,4,256]{3,1,2,0:T(8,128)S(1)}, u32[]{:S(2)}, u32[]{:S(2)}) collective-permute-start(f32[1,32,4,256]{3,1,2,0:T(8,128)S(1)} %fusion.34), channel_id=1, source_target_pairs={{0,1},{1,2},{2,3},{3,4},{4,5},{5,6},{6,7},{7,8},{8,9},{9,10},{10,1... | collective-permute-start | bytes 393224 | tf_op jit(solution)/shard_map/while/body/eval_jaxpr/ppermute | solution.py:19
  17.5 9.7 %collective-permute-done = f32[1,32,4,256]{3,1,2,0:T(8,128)S(1)} collective-permute-done((f32[1,32,4,256]{3,1,2,0:T(8,128)S(1)}, f32[1,32,4,256]{3,1,2,0:T(8,128)S(1)}, u32[]{:S(2)}, u32[]{:S(2)}) %collective-permute-start) | collective-permute-done | bytes 131104 | tf_op jit(solution)/shard_map/while/body/eval_jaxpr/ppermute | solution.py:22
  32.6 9.3 %collective-permute-done.2 = f32[1,32,4,256]{3,1,2,0:T(8,128)S(1)} collective-permute-done((f32[1,32,4,256]{3,1,2,0:T(8,128)S(1)}, f32[1,32,4,256]{3,1,2,0:T(8,128)S(1)}, u32[]{:S(2)}, u32[]{:S(2)}) %collective-permute-start.2) | collective-permute-done | bytes 131104 | tf_op jit(solution)/shard_map/while/body/eval_jaxpr/ppermute | solution.py:22
  45.6 6.2 collective-permute-done.4
  60.3 9.2 %collective-permute-done = f32[1,32,4,256]{3,1,2,0:T(8,128)S(1)} collective-permute-done((f32[1,32,4,256]{3,1,2,0:T(8,128)S(1)}, f32[1,32,4,256]{3,1,2,0:T(8,128)S(1)}, u32[]{:S(2)}, u32[]{:S(2)}) %collective-permute-start) | collective-permute-done | bytes 131104 | tf_op jit(solution)/shard_map/while/body/eval_jaxpr/ppermute | solution.py:22
  74.8 9.3 %collective-permute-done.2 = f32[1,32,4,256]{3,1,2,0:T(8,128)S(1)} collective-permute-done((f32[1,32,4,256]{3,1,2,0:T(8,128)S(1)}, f32[1,32,4,256]{3,1,2,0:T(8,128)S(1)}, u32[]{:S(2)}, u32[]{:S(2)}) %collective-permute-start.2) | collective-permute-done | bytes 131104 | tf_op jit(solution)/shard_map/while/body/eval_jaxpr/ppermute | solution.py:22
  86.7 6.0 collective-permute-done.4
  101.4 9.7 %collective-permute-done = f32[1,32,4,256]{3,1,2,0:T(8,128)S(1)} collective-permute-done((f32[1,32,4,256]{3,1,2,0:T(8,128)S(1)}, f32[1,32,4,256]{3,1,2,0:T(8,128)S(1)}, u32[]{:S(2)}, u32[]{:S(2)}) %collective-permute-start) | collective-permute-done | bytes 131104 | tf_op jit(solution)/shard_map/while/body/eval_jaxpr/ppermute | solution.py:22
  116.5 9.3 %collective-permute-done.2 = f32[1,32,4,256]{3,1,2,0:T(8,128)S(1)} collective-permute-done((f32[1,32,4,256]{3,1,2,0:T(8,128)S(1)}, f32[1,32,4,256]{3,1,2,0:T(8,128)S(1)}, u32[]{:S(2)}, u32[]{:S(2)}) %collective-permute-start.2) | collective-permute-done | bytes 131104 | tf_op jit(solution)/shard_map/while/body/eval_jaxpr/ppermute | solution.py:22
  143.1 9.7 %collective-permute-done = f32[1,32,4,256]{3,1,2,0:T(8,128)S(1)} collective-permute-done((f32[1,32,4,256]{3,1,2,0:T(8,128)S(1)}, f32[1,32,4,256]{3,1,2,0:T(8,128)S(1)}, u32[]{:S(2)}, u32[]{:S(2)}) %collective-permute-start) | collective-permute-done | bytes 131104 | tf_op jit(solution)/shard_map/while/body/eval_jaxpr/ppermute | solution.py:22
  158.1 9.3 %collective-permute-done.2 = f32[1,32,4,256]{3,1,2,0:T(8,128)S(1)} collective-permute-done((f32[1,32,4,256]{3,1,2,0:T(8,128)S(1)}, f32[1,32,4,256]{3,1,2,0:T(8,128)S(1)}, u32[]{:S(2)}, u32[]{:S(2)}) %collective-permute-start.2) | collective-permute-done | bytes 131104 | tf_op jit(solution)/shard_map/while/body/eval_jaxpr/ppermute | solution.py:22
  184.7 9.7 %collective-permute-done = f32[1,32,4,256]{3,1,2,0:T(8,128)S(1)} collective-permute-done((f32[1,32,4,256]{3,1,2,0:T(8,128)S(1)}, f32[1,32,4,256]{3,1,2,0:T(8,128)S(1)}, u32[]{:S(2)}, u32[]{:S(2)}) %collective-permute-start) | collective-permute-done | bytes 131104 | tf_op jit(solution)/shard_map/while/body/eval_jaxpr/ppermute | solution.py:22
  199.8 9.3 %collective-permute-done.2 = f32[1,32,4,256]{3,1,2,0:T(8,128)S(1)} collective-permute-done((f32[1,32,4,256]{3,1,2,0:T(8,128)S(1)}, f32[1,32,4,256]{3,1,2,0:T(8,128)S(1)}, u32[]{:S(2)}, u32[]{:S(2)}) %collective-permute-start.2) | collective-permute-done | bytes 131104 | tf_op jit(solution)/shard_map/while/body/eval_jaxpr/ppermute | solution.py:22
  211.6 5.8 collective-permute-done.4
  226.4 9.7 %collective-permute-done = f32[1,32,4,256]{3,1,2,0:T(8,128)S(1)} collective-permute-done((f32[1,32,4,256]{3,1,2,0:T(8,128)S(1)}, f32[1,32,4,256]{3,1,2,0:T(8,128)S(1)}, u32[]{:S(2)}, u32[]{:S(2)}) %collective-permute-start) | collective-permute-done | bytes 131104 | tf_op jit(solution)/shard_map/while/body/eval_jaxpr/ppermute | solution.py:22
  241.5 9.3 %collective-permute-done.2 = f32[1,32,4,256]{3,1,2,0:T(8,128)S(1)} collective-permute-done((f32[1,32,4,256]{3,1,2,0:T(8,128)S(1)}, f32[1,32,4,256]{3,1,2,0:T(8,128)S(1)}, u32[]{:S(2)}, u32[]{:S(2)}) %collective-permute-start.2) | collective-permute-done | bytes 131104 | tf_op jit(solution)/shard_map/while/body/eval_jaxpr/ppermute | solution.py:22
  268.1 9.7 %collective-permute-done = f32[1,32,4,256]{3,1,2,0:T(8,128)S(1)} collective-permute-done((f32[1,32,4,256]{3,1,2,0:T(8,128)S(1)}, f32[1,32,4,256]{3,1,2,0:T(8,128)S(1)}, u32[]{:S(2)}, u32[]{:S(2)}) %collective-permute-start) | collective-permute-done | bytes 131104 | tf_op jit(solution)/shard_map/while/body/eval_jaxpr/ppermute | solution.py:22
  283.1 9.3 %collective-permute-done.2 = f32[1,32,4,256]{3,1,2,0:T(8,128)S(1)} collective-permute-done((f32[1,32,4,256]{3,1,2,0:T(8,128)S(1)}, f32[1,32,4,256]{3,1,2,0:T(8,128)S(1)}, u32[]{:S(2)}, u32[]{:S(2)}) %collective-permute-start.2) | collective-permute-done | bytes 131104 | tf_op jit(solution)/shard_map/while/body/eval_jaxpr/ppermute | solution.py:22
  309.7 9.7 %collective-permute-done = f32[1,32,4,256]{3,1,2,0:T(8,128)S(1)} collective-permute-done((f32[1,32,4,256]{3,1,2,0:T(8,128)S(1)}, f32[1,32,4,256]{3,1,2,0:T(8,128)S(1)}, u32[]{:S(2)}, u32[]{:S(2)}) %collective-permute-start) | collective-permute-done | bytes 131104 | tf_op jit(solution)/shard_map/while/body/eval_jaxpr/ppermute | solution.py:22
  324.8 9.3 %collective-permute-done.2 = f32[1,32,4,256]{3,1,2,0:T(8,128)S(1)} collective-permute-done((f32[1,32,4,256]{3,1,2,0:T(8,128)S(1)}, f32[1,32,4,256]{3,1,2,0:T(8,128)S(1)}, u32[]{:S(2)}, u32[]{:S(2)}) %collective-permute-start.2) | collective-permute-done | bytes 131104 | tf_op jit(solution)/shard_map/while/body/eval_jaxpr/ppermute | solution.py:22
  336.6 5.8 collective-permute-done.4
  351.4 9.7 %collective-permute-done = f32[1,32,4,256]{3,1,2,0:T(8,128)S(1)} collective-permute-done((f32[1,32,4,256]{3,1,2,0:T(8,128)S(1)}, f32[1,32,4,256]{3,1,2,0:T(8,128)S(1)}, u32[]{:S(2)}, u32[]{:S(2)}) %collective-permute-start) | collective-permute-done | bytes 131104 | tf_op jit(solution)/shard_map/while/body/eval_jaxpr/ppermute | solution.py:22
  366.4 9.3 %collective-permute-done.2 = f32[1,32,4,256]{3,1,2,0:T(8,128)S(1)} collective-permute-done((f32[1,32,4,256]{3,1,2,0:T(8,128)S(1)}, f32[1,32,4,256]{3,1,2,0:T(8,128)S(1)}, u32[]{:S(2)}, u32[]{:S(2)}) %collective-permute-start.2) | collective-permute-done | bytes 131104 | tf_op jit(solution)/shard_map/while/body/eval_jaxpr/ppermute | solution.py:22
  393.0 9.7 %collective-permute-done = f32[1,32,4,256]{3,1,2,0:T(8,128)S(1)} collective-permute-done((f32[1,32,4,256]{3,1,2,0:T(8,128)S(1)}, f32[1,32,4,256]{3,1,2,0:T(8,128)S(1)}, u32[]{:S(2)}, u32[]{:S(2)}) %collective-permute-start) | collective-permute-done | bytes 131104 | tf_op jit(solution)/shard_map/while/body/eval_jaxpr/ppermute | solution.py:22
  408.1 9.3 %collective-permute-done.2 = f32[1,32,4,256]{3,1,2,0:T(8,128)S(1)} collective-permute-done((f32[1,32,4,256]{3,1,2,0:T(8,128)S(1)}, f32[1,32,4,256]{3,1,2,0:T(8,128)S(1)}, u32[]{:S(2)}, u32[]{:S(2)}) %collective-permute-start.2) | collective-permute-done | bytes 131104 | tf_op jit(solution)/shard_map/while/body/eval_jaxpr/ppermute | solution.py:22
  419.9 5.8 collective-permute-done.4
  434.7 9.7 %collective-permute-done = f32[1,32,4,256]{3,1,2,0:T(8,128)S(1)} collective-permute-done((f32[1,32,4,256]{3,1,2,0:T(8,128)S(1)}, f32[1,32,4,256]{3,1,2,0:T(8,128)S(1)}, u32[]{:S(2)}, u32[]{:S(2)}) %collective-permute-start) | collective-permute-done | bytes 131104 | tf_op jit(solution)/shard_map/while/body/eval_jaxpr/ppermute | solution.py:22
  449.7 9.3 %collective-permute-done.2 = f32[1,32,4,256]{3,1,2,0:T(8,128)S(1)} collective-permute-done((f32[1,32,4,256]{3,1,2,0:T(8,128)S(1)}, f32[1,32,4,256]{3,1,2,0:T(8,128)S(1)}, u32[]{:S(2)}, u32[]{:S(2)}) %collective-permute-start.2) | collective-permute-done | bytes 131104 | tf_op jit(solution)/shard_map/while/body/eval_jaxpr/ppermute | solution.py:22
  461.6 5.8 collective-permute-done.4
  476.4 9.7 %collective-permute-done = f32[1,32,4,256]{3,1,2,0:T(8,128)S(1)} collective-permute-done((f32[1,32,4,256]{3,1,2,0:T(8,128)S(1)}, f32[1,32,4,256]{3,1,2,0:T(8,128)S(1)}, u32[]{:S(2)}, u32[]{:S(2)}) %collective-permute-start) | collective-permute-done | bytes 131104 | tf_op jit(solution)/shard_map/while/body/eval_jaxpr/ppermute | solution.py:22
  491.4 9.3 %collective-permute-done.2 = f32[1,32,4,256]{3,1,2,0:T(8,128)S(1)} collective-permute-done((f32[1,32,4,256]{3,1,2,0:T(8,128)S(1)}, f32[1,32,4,256]{3,1,2,0:T(8,128)S(1)}, u32[]{:S(2)}, u32[]{:S(2)}) %collective-permute-start.2) | collective-permute-done | bytes 131104 | tf_op jit(solution)/shard_map/while/body/eval_jaxpr/ppermute | solution.py:22
  518.0 9.7 %collective-permute-done = f32[1,32,4,256]{3,1,2,0:T(8,128)S(1)} collective-permute-done((f32[1,32,4,256]{3,1,2,0:T(8,128)S(1)}, f32[1,32,4,256]{3,1,2,0:T(8,128)S(1)}, u32[]{:S(2)}, u32[]{:S(2)}) %collective-permute-start) | collective-permute-done | bytes 131104 | tf_op jit(solution)/shard_map/while/body/eval_jaxpr/ppermute | solution.py:22
  533.1 9.3 %collective-permute-done.2 = f32[1,32,4,256]{3,1,2,0:T(8,128)S(1)} collective-permute-done((f32[1,32,4,256]{3,1,2,0:T(8,128)S(1)}, f32[1,32,4,256]{3,1,2,0:T(8,128)S(1)}, u32[]{:S(2)}, u32[]{:S(2)}) %collective-permute-start.2) | collective-permute-done | bytes 131104 | tf_op jit(solution)/shard_map/while/body/eval_jaxpr/ppermute | solution.py:22
  544.9 5.8 collective-permute-done.4
  559.7 9.7 %collective-permute-done = f32[1,32,4,256]{3,1,2,0:T(8,128)S(1)} collective-permute-done((f32[1,32,4,256]{3,1,2,0:T(8,128)S(1)}, f32[1,32,4,256]{3,1,2,0:T(8,128)S(1)}, u32[]{:S(2)}, u32[]{:S(2)}) %collective-permute-start) | collective-permute-done | bytes 131104 | tf_op jit(solution)/shard_map/while/body/eval_jaxpr/ppermute | solution.py:22
  574.7 9.3 %collective-permute-done.2 = f32[1,32,4,256]{3,1,2,0:T(8,128)S(1)} collective-permute-done((f32[1,32,4,256]{3,1,2,0:T(8,128)S(1)}, f32[1,32,4,256]{3,1,2,0:T(8,128)S(1)}, u32[]{:S(2)}, u32[]{:S(2)}) %collective-permute-start.2) | collective-permute-done | bytes 131104 | tf_op jit(solution)/shard_map/while/body/eval_jaxpr/ppermute | solution.py:22
  601.3 9.7 %collective-permute-done = f32[1,32,4,256]{3,1,2,0:T(8,128)S(1)} collective-permute-done((f32[1,32,4,256]{3,1,2,0:T(8,128)S(1)}, f32[1,32,4,256]{3,1,2,0:T(8,128)S(1)}, u32[]{:S(2)}, u32[]{:S(2)}) %collective-permute-start) | collective-permute-done | bytes 131104 | tf_op jit(solution)/shard_map/while/body/eval_jaxpr/ppermute | solution.py:22
  616.4 9.3 %collective-permute-done.2 = f32[1,32,4,256]{3,1,2,0:T(8,128)S(1)} collective-permute-done((f32[1,32,4,256]{3,1,2,0:T(8,128)S(1)}, f32[1,32,4,256]{3,1,2,0:T(8,128)S(1)}, u32[]{:S(2)}, u32[]{:S(2)}) %collective-permute-start.2) | collective-permute-done | bytes 131104 | tf_op jit(solution)/shard_map/while/body/eval_jaxpr/ppermute | solution.py:22
  643.0 9.7 %collective-permute-done = f32[1,32,4,256]{3,1,2,0:T(8,128)S(1)} collective-permute-done((f32[1,32,4,256]{3,1,2,0:T(8,128)S(1)}, f32[1,32,4,256]{3,1,2,0:T(8,128)S(1)}, u32[]{:S(2)}, u32[]{:S(2)}) %collective-permute-start) | collective-permute-done | bytes 131104 | tf_op jit(solution)/shard_map/while/body/eval_jaxpr/ppermute | solution.py:22
  658.0 9.3 %collective-permute-done.2 = f32[1,32,4,256]{3,1,2,0:T(8,128)S(1)} collective-permute-done((f32[1,32,4,256]{3,1,2,0:T(8,128)S(1)}, f32[1,32,4,256]{3,1,2,0:T(8,128)S(1)}, u32[]{:S(2)}, u32[]{:S(2)}) %collective-permute-start.2) | collective-permute-done | bytes 131104 | tf_op jit(solution)/shard_map/while/body/eval_jaxpr/ppermute | solution.py:22
  669.9 5.8 collective-permute-done.4
  684.7 9.7 %collective-permute-done = f32[1,32,4,256]{3,1,2,0:T(8,128)S(1)} collective-permute-done((f32[1,32,4,256]{3,1,2,0:T(8,128)S(1)}, f32[1,32,4,256]{3,1,2,0:T(8,128)S(1)}, u32[]{:S(2)}, u32[]{:S(2)}) %collective-permute-start) | collective-permute-done | bytes 131104 | tf_op jit(solution)/shard_map/while/body/eval_jaxpr/ppermute | solution.py:22
  699.7 9.3 %collective-permute-done.2 = f32[1,32,4,256]{3,1,2,0:T(8,128)S(1)} collective-permute-done((f32[1,32,4,256]{3,1,2,0:T(8,128)S(1)}, f32[1,32,4,256]{3,1,2,0:T(8,128)S(1)}, u32[]{:S(2)}, u32[]{:S(2)}) %collective-permute-start.2) | collective-permute-done | bytes 131104 | tf_op jit(solution)/shard_map/while/body/eval_jaxpr/ppermute | solution.py:22
  726.3 9.7 %collective-permute-done = f32[1,32,4,256]{3,1,2,0:T(8,128)S(1)} collective-permute-done((f32[1,32,4,256]{3,1,2,0:T(8,128)S(1)}, f32[1,32,4,256]{3,1,2,0:T(8,128)S(1)}, u32[]{:S(2)}, u32[]{:S(2)}) %collective-permute-start) | collective-permute-done | bytes 131104 | tf_op jit(solution)/shard_map/while/body/eval_jaxpr/ppermute | solution.py:22
  741.4 9.3 %collective-permute-done.2 = f32[1,32,4,256]{3,1,2,0:T(8,128)S(1)} collective-permute-done((f32[1,32,4,256]{3,1,2,0:T(8,128)S(1)}, f32[1,32,4,256]{3,1,2,0:T(8,128)S(1)}, u32[]{:S(2)}, u32[]{:S(2)}) %collective-permute-start.2) | collective-permute-done | bytes 131104 | tf_op jit(solution)/shard_map/while/body/eval_jaxpr/ppermute | solution.py:22
  768.0 9.7 %collective-permute-done = f32[1,32,4,256]{3,1,2,0:T(8,128)S(1)} collective-permute-done((f32[1,32,4,256]{3,1,2,0:T(8,128)S(1)}, f32[1,32,4,256]{3,1,2,0:T(8,128)S(1)}, u32[]{:S(2)}, u32[]{:S(2)}) %collective-permute-start) | collective-permute-done | bytes 131104 | tf_op jit(solution)/shard_map/while/body/eval_jaxpr/ppermute | solution.py:22
  783.0 9.3 %collective-permute-done.2 = f32[1,32,4,256]{3,1,2,0:T(8,128)S(1)} collective-permute-done((f32[1,32,4,256]{3,1,2,0:T(8,128)S(1)}, f32[1,32,4,256]{3,1,2,0:T(8,128)S(1)}, u32[]{:S(2)}, u32[]{:S(2)}) %collective-permute-start.2) | collective-permute-done | bytes 131104 | tf_op jit(solution)/shard_map/while/body/eval_jaxpr/ppermute | solution.py:22
  (575 shorter events, 345.2 us)
Async XLA Ops:
  5.4 12.1 %collective-permute-start.1 = (f32[1,32,4,256]{3,1,2,0:T(8,128)S(1)}, f32[1,32,4,256]{3,1,2,0:T(8,128)S(1)}, u32[]{:S(2)}, u32[]{:S(2)}) collective-permute-start(f32[1,32,4,256]{3,1,2,0:T(8,128)S(1)} %fusion.34), channel_id=1, source_target_pairs={{0,1},{1,2},{2,3},{3,4},{4,5},{5,6},{6,7},{7,8},{8,9},{9,10},{10,1... | collective-permute-start | bytes 393224 | tf_op jit(solution)/shard_map/while/body/eval_jaxpr/ppermute | solution.py:19
  14.9 12.3 %collective-permute-start = (f32[1,32,4,256]{3,1,2,0:T(8,128)S(1)}, f32[1,32,4,256]{3,1,2,0:T(8,128)S(1)}, u32[]{:S(2)}, u32[]{:S(2)}) collective-permute-start(f32[1,32,4,256]{3,1,2,0:T(8,128)S(1)} %fusion.34), channel_id=1, source_target_pairs={{1,0},{2,1},{3,2},{4,3},{5,4},{6,5},{7,6},{8,7},{9,8},{10,9},{11,1... | collective-permute-start | bytes 393224 | tf_op jit(solution)/shard_map/while/body/eval_jaxpr/ppermute | solution.py:22
  29.5 12.3 %collective-permute-start.2 = (f32[1,32,4,256]{3,1,2,0:T(8,128)S(1)}, f32[1,32,4,256]{3,1,2,0:T(8,128)S(1)}, u32[]{:S(2)}, u32[]{:S(2)}) collective-permute-start(f32[1,32,4,256]{3,1,2,0:T(8,128)S(1)} %broadcast_multiply_fusion.4), channel_id=1, source_target_pairs={{1,0},{2,1},{3,2},{4,3},{5,4},{6,5},{7,6},{8,7},{9,8},{10,9},{11,1... | collective-permute-start | bytes 393224 | tf_op jit(solution)/shard_map/while/body/eval_jaxpr/ppermute | solution.py:22
  42.4 9.4 %collective-permute-start.4 = (f32[1,32,4,256]{3,1,2,0:T(8,128)S(1)}, f32[1,32,4,256]{3,1,2,0:T(8,128)S(1)}, u32[]{:S(2)}, u32[]{:S(2)}) collective-permute-start(f32[1,32,4,256]{3,1,2,0:T(8,128)S(1)} %get-tuple-element.446), channel_id=1, source_target_pairs={{0,32},{32,64},{64,96},{96,128},{128,160},{160,192},{192,224},{224... | collective-permute-start | bytes 393224 | tf_op jit(solution)/shard_map/while/body/eval_jaxpr/ppermute | solution.py:30
  57.2 12.3 %collective-permute-start = (f32[1,32,4,256]{3,1,2,0:T(8,128)S(1)}, f32[1,32,4,256]{3,1,2,0:T(8,128)S(1)}, u32[]{:S(2)}, u32[]{:S(2)}) collective-permute-start(f32[1,32,4,256]{3,1,2,0:T(8,128)S(1)} %fusion.34), channel_id=1, source_target_pairs={{1,0},{2,1},{3,2},{4,3},{5,4},{6,5},{7,6},{8,7},{9,8},{10,9},{11,1... | collective-permute-start | bytes 393224 | tf_op jit(solution)/shard_map/while/body/eval_jaxpr/ppermute | solution.py:22
  71.8 12.3 %collective-permute-start.2 = (f32[1,32,4,256]{3,1,2,0:T(8,128)S(1)}, f32[1,32,4,256]{3,1,2,0:T(8,128)S(1)}, u32[]{:S(2)}, u32[]{:S(2)}) collective-permute-start(f32[1,32,4,256]{3,1,2,0:T(8,128)S(1)} %broadcast_multiply_fusion.4), channel_id=1, source_target_pairs={{1,0},{2,1},{3,2},{4,3},{5,4},{6,5},{7,6},{8,7},{9,8},{10,9},{11,1... | collective-permute-start | bytes 393224 | tf_op jit(solution)/shard_map/while/body/eval_jaxpr/ppermute | solution.py:22
  84.6 8.1 %collective-permute-start.4 = (f32[1,32,4,256]{3,1,2,0:T(8,128)S(1)}, f32[1,32,4,256]{3,1,2,0:T(8,128)S(1)}, u32[]{:S(2)}, u32[]{:S(2)}) collective-permute-start(f32[1,32,4,256]{3,1,2,0:T(8,128)S(1)} %get-tuple-element.446), channel_id=1, source_target_pairs={{0,32},{32,64},{64,96},{96,128},{128,160},{160,192},{192,224},{224... | collective-permute-start | bytes 393224 | tf_op jit(solution)/shard_map/while/body/eval_jaxpr/ppermute | solution.py:30
  98.8 12.3 %collective-permute-start = (f32[1,32,4,256]{3,1,2,0:T(8,128)S(1)}, f32[1,32,4,256]{3,1,2,0:T(8,128)S(1)}, u32[]{:S(2)}, u32[]{:S(2)}) collective-permute-start(f32[1,32,4,256]{3,1,2,0:T(8,128)S(1)} %fusion.34), channel_id=1, source_target_pairs={{1,0},{2,1},{3,2},{4,3},{5,4},{6,5},{7,6},{8,7},{9,8},{10,9},{11,1... | collective-permute-start | bytes 393224 | tf_op jit(solution)/shard_map/while/body/eval_jaxpr/ppermute | solution.py:22
  113.5 12.3 %collective-permute-start.2 = (f32[1,32,4,256]{3,1,2,0:T(8,128)S(1)}, f32[1,32,4,256]{3,1,2,0:T(8,128)S(1)}, u32[]{:S(2)}, u32[]{:S(2)}) collective-permute-start(f32[1,32,4,256]{3,1,2,0:T(8,128)S(1)} %broadcast_multiply_fusion.4), channel_id=1, source_target_pairs={{1,0},{2,1},{3,2},{4,3},{5,4},{6,5},{7,6},{8,7},{9,8},{10,9},{11,1... | collective-permute-start | bytes 393224 | tf_op jit(solution)/shard_map/while/body/eval_jaxpr/ppermute | solution.py:22
  140.5 12.3 %collective-permute-start = (f32[1,32,4,256]{3,1,2,0:T(8,128)S(1)}, f32[1,32,4,256]{3,1,2,0:T(8,128)S(1)}, u32[]{:S(2)}, u32[]{:S(2)}) collective-permute-start(f32[1,32,4,256]{3,1,2,0:T(8,128)S(1)} %fusion.34), channel_id=1, source_target_pairs={{1,0},{2,1},{3,2},{4,3},{5,4},{6,5},{7,6},{8,7},{9,8},{10,9},{11,1... | collective-permute-start | bytes 393224 | tf_op jit(solution)/shard_map/while/body/eval_jaxpr/ppermute | solution.py:22
  155.1 12.3 %collective-permute-start.2 = (f32[1,32,4,256]{3,1,2,0:T(8,128)S(1)}, f32[1,32,4,256]{3,1,2,0:T(8,128)S(1)}, u32[]{:S(2)}, u32[]{:S(2)}) collective-permute-start(f32[1,32,4,256]{3,1,2,0:T(8,128)S(1)} %broadcast_multiply_fusion.4), channel_id=1, source_target_pairs={{1,0},{2,1},{3,2},{4,3},{5,4},{6,5},{7,6},{8,7},{9,8},{10,9},{11,1... | collective-permute-start | bytes 393224 | tf_op jit(solution)/shard_map/while/body/eval_jaxpr/ppermute | solution.py:22
  182.2 12.3 %collective-permute-start = (f32[1,32,4,256]{3,1,2,0:T(8,128)S(1)}, f32[1,32,4,256]{3,1,2,0:T(8,128)S(1)}, u32[]{:S(2)}, u32[]{:S(2)}) collective-permute-start(f32[1,32,4,256]{3,1,2,0:T(8,128)S(1)} %fusion.34), channel_id=1, source_target_pairs={{1,0},{2,1},{3,2},{4,3},{5,4},{6,5},{7,6},{8,7},{9,8},{10,9},{11,1... | collective-permute-start | bytes 393224 | tf_op jit(solution)/shard_map/while/body/eval_jaxpr/ppermute | solution.py:22
  196.8 12.3 %collective-permute-start.2 = (f32[1,32,4,256]{3,1,2,0:T(8,128)S(1)}, f32[1,32,4,256]{3,1,2,0:T(8,128)S(1)}, u32[]{:S(2)}, u32[]{:S(2)}) collective-permute-start(f32[1,32,4,256]{3,1,2,0:T(8,128)S(1)} %broadcast_multiply_fusion.4), channel_id=1, source_target_pairs={{1,0},{2,1},{3,2},{4,3},{5,4},{6,5},{7,6},{8,7},{9,8},{10,9},{11,1... | collective-permute-start | bytes 393224 | tf_op jit(solution)/shard_map/while/body/eval_jaxpr/ppermute | solution.py:22
  209.6 7.8 collective-permute-start.4
  223.8 12.3 %collective-permute-start = (f32[1,32,4,256]{3,1,2,0:T(8,128)S(1)}, f32[1,32,4,256]{3,1,2,0:T(8,128)S(1)}, u32[]{:S(2)}, u32[]{:S(2)}) collective-permute-start(f32[1,32,4,256]{3,1,2,0:T(8,128)S(1)} %fusion.34), channel_id=1, source_target_pairs={{1,0},{2,1},{3,2},{4,3},{5,4},{6,5},{7,6},{8,7},{9,8},{10,9},{11,1... | collective-permute-start | bytes 393224 | tf_op jit(solution)/shard_map/while/body/eval_jaxpr/ppermute | solution.py:22
  238.4 12.3 %collective-permute-start.2 = (f32[1,32,4,256]{3,1,2,0:T(8,128)S(1)}, f32[1,32,4,256]{3,1,2,0:T(8,128)S(1)}, u32[]{:S(2)}, u32[]{:S(2)}) collective-permute-start(f32[1,32,4,256]{3,1,2,0:T(8,128)S(1)} %broadcast_multiply_fusion.4), channel_id=1, source_target_pairs={{1,0},{2,1},{3,2},{4,3},{5,4},{6,5},{7,6},{8,7},{9,8},{10,9},{11,1... | collective-permute-start | bytes 393224 | tf_op jit(solution)/shard_map/while/body/eval_jaxpr/ppermute | solution.py:22
  265.5 12.3 %collective-permute-start = (f32[1,32,4,256]{3,1,2,0:T(8,128)S(1)}, f32[1,32,4,256]{3,1,2,0:T(8,128)S(1)}, u32[]{:S(2)}, u32[]{:S(2)}) collective-permute-start(f32[1,32,4,256]{3,1,2,0:T(8,128)S(1)} %fusion.34), channel_id=1, source_target_pairs={{1,0},{2,1},{3,2},{4,3},{5,4},{6,5},{7,6},{8,7},{9,8},{10,9},{11,1... | collective-permute-start | bytes 393224 | tf_op jit(solution)/shard_map/while/body/eval_jaxpr/ppermute | solution.py:22
  280.1 12.3 %collective-permute-start.2 = (f32[1,32,4,256]{3,1,2,0:T(8,128)S(1)}, f32[1,32,4,256]{3,1,2,0:T(8,128)S(1)}, u32[]{:S(2)}, u32[]{:S(2)}) collective-permute-start(f32[1,32,4,256]{3,1,2,0:T(8,128)S(1)} %broadcast_multiply_fusion.4), channel_id=1, source_target_pairs={{1,0},{2,1},{3,2},{4,3},{5,4},{6,5},{7,6},{8,7},{9,8},{10,9},{11,1... | collective-permute-start | bytes 393224 | tf_op jit(solution)/shard_map/while/body/eval_jaxpr/ppermute | solution.py:22
  307.1 12.3 %collective-permute-start = (f32[1,32,4,256]{3,1,2,0:T(8,128)S(1)}, f32[1,32,4,256]{3,1,2,0:T(8,128)S(1)}, u32[]{:S(2)}, u32[]{:S(2)}) collective-permute-start(f32[1,32,4,256]{3,1,2,0:T(8,128)S(1)} %fusion.34), channel_id=1, source_target_pairs={{1,0},{2,1},{3,2},{4,3},{5,4},{6,5},{7,6},{8,7},{9,8},{10,9},{11,1... | collective-permute-start | bytes 393224 | tf_op jit(solution)/shard_map/while/body/eval_jaxpr/ppermute | solution.py:22
  321.7 12.3 %collective-permute-start.2 = (f32[1,32,4,256]{3,1,2,0:T(8,128)S(1)}, f32[1,32,4,256]{3,1,2,0:T(8,128)S(1)}, u32[]{:S(2)}, u32[]{:S(2)}) collective-permute-start(f32[1,32,4,256]{3,1,2,0:T(8,128)S(1)} %broadcast_multiply_fusion.4), channel_id=1, source_target_pairs={{1,0},{2,1},{3,2},{4,3},{5,4},{6,5},{7,6},{8,7},{9,8},{10,9},{11,1... | collective-permute-start | bytes 393224 | tf_op jit(solution)/shard_map/while/body/eval_jaxpr/ppermute | solution.py:22
  334.6 7.8 collective-permute-start.4
  348.8 12.3 %collective-permute-start = (f32[1,32,4,256]{3,1,2,0:T(8,128)S(1)}, f32[1,32,4,256]{3,1,2,0:T(8,128)S(1)}, u32[]{:S(2)}, u32[]{:S(2)}) collective-permute-start(f32[1,32,4,256]{3,1,2,0:T(8,128)S(1)} %fusion.34), channel_id=1, source_target_pairs={{1,0},{2,1},{3,2},{4,3},{5,4},{6,5},{7,6},{8,7},{9,8},{10,9},{11,1... | collective-permute-start | bytes 393224 | tf_op jit(solution)/shard_map/while/body/eval_jaxpr/ppermute | solution.py:22
  363.4 12.3 %collective-permute-start.2 = (f32[1,32,4,256]{3,1,2,0:T(8,128)S(1)}, f32[1,32,4,256]{3,1,2,0:T(8,128)S(1)}, u32[]{:S(2)}, u32[]{:S(2)}) collective-permute-start(f32[1,32,4,256]{3,1,2,0:T(8,128)S(1)} %broadcast_multiply_fusion.4), channel_id=1, source_target_pairs={{1,0},{2,1},{3,2},{4,3},{5,4},{6,5},{7,6},{8,7},{9,8},{10,9},{11,1... | collective-permute-start | bytes 393224 | tf_op jit(solution)/shard_map/while/body/eval_jaxpr/ppermute | solution.py:22
  390.5 12.3 %collective-permute-start = (f32[1,32,4,256]{3,1,2,0:T(8,128)S(1)}, f32[1,32,4,256]{3,1,2,0:T(8,128)S(1)}, u32[]{:S(2)}, u32[]{:S(2)}) collective-permute-start(f32[1,32,4,256]{3,1,2,0:T(8,128)S(1)} %fusion.34), channel_id=1, source_target_pairs={{1,0},{2,1},{3,2},{4,3},{5,4},{6,5},{7,6},{8,7},{9,8},{10,9},{11,1... | collective-permute-start | bytes 393224 | tf_op jit(solution)/shard_map/while/body/eval_jaxpr/ppermute | solution.py:22
  405.1 12.3 %collective-permute-start.2 = (f32[1,32,4,256]{3,1,2,0:T(8,128)S(1)}, f32[1,32,4,256]{3,1,2,0:T(8,128)S(1)}, u32[]{:S(2)}, u32[]{:S(2)}) collective-permute-start(f32[1,32,4,256]{3,1,2,0:T(8,128)S(1)} %broadcast_multiply_fusion.4), channel_id=1, source_target_pairs={{1,0},{2,1},{3,2},{4,3},{5,4},{6,5},{7,6},{8,7},{9,8},{10,9},{11,1... | collective-permute-start | bytes 393224 | tf_op jit(solution)/shard_map/while/body/eval_jaxpr/ppermute | solution.py:22
  417.9 7.8 collective-permute-start.4
  432.1 12.3 %collective-permute-start = (f32[1,32,4,256]{3,1,2,0:T(8,128)S(1)}, f32[1,32,4,256]{3,1,2,0:T(8,128)S(1)}, u32[]{:S(2)}, u32[]{:S(2)}) collective-permute-start(f32[1,32,4,256]{3,1,2,0:T(8,128)S(1)} %fusion.34), channel_id=1, source_target_pairs={{1,0},{2,1},{3,2},{4,3},{5,4},{6,5},{7,6},{8,7},{9,8},{10,9},{11,1... | collective-permute-start | bytes 393224 | tf_op jit(solution)/shard_map/while/body/eval_jaxpr/ppermute | solution.py:22
  446.7 12.3 %collective-permute-start.2 = (f32[1,32,4,256]{3,1,2,0:T(8,128)S(1)}, f32[1,32,4,256]{3,1,2,0:T(8,128)S(1)}, u32[]{:S(2)}, u32[]{:S(2)}) collective-permute-start(f32[1,32,4,256]{3,1,2,0:T(8,128)S(1)} %broadcast_multiply_fusion.4), channel_id=1, source_target_pairs={{1,0},{2,1},{3,2},{4,3},{5,4},{6,5},{7,6},{8,7},{9,8},{10,9},{11,1... | collective-permute-start | bytes 393224 | tf_op jit(solution)/shard_map/while/body/eval_jaxpr/ppermute | solution.py:22
  473.8 12.3 %collective-permute-start = (f32[1,32,4,256]{3,1,2,0:T(8,128)S(1)}, f32[1,32,4,256]{3,1,2,0:T(8,128)S(1)}, u32[]{:S(2)}, u32[]{:S(2)}) collective-permute-start(f32[1,32,4,256]{3,1,2,0:T(8,128)S(1)} %fusion.34), channel_id=1, source_target_pairs={{1,0},{2,1},{3,2},{4,3},{5,4},{6,5},{7,6},{8,7},{9,8},{10,9},{11,1... | collective-permute-start | bytes 393224 | tf_op jit(solution)/shard_map/while/body/eval_jaxpr/ppermute | solution.py:22
  488.4 12.3 %collective-permute-start.2 = (f32[1,32,4,256]{3,1,2,0:T(8,128)S(1)}, f32[1,32,4,256]{3,1,2,0:T(8,128)S(1)}, u32[]{:S(2)}, u32[]{:S(2)}) collective-permute-start(f32[1,32,4,256]{3,1,2,0:T(8,128)S(1)} %broadcast_multiply_fusion.4), channel_id=1, source_target_pairs={{1,0},{2,1},{3,2},{4,3},{5,4},{6,5},{7,6},{8,7},{9,8},{10,9},{11,1... | collective-permute-start | bytes 393224 | tf_op jit(solution)/shard_map/while/body/eval_jaxpr/ppermute | solution.py:22
  515.4 12.3 %collective-permute-start = (f32[1,32,4,256]{3,1,2,0:T(8,128)S(1)}, f32[1,32,4,256]{3,1,2,0:T(8,128)S(1)}, u32[]{:S(2)}, u32[]{:S(2)}) collective-permute-start(f32[1,32,4,256]{3,1,2,0:T(8,128)S(1)} %fusion.34), channel_id=1, source_target_pairs={{1,0},{2,1},{3,2},{4,3},{5,4},{6,5},{7,6},{8,7},{9,8},{10,9},{11,1... | collective-permute-start | bytes 393224 | tf_op jit(solution)/shard_map/while/body/eval_jaxpr/ppermute | solution.py:22
  530.0 12.3 %collective-permute-start.2 = (f32[1,32,4,256]{3,1,2,0:T(8,128)S(1)}, f32[1,32,4,256]{3,1,2,0:T(8,128)S(1)}, u32[]{:S(2)}, u32[]{:S(2)}) collective-permute-start(f32[1,32,4,256]{3,1,2,0:T(8,128)S(1)} %broadcast_multiply_fusion.4), channel_id=1, source_target_pairs={{1,0},{2,1},{3,2},{4,3},{5,4},{6,5},{7,6},{8,7},{9,8},{10,9},{11,1... | collective-permute-start | bytes 393224 | tf_op jit(solution)/shard_map/while/body/eval_jaxpr/ppermute | solution.py:22
  542.9 7.8 collective-permute-start.4
  557.1 12.3 %collective-permute-start = (f32[1,32,4,256]{3,1,2,0:T(8,128)S(1)}, f32[1,32,4,256]{3,1,2,0:T(8,128)S(1)}, u32[]{:S(2)}, u32[]{:S(2)}) collective-permute-start(f32[1,32,4,256]{3,1,2,0:T(8,128)S(1)} %fusion.34), channel_id=1, source_target_pairs={{1,0},{2,1},{3,2},{4,3},{5,4},{6,5},{7,6},{8,7},{9,8},{10,9},{11,1... | collective-permute-start | bytes 393224 | tf_op jit(solution)/shard_map/while/body/eval_jaxpr/ppermute | solution.py:22
  571.7 12.3 %collective-permute-start.2 = (f32[1,32,4,256]{3,1,2,0:T(8,128)S(1)}, f32[1,32,4,256]{3,1,2,0:T(8,128)S(1)}, u32[]{:S(2)}, u32[]{:S(2)}) collective-permute-start(f32[1,32,4,256]{3,1,2,0:T(8,128)S(1)} %broadcast_multiply_fusion.4), channel_id=1, source_target_pairs={{1,0},{2,1},{3,2},{4,3},{5,4},{6,5},{7,6},{8,7},{9,8},{10,9},{11,1... | collective-permute-start | bytes 393224 | tf_op jit(solution)/shard_map/while/body/eval_jaxpr/ppermute | solution.py:22
  598.8 12.3 %collective-permute-start = (f32[1,32,4,256]{3,1,2,0:T(8,128)S(1)}, f32[1,32,4,256]{3,1,2,0:T(8,128)S(1)}, u32[]{:S(2)}, u32[]{:S(2)}) collective-permute-start(f32[1,32,4,256]{3,1,2,0:T(8,128)S(1)} %fusion.34), channel_id=1, source_target_pairs={{1,0},{2,1},{3,2},{4,3},{5,4},{6,5},{7,6},{8,7},{9,8},{10,9},{11,1... | collective-permute-start | bytes 393224 | tf_op jit(solution)/shard_map/while/body/eval_jaxpr/ppermute | solution.py:22
  613.4 12.3 %collective-permute-start.2 = (f32[1,32,4,256]{3,1,2,0:T(8,128)S(1)}, f32[1,32,4,256]{3,1,2,0:T(8,128)S(1)}, u32[]{:S(2)}, u32[]{:S(2)}) collective-permute-start(f32[1,32,4,256]{3,1,2,0:T(8,128)S(1)} %broadcast_multiply_fusion.4), channel_id=1, source_target_pairs={{1,0},{2,1},{3,2},{4,3},{5,4},{6,5},{7,6},{8,7},{9,8},{10,9},{11,1... | collective-permute-start | bytes 393224 | tf_op jit(solution)/shard_map/while/body/eval_jaxpr/ppermute | solution.py:22
  640.4 12.3 %collective-permute-start = (f32[1,32,4,256]{3,1,2,0:T(8,128)S(1)}, f32[1,32,4,256]{3,1,2,0:T(8,128)S(1)}, u32[]{:S(2)}, u32[]{:S(2)}) collective-permute-start(f32[1,32,4,256]{3,1,2,0:T(8,128)S(1)} %fusion.34), channel_id=1, source_target_pairs={{1,0},{2,1},{3,2},{4,3},{5,4},{6,5},{7,6},{8,7},{9,8},{10,9},{11,1... | collective-permute-start | bytes 393224 | tf_op jit(solution)/shard_map/while/body/eval_jaxpr/ppermute | solution.py:22
  655.0 12.3 %collective-permute-start.2 = (f32[1,32,4,256]{3,1,2,0:T(8,128)S(1)}, f32[1,32,4,256]{3,1,2,0:T(8,128)S(1)}, u32[]{:S(2)}, u32[]{:S(2)}) collective-permute-start(f32[1,32,4,256]{3,1,2,0:T(8,128)S(1)} %broadcast_multiply_fusion.4), channel_id=1, source_target_pairs={{1,0},{2,1},{3,2},{4,3},{5,4},{6,5},{7,6},{8,7},{9,8},{10,9},{11,1... | collective-permute-start | bytes 393224 | tf_op jit(solution)/shard_map/while/body/eval_jaxpr/ppermute | solution.py:22
  667.8 7.8 collective-permute-start.4
  682.1 12.3 %collective-permute-start = (f32[1,32,4,256]{3,1,2,0:T(8,128)S(1)}, f32[1,32,4,256]{3,1,2,0:T(8,128)S(1)}, u32[]{:S(2)}, u32[]{:S(2)}) collective-permute-start(f32[1,32,4,256]{3,1,2,0:T(8,128)S(1)} %fusion.34), channel_id=1, source_target_pairs={{1,0},{2,1},{3,2},{4,3},{5,4},{6,5},{7,6},{8,7},{9,8},{10,9},{11,1... | collective-permute-start | bytes 393224 | tf_op jit(solution)/shard_map/while/body/eval_jaxpr/ppermute | solution.py:22
  696.7 12.3 %collective-permute-start.2 = (f32[1,32,4,256]{3,1,2,0:T(8,128)S(1)}, f32[1,32,4,256]{3,1,2,0:T(8,128)S(1)}, u32[]{:S(2)}, u32[]{:S(2)}) collective-permute-start(f32[1,32,4,256]{3,1,2,0:T(8,128)S(1)} %broadcast_multiply_fusion.4), channel_id=1, source_target_pairs={{1,0},{2,1},{3,2},{4,3},{5,4},{6,5},{7,6},{8,7},{9,8},{10,9},{11,1... | collective-permute-start | bytes 393224 | tf_op jit(solution)/shard_map/while/body/eval_jaxpr/ppermute | solution.py:22
  723.7 12.3 %collective-permute-start = (f32[1,32,4,256]{3,1,2,0:T(8,128)S(1)}, f32[1,32,4,256]{3,1,2,0:T(8,128)S(1)}, u32[]{:S(2)}, u32[]{:S(2)}) collective-permute-start(f32[1,32,4,256]{3,1,2,0:T(8,128)S(1)} %fusion.34), channel_id=1, source_target_pairs={{1,0},{2,1},{3,2},{4,3},{5,4},{6,5},{7,6},{8,7},{9,8},{10,9},{11,1... | collective-permute-start | bytes 393224 | tf_op jit(solution)/shard_map/while/body/eval_jaxpr/ppermute | solution.py:22
  738.3 12.3 %collective-permute-start.2 = (f32[1,32,4,256]{3,1,2,0:T(8,128)S(1)}, f32[1,32,4,256]{3,1,2,0:T(8,128)S(1)}, u32[]{:S(2)}, u32[]{:S(2)}) collective-permute-start(f32[1,32,4,256]{3,1,2,0:T(8,128)S(1)} %broadcast_multiply_fusion.4), channel_id=1, source_target_pairs={{1,0},{2,1},{3,2},{4,3},{5,4},{6,5},{7,6},{8,7},{9,8},{10,9},{11,1... | collective-permute-start | bytes 393224 | tf_op jit(solution)/shard_map/while/body/eval_jaxpr/ppermute | solution.py:22
  751.1 7.8 collective-permute-start.4
  765.4 12.3 %collective-permute-start = (f32[1,32,4,256]{3,1,2,0:T(8,128)S(1)}, f32[1,32,4,256]{3,1,2,0:T(8,128)S(1)}, u32[]{:S(2)}, u32[]{:S(2)}) collective-permute-start(f32[1,32,4,256]{3,1,2,0:T(8,128)S(1)} %fusion.34), channel_id=1, source_target_pairs={{1,0},{2,1},{3,2},{4,3},{5,4},{6,5},{7,6},{8,7},{9,8},{10,9},{11,1... | collective-permute-start | bytes 393224 | tf_op jit(solution)/shard_map/while/body/eval_jaxpr/ppermute | solution.py:22
  780.0 12.3 %collective-permute-start.2 = (f32[1,32,4,256]{3,1,2,0:T(8,128)S(1)}, f32[1,32,4,256]{3,1,2,0:T(8,128)S(1)}, u32[]{:S(2)}, u32[]{:S(2)}) collective-permute-start(f32[1,32,4,256]{3,1,2,0:T(8,128)S(1)} %broadcast_multiply_fusion.4), channel_id=1, source_target_pairs={{1,0},{2,1},{3,2},{4,3},{5,4},{6,5},{7,6},{8,7},{9,8},{10,9},{11,1... | collective-permute-start | bytes 393224 | tf_op jit(solution)/shard_map/while/body/eval_jaxpr/ppermute | solution.py:22
  792.8 7.8 collective-permute-start.4
  (52 other events, 274.1 us)
where the time goes:
time: 805 us; the launch traced here: 801 us
  waiting for transfers between devices  471 us (59%)
  starting transfers between devices  218 us (27%)
  loops' own time  39.3 us (5%)
  local copies, waits for them, and re-layouts  34.6 us (4%)
  matrix products  21.5 us (3%)
  other arithmetic  17.2 us (2%)
    ppermute x38, waiting for transfers between devices, padded_2(): lax.ppermute(lax.slice_in_dim(block, 0, width, axis=dim), axis, backward)  361 us
    ppermute x19, waiting for transfers between devices, from_behind(): return lax.ppermute(block, axis, route)  110 us
    ppermute x38, starting transfers between devices, padded_2(): lax.ppermute(lax.slice_in_dim(block, block.shape[dim] - width, None, axis...  97.5 us
    ppermute x38, starting transfers between devices, padded_2(): lax.ppermute(lax.slice_in_dim(block, 0, width, axis=dim), axis, backward)  82.7 us
    another operation x1, loops' own time, local(): lax.fori_loop(0, turn_count, turn_step, (arrived_start, inversion[0], tap...  39.3 us
    ppermute x19, starting transfers between devices, from_behind(): return lax.ppermute(block, axis, route)  37.6 us
    dot_general x38, matrix products, advance(): jnp.dot(own_rows.reshape(-1, block_width), kernel, precision=lax.Precisio...  21.5 us
    dynamic_slice x19, local copies, waits for them, and re-layouts, turn_step(): injected = lax.dynamic_index_in_dim(input_fields, chosen, 0, keepdims=False)  17.4 us
  transfers between devices with their start and end apart: 95, of which 57 were waited for; matrix products, arithmetic and copies ran while one was open for 3% of the time, Pallas kernels for 0%

commit v1 on v0

v1 whole, which is shorter than its diff:
```python
import functools

import jax
import jax.numpy as jnp
from jax import lax
from jax.experimental import pallas as pl
from jax.experimental.pallas import tpu as pltpu
from jax.sharding import PartitionSpec as P

STEPS = 2
loss_rate = 0.2
recovery = 0.8
F32 = jnp.float32
BF16 = jnp.bfloat16

ROWS = 16
GROUP = 4
LAG = 2


def section_kernel(
    turn, blocks, info, e_in, halo, msg, coef, *rest
):
    w_refs = rest[:blocks]
    taps_in, e_out, pay, taps_out, mid, w_f32, w_hi, w_lo, w_sem, t_sem = rest[blocks:]
    active = info[0]
    slot = info[1]
    block = info[2]
    first = info[3]
    core = info[4]
    keep = info[5]
    keep_row = info[6]
    lane = lax.broadcasted_iota(jnp.int32, (32, 128), 1)
    other = 1 - core

    @pl.when(active == 0)
    def _():
        e_out[...] = e_in[...]
        pay[0:128, :] = e_in[ROWS - 1].reshape(128, 256)
        pay[128:256, :] = e_in[ROWS - 2].reshape(128, 256)
        pay[256:288, :] = jnp.zeros((32, 256), F32)

    @pl.when(active == 1)
    def _():
        for k in range(blocks):

            @pl.when(block == k)
            def _(k=k):
                copy = pltpu.make_async_copy(w_refs[k].at[:, slot], w_f32, w_sem)
                copy.start()
                copy.wait()

        w = w_f32[...].reshape(768, 256)
        hi = w.astype(BF16)
        w_hi[...] = hi
        w_lo[...] = (w - hi.astype(F32)).astype(BF16)

        theirs = pltpu.roll(msg[other, :, 0:128], 1, 1)
        received = jnp.where(lane == ROWS, theirs, msg[core, :, 0:128])
        n = jnp.where(first == 1, coef[0], received)
        gain_n = coef[1] * n

        def products(x):
            rows = x.shape[0]
            flat = x.reshape(rows * 4, 32, 256)
            hi = flat.astype(BF16)
            lo = (flat - hi.astype(F32)).astype(BF16)
            zero = jnp.zeros((32, 256), BF16)

            def wide(v):
                parts = []
                for i in range(rows * 4):
                    b = i % 4
                    before = v[i - 1] if b > 0 else zero
                    after = v[i + 1] if b < 3 else zero
                    parts.append(jnp.concatenate([before, v[i], after], axis=1))
                return jnp.concatenate(parts, axis=0)

            hi, lo = wide(hi), wide(lo)
            y = jnp.dot(hi, w_hi[...], preferred_element_type=F32)
            y += jnp.dot(lo, w_hi[...], preferred_element_type=F32)
            y += jnp.dot(hi, w_lo[...], preferred_element_type=F32)
            return y.reshape(rows, 4, 32, 256)

        def rows_step(get, get_next, put, base, count, last_n):
            static = isinstance(base, int)
            turn_by = (128 - base) % 128 if static else lax.rem(128 - base, 128)
            gn = pltpu.roll(gain_n, turn_by, 1)
            c_prev = pltpu.roll(coef[2], turn_by, 1)
            c_next = pltpu.roll(coef[3], turn_by, 1)
            c_left = pltpu.roll(coef[4], turn_by, 1)
            c_right = pltpu.roll(coef[5], turn_by, 1)
            n_here = pltpu.roll(n, turn_by, 1)
            x = get(base, count)
            y = products(x)
            for r in range(count):
                before = get(max(base - 1, 0) if static else jnp.maximum(base - 1, 0), 1)[0] if r == 0 else x[r - 1]
                after = get_next() if r == count - 1 else x[r + 1]
                cp, cn = c_prev[:, r : r + 1], c_next[:, r : r + 1]
                cl, cr = c_left[:, r : r + 1], c_right[:, r : r + 1]
                linear = []
                power = jnp.zeros((32, 128), F32)
                for b in range(4):
                    own = x[r, b]
                    spread = (
                        cp * before[b]
                        + cn * after[b]
                        + cl * pltpu.roll(own, 1, 0)
                        + cr * pltpu.roll(own, 31, 0)
                    )
                    re = y[r, b, :, 0:128] - spread[:, 128:256]
                    im = y[r, b, :, 128:256] + spread[:, 0:128]
                    power += re * re + im * im
                    linear.append((re, im))
                mean = jnp.sum(power, axis=1, keepdims=True) * (1.0 / 512.0)
                factor = jnp.exp(0.5 * (gn[:, r : r + 1] / (1.0 + mean) - loss_rate))
                for b in range(4):
                    put(base + r, b, factor * linear[b][0], factor * linear[b][1])
                if last_n is not None:
                    leaving = factor * factor * mean
                    updated = 1.0 - recovery * (1.0 - n_here[:, r : r + 1] / (1.0 + leaving))
                    last_n = jnp.where(lane == base + r, updated, last_n)
            return last_n

        def get_e(base, count):
            return e_in[pl.ds(base, count)]

        def put_mid(i, b, re, im):
            mid[i, b, :, 0:128] = re
            mid[i, b, :, 128:256] = im

        def put_out(i, b, re, im):
            e_out[i, b, :, 0:128] = re
            e_out[i, b, :, 128:256] = im

        def get_mid(base, count):
            return mid[pl.ds(base, count)]

        halo_near = halo[other, 0:128, :].reshape(4, 32, 256)

        def one(g, carry):
            base = g * GROUP
            rows_step(get_e, lambda: e_in[base + GROUP], put_mid, base, GROUP, None)
            return carry

        lax.fori_loop(0, ROWS // GROUP - 1, one, 0)
        rows_step(get_e, lambda: halo_near, put_mid, ROWS - GROUP, GROUP, None)

        def edge_row():
            turn_by = 128 - ROWS
            gn = pltpu.roll(gain_n, turn_by, 1)[:, 0:1]
            cs = [pltpu.roll(coef[k], turn_by, 1)[:, 0:1] for k in range(2, 6)]
            x = halo_near[None]
            y = products(x)
            before = e_in[ROWS - 1]
            after = halo[other, 128:256, :].reshape(4, 32, 256)
            linear = []
            power = jnp.zeros((32, 128), F32)
            for b in range(4):
                own = x[0, b]
                spread = (
                    cs[0] * before[b]
                    + cs[1] * after[b]
                    + cs[2] * pltpu.roll(own, 1, 0)
                    + cs[3] * pltpu.roll(own, 31, 0)
                )
                re = y[0, b, :, 0:128] - spread[:, 128:256]
                im = y[0, b, :, 128:256] + spread[:, 0:128]
                power += re * re + im * im
                linear.append((re, im))
            mean = jnp.sum(power, axis=1, keepdims=True) * (1.0 / 512.0)
            factor = jnp.exp(0.5 * (gn / (1.0 + mean) - loss_rate))
            for b in range(4):
                put_mid(ROWS, b, factor * linear[b][0], factor * linear[b][1])

        edge_row()

        def two(g, last_n):
            base = g * GROUP
            return rows_step(get_mid, lambda: mid[base + GROUP], put_out, base, GROUP, last_n)

        last_n = lax.fori_loop(0, ROWS // GROUP, two, jnp.zeros((32, 128), F32))

        @pl.when(keep == 1)
        def _():
            copy = pltpu.make_async_copy(
                e_out.at[pl.ds(keep_row, 2)], taps_out.at[slot], t_sem
            )
            copy.start()
            copy.wait()

        pay[0:128, :] = e_out[ROWS - 1].reshape(128, 256)
        pay[128:256, :] = e_out[ROWS - 2].reshape(128, 256)
        pay[256:288, 0:128] = last_n
        pay[256:288, 128:256] = last_n


def section_call(turn, info, e, halo, msg, coef, w_blocks, taps):
    blocks = len(w_blocks)
    vmem = pl.BlockSpec(memory_space=pltpu.VMEM)
    hbm = pl.BlockSpec(memory_space=pl.ANY)
    n_in = 5 + blocks + 1
    return pl.pallas_call(
        functools.partial(section_kernel, turn, blocks),
        out_shape=(
            jax.ShapeDtypeStruct((ROWS, 4, 32, 256), F32),
            jax.ShapeDtypeStruct((288, 256), F32),
            jax.ShapeDtypeStruct(taps.shape, F32),
        ),
        in_specs=[pl.BlockSpec(memory_space=pltpu.SMEM), vmem, vmem, vmem, vmem]
        + [hbm] * (blocks + 1),
        out_specs=(vmem, vmem, hbm),
        scratch_shapes=[
            pltpu.VMEM((ROWS + 1, 4, 32, 256), F32),
            pltpu.VMEM((16, 48, 256), F32),
            pltpu.VMEM((768, 256), BF16),
            pltpu.VMEM((768, 256), BF16),
            pltpu.SemaphoreType.DMA,
            pltpu.SemaphoreType.DMA,
        ],
        input_output_aliases={n_in - 1: 2},
        compiler_params=pltpu.CompilerParams(vmem_limit_bytes=32 * 1024 * 1024),
        name="section",
    )(info, e, halo, msg, coef, *w_blocks, taps)


def local(input_fields, injection_order, dispersion, coupling, amplifier_gain, inversion):
    seg, row = lax.axis_index("segment"), lax.axis_index("row")
    x, z_lo = seg % 4, seg // 4
    core, y, z_hi = row % 2, (row // 2) % 8, row // 16
    chips = [[2 * k, 2 * k + 1] for k in range(16)]
    rings = [[4 * k + i for i in range(4)] for k in range(4)]
    ahead = [(g, g + 1) for g in range(16) if g % 4 < 3]

    own = jnp.concatenate(
        [inversion[0], amplifier_gain[0], coupling[0, :, 0]], axis=0
    ).reshape(1, 192)
    own = jnp.pad(own, ((0, 7), (0, 64)))
    sent = jnp.concatenate(
        [dispersion[0].reshape(16, 48, 256), jnp.broadcast_to(own[None], (16, 8, 256))], axis=1
    )
    got = lax.all_to_all(sent, "segment", 0, 0)
    w_all = [lax.all_gather(got[4 * k : 4 * k + 4, :48], "segment") for k in range(4)]

    field = lax.dynamic_index_in_dim(input_fields, injection_order[x], 0, keepdims=False)[0]
    field = field.transpose(1, 0, 2).reshape(128, 256)
    rows = lax.all_gather(jnp.concatenate([field, got[:, 48]], axis=0), "row")
    rows = jnp.where(core == 0, rows[: ROWS + 2], jnp.flip(rows[32 - ROWS - 2 :], 0))
    e = rows[:ROWS, :128].reshape(ROWS, 4, 32, 256)
    edge = rows[ROWS:, :128].reshape(256, 256)
    halo = jnp.broadcast_to(jnp.pad(edge, ((0, 32), (0, 0)))[None], (2, 288, 256))
    table = rows[: ROWS + 1, 128:, :192].reshape(ROWS + 1, 16, 6, 32).transpose(1, 2, 3, 0)
    n0, gain, up, down, left, right = (table[:, k] for k in range(6))
    before = jnp.where(core == 0, up, down)
    after = jnp.where(core == 0, down, up)
    at_row = jnp.arange(ROWS + 1)[None, None, :]
    at_col = jnp.arange(32)[None, :, None]
    before = jnp.where(at_row == 0, 0.0, before)
    left = jnp.where(at_col == 0, 0.0, left)
    right = jnp.where(at_col == 31, 0.0, right)
    table = jnp.stack([n0, gain, before, after, left, right], axis=1)
    table = jnp.pad(table, ((0, 0), (0, 0), (0, 0), (0, 128 - ROWS - 1)))

    taps = jnp.zeros((4, 2, 4, 32, 256), F32)
    keep_row = jnp.where(core == 0, 2 * y, 14 - 2 * y)
    turns = 16 + 3 * LAG
    msgs = {}
    for turn in range(turns):
        section = turn - LAG * x
        active = jnp.logical_and(section >= 0, section < 16)
        at = jnp.clip(section, 0, 15)
        keep = active & (at // 4 == z_lo) & (core == z_hi)
        info = jnp.stack(
            [active, at % 4, at // 4, x == 0, core, keep, keep_row, 0 * x]
        ).astype(jnp.int32)
        msg = msgs.pop(turn - LAG, None)
        if msg is None:
            msg = jnp.zeros((2, 32, 256), F32)
        coef = lax.dynamic_index_in_dim(table, at, 0, keepdims=False)
        have = w_all[: min(turn, 15) // 4 + 1]
        e, pay, taps = section_call(turn, info, e, halo, msg, coef, have, taps)
        if turn + 1 < turns:
            halo = lax.all_gather(pay, "row", axis_index_groups=chips)
        if turn + LAG < turns:
            msgs[turn] = lax.ppermute(halo[:, 256:], "segment", ahead)

    both = lax.all_gather(taps, "row", axis_index_groups=chips)
    mine = lax.dynamic_index_in_dim(both, z_hi, 0, keepdims=False)
    mine = lax.dynamic_index_in_dim(
        mine, jnp.where(z_hi == 0, core, 1 - core), 1, keepdims=False
    )
    out = lax.all_to_all(mine, "segment", 0, 0, axis_index_groups=rings)
    return out.transpose(0, 2, 1, 3)[None, :, None]


def solution(mesh):
    return jax.shard_map(
        local,
        mesh=mesh,
        in_specs=(
            P(None, "row", None, None, None),
            P(),
            P("segment", None, None),
            P("segment", None, "row", None),
            P("segment", "row", None),
            P("segment", "row", None),
        ),
        out_specs=P("segment", None, "row", None, None, None),
        check_vma=False,
    )
```

time: 805 us -> 695 us (0.86)
  the two profiles are of different devices: /device:TPU:121 before, /device:TPU:1 now
where the time goes in v1:
time: 695 us; the launch traced here: 685 us
  waiting for transfers between devices  264 us (38%)
  Pallas kernels  162 us (23%)
  blocking collectives  102 us (15%)
  local copies, waits for them, and re-layouts  69 us (10%)
  starting transfers between devices  64.5 us (9%)
  between operations  17.7 us (3%)
    pallas_call x22, Pallas kernels, section_call(): pl.pallas_call(functools.partial(section_kernel, turn, blocks), out_shape...  162 us
    all_gather x4, waiting for transfers between devices, local(): lax.all_gather(got[4 * k:4 * k + 4, :48], 'segment')  105 us
    all_gather x1, waiting for transfers between devices, local(): rows = lax.all_gather(jnp.concatenate([field, got[:, 48]], axis=0), 'row')  101 us
    all_gather x21, blocking collectives, local(): halo = lax.all_gather(pay, 'row', axis_index_groups=chips)  90.5 us
    ppermute x20, starting transfers between devices, local(): msgs[turn] = lax.ppermute(halo[:, 256:], 'segment', ahead)  53.9 us
    unnamed x129, local copies, waits for them, and re-layouts  43.1 us
    all_gather x1, waiting for transfers between devices, local(): both = lax.all_gather(taps, 'row', axis_index_groups=chips)  38.4 us
    all_to_all x1, waiting for transfers between devices, local(): got = lax.all_to_all(sent, 'segment', 0, 0)  17.5 us
  transfers between devices with their start and end apart: 27, of which 7 were waited for; matrix products, arithmetic and copies ran while one was open for 4% of the time, Pallas kernels for 23%

profile of v1, /device:TPU:1, one launch (start us, length us, event | category | flops | bytes accessed | tf_op | source)
XLA Modules:
  0.0 685.4 jit_solution(5885385474859496948)
XLA Ops:
  9.6 10.4 %all-to-all-start = ((f32[16,56,256]{2,1,0:T(8,128)}), f32[16,56,256]{2,1,0:T(8,128)S(1)}, u32[]{:S(2)}, u32[]{:S(2)}) async-start(f32[16,56,256]{2,1,0:T(8,128)} %pad_maximum_fusion), calls=%async_computation | async-start | bytes 1835008 | tf_op jit(solution)/shard_map/all_to_all | solution.py:242
  22.6 17.5 %all-to-all-done = f32[16,56,256]{2,1,0:T(8,128)S(1)} async-done(((f32[16,56,256]{2,1,0:T(8,128)}), f32[16,56,256]{2,1,0:T(8,128)S(1)}, u32[]{:S(2)}, u32[]{:S(2)}) %all-to-all-start) | async-done | bytes 917536 | tf_op jit(solution)/shard_map/all_to_all | solution.py:242
  55.6 101.3 %all-gather.34.cloned.1.call-done = f32[4608,256]{1,0:T(8,128)} async-done(((f32[144,256]{1,0:T(8,128)}), f32[4608,256]{1,0:T(8,128)}) %all-gather.34.cloned.1.call-update) | async-done | bytes 4718608 | tf_op jit(solution)/shard_map/all_gather | solution.py:247
  156.9 2.9 fusion.2
  166.5 64.8 %all-gather.36.cloned.1.call-done = f32[64,48,256]{2,1,0:T(8,128)} async-done(((f32[4,48,256]{2,1,0:T(8,128)}), f32[64,48,256]{2,1,0:T(8,128)}) %all-gather.36.cloned.1.call-update) | async-done | bytes 3145744 | tf_op jit(solution)/shard_map/all_gather | solution.py:243
  233.3 9.0 %section.22 = (f32[16,4,32,256]{3,2,1,0:T(8,128)S(1)}, f32[288,256]{1,0:T(8,128)S(1)}, f32[4,2,4,32,256]{4,3,2,1,0:T(8,128)S(1)}) custom-call(s32[8]{0:T(128)S(1)} %stack.702.info, f32[16,4,32,256]{3,2,1,0:T(8,128)S(1)} %bitcast.251, f32[2,288,256]{2,1,0:T(8,128)S(1)} %broadcast_in_dim.49.halo, ...), custom_call_target="tpu_custom_call", output_to_operand_aliasing={{2}: (6, {})} | custom-call | tf_op jit(solution)/shard_map/section/pallas_call | solution.py:203
  242.4 12.2 %all-gather.2 = f32[576,256]{1,0:T(8,128)S(1)} all-gather(f32[288,256]{1,0:T(8,128)S(1)} %get-tuple-element.70), channel_id=4, replica_groups={{0,1},{2,3},{4,5},{6,7},{8,9},{10,11},{12,13},{14,15},{16,17},{18,19},{..., dimensions={0}, use_global_device_ids=true | all-gather | bytes 884736 | tf_op jit(solution)/shard_map/all_gather | solution.py:283
  256.6 9.1 %section.23 = (f32[16,4,32,256]{3,2,1,0:T(8,128)S(1)}, f32[288,256]{1,0:T(8,128)S(1)}, f32[4,2,4,32,256]{4,3,2,1,0:T(8,128)S(1)}) custom-call(s32[8]{0:T(128)S(1)} %stack.695.info, f32[16,4,32,256]{3,2,1,0:T(8,128)S(1)} %get-tuple-element.69.e_in, f32[2,288,256]{2,1,0:T(8,128)S(1)} %bitcast.255, ...), custom_call_target="tpu_custom_call", output_to_operand_aliasing={{2}: (6, {})} | custom-call | tf_op jit(solution)/shard_map/section/pallas_call | solution.py:203
  271.0 9.8 %section.24 = (f32[16,4,32,256]{3,2,1,0:T(8,128)S(1)}, f32[288,256]{1,0:T(8,128)S(1)}, f32[4,2,4,32,256]{4,3,2,1,0:T(8,128)S(1)}) custom-call(s32[8]{0:T(128)S(1)} %copy-done.54, f32[16,4,32,256]{3,2,1,0:T(8,128)S(1)} %get-tuple-element.72.e_in, f32[2,288,256]{2,1,0:T(8,128)S(1)} %bitcast.253, ...), custom_call_target="tpu_custom_call", output_to_operand_aliasing={{2}: (6, {})} | custom-call | tf_op jit(solution)/shard_map/section/pallas_call | solution.py:203
  285.6 9.0 %section.25 = (f32[16,4,32,256]{3,2,1,0:T(8,128)S(1)}, f32[288,256]{1,0:T(8,128)S(1)}, f32[4,2,4,32,256]{4,3,2,1,0:T(8,128)S(1)}) custom-call(s32[8]{0:T(128)S(1)} %copy-done.53, f32[16,4,32,256]{3,2,1,0:T(8,128)S(1)} %get-tuple-element.75.e_in, f32[2,288,256]{2,1,0:T(8,128)S(1)} %bitcast.267, ...), custom_call_target="tpu_custom_call", output_to_operand_aliasing={{2}: (6, {})} | custom-call | tf_op jit(solution)/shard_map/section/pallas_call | solution.py:203
  302.5 18.9 %all-gather.38.cloned.1.call-done = f32[64,48,256]{2,1,0:T(8,128)} async-done(((f32[4,48,256]{2,1,0:T(8,128)}), f32[64,48,256]{2,1,0:T(8,128)}) %all-gather.38.cloned.1.call-update) | async-done | bytes 3145744 | tf_op jit(solution)/shard_map/all_gather | solution.py:243
  328.7 9.4 %section.26 = (f32[16,4,32,256]{3,2,1,0:T(8,128)S(1)}, f32[288,256]{1,0:T(8,128)S(1)}, f32[4,2,4,32,256]{4,3,2,1,0:T(8,128)S(1)}) custom-call(s32[8]{0:T(128)S(1)} %copy-done.52, f32[16,4,32,256]{3,2,1,0:T(8,128)S(1)} %copy-done.24, f32[2,288,256]{2,1,0:T(8,128)S(1)} %bitcast.257, ...), custom_call_target="tpu_custom_call", output_to_operand_aliasing={{2}: (7, {})} | custom-call | tf_op jit(solution)/shard_map/section/pallas_call | solution.py:203
  338.1 12.0 %all-gather.7 = f32[576,256]{1,0:T(8,128)S(1)} all-gather(f32[288,256]{1,0:T(8,128)S(1)} %get-tuple-element.82), channel_id=9, replica_groups={{0,1},{2,3},{4,5},{6,7},{8,9},{10,11},{12,13},{14,15},{16,17},{18,19},{..., dimensions={0}, use_global_device_ids=true | all-gather | bytes 884736 | tf_op jit(solution)/shard_map/all_gather | solution.py:283
  352.7 9.5 %section.27 = (f32[16,4,32,256]{3,2,1,0:T(8,128)S(1)}, f32[288,256]{1,0:T(8,128)S(1)}, f32[4,2,4,32,256]{4,3,2,1,0:T(8,128)S(1)}) custom-call(s32[8]{0:T(128)S(1)} %copy-done.51, f32[16,4,32,256]{3,2,1,0:T(8,128)S(1)} %get-tuple-element.81.e_in, f32[2,288,256]{2,1,0:T(8,128)S(1)} %bitcast.269, ...), custom_call_target="tpu_custom_call", output_to_operand_aliasing={{2}: (7, {})} | custom-call | tf_op jit(solution)/shard_map/section/pallas_call | solution.py:203
  362.2 2.5 all-gather.8
  366.4 9.4 %section.28 = (f32[16,4,32,256]{3,2,1,0:T(8,128)S(1)}, f32[288,256]{1,0:T(8,128)S(1)}, f32[4,2,4,32,256]{4,3,2,1,0:T(8,128)S(1)}) custom-call(s32[8]{0:T(128)S(1)} %copy-done.50, f32[16,4,32,256]{3,2,1,0:T(8,128)S(1)} %get-tuple-element.84.e_in, f32[2,288,256]{2,1,0:T(8,128)S(1)} %bitcast.271, ...), custom_call_target="tpu_custom_call", output_to_operand_aliasing={{2}: (7, {})} | custom-call | tf_op jit(solution)/shard_map/section/pallas_call | solution.py:203
  375.8 2.5 all-gather.9
  381.2 9.0 %section.29 = (f32[16,4,32,256]{3,2,1,0:T(8,128)S(1)}, f32[288,256]{1,0:T(8,128)S(1)}, f32[4,2,4,32,256]{4,3,2,1,0:T(8,128)S(1)}) custom-call(s32[8]{0:T(128)S(1)} %copy-done.49, f32[16,4,32,256]{3,2,1,0:T(8,128)S(1)} %get-tuple-element.87.e_in, f32[2,288,256]{2,1,0:T(8,128)S(1)} %bitcast.273, ...), custom_call_target="tpu_custom_call", output_to_operand_aliasing={{2}: (7, {})} | custom-call | tf_op jit(solution)/shard_map/section/pallas_call | solution.py:203
  398.4 11.3 %all-gather.40.cloned.1.call-done = f32[64,48,256]{2,1,0:T(8,128)} async-done(((f32[4,48,256]{2,1,0:T(8,128)}), f32[64,48,256]{2,1,0:T(8,128)}) %all-gather.40.cloned.1.call-update) | async-done | bytes 3145744 | tf_op jit(solution)/shard_map/all_gather | solution.py:243
  419.0 9.4 %section.30 = (f32[16,4,32,256]{3,2,1,0:T(8,128)S(1)}, f32[288,256]{1,0:T(8,128)S(1)}, f32[4,2,4,32,256]{4,3,2,1,0:T(8,128)S(1)}) custom-call(s32[8]{0:T(128)S(1)} %copy-done.58, f32[16,4,32,256]{3,2,1,0:T(8,128)S(1)} %copy-done.28, f32[2,288,256]{2,1,0:T(8,128)S(1)} %bitcast.285, ...), custom_call_target="tpu_custom_call", output_to_operand_aliasing={{2}: (8, {})} | custom-call | tf_op jit(solution)/shard_map/section/pallas_call | solution.py:203
  428.3 12.6 %all-gather.12 = f32[576,256]{1,0:T(8,128)S(1)} all-gather(f32[288,256]{1,0:T(8,128)S(1)} %get-tuple-element.94), channel_id=14, replica_groups={{0,1},{2,3},{4,5},{6,7},{8,9},{10,11},{12,13},{14,15},{16,17},{18,19},{..., dimensions={0}, use_global_device_ids=true | all-gather | bytes 884736 | tf_op jit(solution)/shard_map/all_gather | solution.py:283
  440.9 2.6 collective-permute-start.8
  443.6 9.5 %section.31 = (f32[16,4,32,256]{3,2,1,0:T(8,128)S(1)}, f32[288,256]{1,0:T(8,128)S(1)}, f32[4,2,4,32,256]{4,3,2,1,0:T(8,128)S(1)}) custom-call(s32[8]{0:T(128)S(1)} %copy-done.57, f32[16,4,32,256]{3,2,1,0:T(8,128)S(1)} %get-tuple-element.93.e_in, f32[2,288,256]{2,1,0:T(8,128)S(1)} %bitcast.287, ...), custom_call_target="tpu_custom_call", output_to_operand_aliasing={{2}: (8, {})} | custom-call | tf_op jit(solution)/shard_map/section/pallas_call | solution.py:203
  453.1 2.5 all-gather.13
  457.3 9.6 %section.32 = (f32[16,4,32,256]{3,2,1,0:T(8,128)S(1)}, f32[288,256]{1,0:T(8,128)S(1)}, f32[4,2,4,32,256]{4,3,2,1,0:T(8,128)S(1)}) custom-call(s32[8]{0:T(128)S(1)} %copy-done.56, f32[16,4,32,256]{3,2,1,0:T(8,128)S(1)} %get-tuple-element.96.e_in, f32[2,288,256]{2,1,0:T(8,128)S(1)} %bitcast.289, ...), custom_call_target="tpu_custom_call", output_to_operand_aliasing={{2}: (8, {})} | custom-call | tf_op jit(solution)/shard_map/section/pallas_call | solution.py:203
  466.9 2.5 all-gather.14
  472.3 9.0 %section.33 = (f32[16,4,32,256]{3,2,1,0:T(8,128)S(1)}, f32[288,256]{1,0:T(8,128)S(1)}, f32[4,2,4,32,256]{4,3,2,1,0:T(8,128)S(1)}) custom-call(s32[8]{0:T(128)S(1)} %copy-done.55, f32[16,4,32,256]{3,2,1,0:T(8,128)S(1)} %get-tuple-element.99.e_in, f32[2,288,256]{2,1,0:T(8,128)S(1)} %bitcast.291, ...), custom_call_target="tpu_custom_call", output_to_operand_aliasing={{2}: (8, {})} | custom-call | tf_op jit(solution)/shard_map/section/pallas_call | solution.py:203
  483.6 2.5 all-gather.15
  489.5 10.0 %all-gather.42.cloned.1.call-done = f32[64,48,256]{2,1,0:T(8,128)} async-done(((f32[4,48,256]{2,1,0:T(8,128)}), f32[64,48,256]{2,1,0:T(8,128)}) %all-gather.42.cloned.1.call-update) | async-done | bytes 3145744 | tf_op jit(solution)/shard_map/all_gather | solution.py:243
  510.6 9.4 %section.34 = (f32[16,4,32,256]{3,2,1,0:T(8,128)S(1)}, f32[288,256]{1,0:T(8,128)S(1)}, f32[4,2,4,32,256]{4,3,2,1,0:T(8,128)S(1)}) custom-call(s32[8]{0:T(128)S(1)} %copy-done.48, f32[16,4,32,256]{3,2,1,0:T(8,128)S(1)} %copy-done.26, f32[2,288,256]{2,1,0:T(8,128)S(1)} %bitcast.259, ...), custom_call_target="tpu_custom_call", output_to_operand_aliasing={{2}: (9, {})} | custom-call | tf_op jit(solution)/shard_map/section/pallas_call | solution.py:203
  520.0 11.9 %all-gather.17 = f32[576,256]{1,0:T(8,128)S(1)} all-gather(f32[288,256]{1,0:T(8,128)S(1)} %get-tuple-element.106), channel_id=19, replica_groups={{0,1},{2,3},{4,5},{6,7},{8,9},{10,11},{12,13},{14,15},{16,17},{18,19},{..., dimensions={0}, use_global_device_ids=true | all-gather | bytes 884736 | tf_op jit(solution)/shard_map/all_gather | solution.py:283
  531.9 2.6 collective-permute-start.12
  534.6 9.5 %section.35 = (f32[16,4,32,256]{3,2,1,0:T(8,128)S(1)}, f32[288,256]{1,0:T(8,128)S(1)}, f32[4,2,4,32,256]{4,3,2,1,0:T(8,128)S(1)}) custom-call(s32[8]{0:T(128)S(1)} %copy-done.47, f32[16,4,32,256]{3,2,1,0:T(8,128)S(1)} %get-tuple-element.105.e_in, f32[2,288,256]{2,1,0:T(8,128)S(1)} %bitcast.275, ...), custom_call_target="tpu_custom_call", output_to_operand_aliasing={{2}: (9, {})} | custom-call | tf_op jit(solution)/shard_map/section/pallas_call | solution.py:203
  544.1 2.5 all-gather.18
  548.3 9.7 %section.36 = (f32[16,4,32,256]{3,2,1,0:T(8,128)S(1)}, f32[288,256]{1,0:T(8,128)S(1)}, f32[4,2,4,32,256]{4,3,2,1,0:T(8,128)S(1)}) custom-call(s32[8]{0:T(128)S(1)} %copy-done.46, f32[16,4,32,256]{3,2,1,0:T(8,128)S(1)} %get-tuple-element.108.e_in, f32[2,288,256]{2,1,0:T(8,128)S(1)} %bitcast.277, ...), custom_call_target="tpu_custom_call", output_to_operand_aliasing={{2}: (9, {})} | custom-call | tf_op jit(solution)/shard_map/section/pallas_call | solution.py:203
  558.0 2.5 all-gather.19
  562.2 9.0 %section.37 = (f32[16,4,32,256]{3,2,1,0:T(8,128)S(1)}, f32[288,256]{1,0:T(8,128)S(1)}, f32[4,2,4,32,256]{4,3,2,1,0:T(8,128)S(1)}) custom-call(s32[8]{0:T(128)S(1)} %copy-done.45, f32[16,4,32,256]{3,2,1,0:T(8,128)S(1)} %get-tuple-element.111.e_in, f32[2,288,256]{2,1,0:T(8,128)S(1)} %bitcast.279, ...), custom_call_target="tpu_custom_call", output_to_operand_aliasing={{2}: (9, {})} | custom-call | tf_op jit(solution)/shard_map/section/pallas_call | solution.py:203
  571.3 2.5 all-gather.20
  576.2 2.5 all-gather.21
  578.7 9.9 %collective-permute-start.16 = (f32[2,32,256]{2,1,0:T(8,128)S(1)}, f32[2,32,256]{2,1,0:T(8,128)S(1)}, u32[]{:S(2)}, u32[]{:S(2)}) collective-permute-start(f32[2,32,256]{2,1,0:T(8,128)S(1)} %slice.175), channel_id=1, source_target_pairs={{0,32},{32,64},{64,96},{128,160},{160,192},{192,224},{256,288},{28... | collective-permute-start | bytes 196616 | tf_op jit(solution)/shard_map/ppermute | solution.py:285
  589.4 2.5 all-gather.22
  591.9 10.1 %collective-permute-start.17 = (f32[2,32,256]{2,1,0:T(8,128)S(1)}, f32[2,32,256]{2,1,0:T(8,128)S(1)}, u32[]{:S(2)}, u32[]{:S(2)}) collective-permute-start(f32[2,32,256]{2,1,0:T(8,128)S(1)} %slice.176), channel_id=1, source_target_pairs={{0,32},{32,64},{64,96},{128,160},{160,192},{192,224},{256,288},{28... | collective-permute-start | bytes 196616 | tf_op jit(solution)/shard_map/ppermute | solution.py:285
  602.0 8.1 %section.40 = (f32[16,4,32,256]{3,2,1,0:T(8,128)S(1)}, f32[288,256]{1,0:T(8,128)S(1)}, f32[4,2,4,32,256]{4,3,2,1,0:T(8,128)S(1)}) custom-call(s32[8]{0:T(128)S(1)} %stack.576.info, f32[16,4,32,256]{3,2,1,0:T(8,128)S(1)} %get-tuple-element.120.e_in, f32[2,288,256]{2,1,0:T(8,128)S(1)} %bitcast.261, ...), custom_call_target="tpu_custom_call", output_to_operand_aliasing={{2}: (9, {})} | custom-call | tf_op jit(solution)/shard_map/section/pallas_call | solution.py:203
  610.1 2.5 all-gather.23
  615.0 2.5 all-gather.24
  620.0 2.5 all-gather.25
  625.7 38.4 %all-gather.44.cloned.1.call-done = f32[8,2,4,32,256]{4,3,2,1,0:T(8,128)} async-done(((f32[4,2,4,32,256]{4,3,2,1,0:T(8,128)}), f32[8,2,4,32,256]{4,3,2,1,0:T(8,128)}) %all-gather.44.cloned.1.call-update) | async-done | bytes 2097168 | tf_op jit(solution)/shard_map/all_gather | solution.py:287
  665.6 11.9 %all_to_all.10 = f32[4,4,32,256]{3,1,2,0:T(4,128)S(1)} all-to-all(f32[4,4,32,256]{3,1,2,0:T(4,128)S(1)} %bitcast.300), channel_id=1, replica_groups={{0,32,64,96},{128,160,192,224},{256,288,320,352},{384,416,448,480},{1,3..., dimensions={0} | all-to-all | bytes 1048576 | tf_op jit(solution)/shard_map/all_to_all | solution.py:292
  (261 shorter events, 116.3 us)
Async XLA Ops:
  6.5 16.0 %copy-start = (f32[4,1,32,4,256]{4,3,2,1,0:T(4,128)S(1)}, f32[4,1,32,4,256]{4,3,2,1,0:T(4,128)}, u32[]{:S(2)}) copy-start(f32[4,1,32,4,256]{4,3,2,1,0:T(4,128)} %param.6) | copy-start | bytes 1572868
  9.6 30.6 %all-to-all-start = ((f32[16,56,256]{2,1,0:T(8,128)}), f32[16,56,256]{2,1,0:T(8,128)S(1)}, u32[]{:S(2)}, u32[]{:S(2)}) async-start(f32[16,56,256]{2,1,0:T(8,128)} %pad_maximum_fusion), calls=%async_computation | async-start | bytes 1835008 | tf_op jit(solution)/shard_map/all_to_all | solution.py:242
  19.9 136.9 %all-gather.34.cloned.1.call-start = ((), (), s32[]{:S(2)}) async-start(), calls=%async_computation.2 | async-start | bytes 4866048 | tf_op jit(solution)/shard_map/all_gather | solution.py:247
  40.9 190.4 %all-gather.36.cloned.1.call-start = ((), (), s32[]{:S(2)}) async-start(), calls=%async_computation.3 | async-start | bytes 3342336 | tf_op jit(solution)/shard_map/all_gather | solution.py:243
  41.8 279.6 %all-gather.38.cloned.1.call-start = ((), (), s32[]{:S(2)}) async-start(), calls=%async_computation.4 | async-start | bytes 3342336 | tf_op jit(solution)/shard_map/all_gather | solution.py:243
  42.6 367.2 %all-gather.40.cloned.1.call-start = ((), (), s32[]{:S(2)}) async-start(), calls=%async_computation.5 | async-start | bytes 3342336 | tf_op jit(solution)/shard_map/all_gather | solution.py:243
  43.1 456.4 %all-gather.42.cloned.1.call-start = ((), (), s32[]{:S(2)}) async-start(), calls=%async_computation.6 | async-start | bytes 3342336 | tf_op jit(solution)/shard_map/all_gather | solution.py:243
  43.7 620.4 %all-gather.44.cloned.1.call-start = ((), (), s32[]{:S(2)}) async-start(), calls=%async_computation.7 | async-start | bytes 3145728 | tf_op jit(solution)/shard_map/all_gather | solution.py:287
  233.3 22.5 %copy-start.60 = (f32[16,6,32,17]{3,2,1,0:T(8,128)S(1)}, f32[16,6,32,17]{3,2,1,0:T(8,128)}, u32[]{:S(2)}) copy-start(f32[16,6,32,17]{3,2,1,0:T(8,128)} %copy-done.59) | copy-start | bytes 626692
  242.4 14.2 %copy-start.3 = (f32[64,48,256]{2,1,0:T(8,128)S(1)}, f32[64,48,256]{2,1,0:T(8,128)}, u32[]{:S(2)}) copy-start(f32[64,48,256]{2,1,0:T(8,128)} %all-gather.36.cloned.1.call-done) | copy-start | bytes 9437188
  254.5 16.4 %collective-permute-start = (f32[2,32,256]{2,1,0:T(8,128)S(1)}, f32[2,32,256]{2,1,0:T(8,128)S(1)}, u32[]{:S(2)}, u32[]{:S(2)}) collective-permute-start(f32[2,32,256]{2,1,0:T(8,128)S(1)} %slice.156), channel_id=1, source_target_pairs={{0,32},{32,64},{64,96},{128,160},{160,192},{192,224},{256,288},{28... | collective-permute-start | bytes 196616 | tf_op jit(solution)/shard_map/ppermute | solution.py:285
  268.0 17.6 %collective-permute-start.1 = (f32[2,32,256]{2,1,0:T(8,128)S(1)}, f32[2,32,256]{2,1,0:T(8,128)S(1)}, u32[]{:S(2)}, u32[]{:S(2)}) collective-permute-start(f32[2,32,256]{2,1,0:T(8,128)S(1)} %slice.157), channel_id=1, source_target_pairs={{0,32},{32,64},{64,96},{128,160},{160,192},{192,224},{256,288},{28... | collective-permute-start | bytes 196616 | tf_op jit(solution)/shard_map/ppermute | solution.py:285
  271.0 14.6 %copy-start.53 = (s32[8]{0:T(128)S(1)}, s32[8]{0:T(128)}, u32[]{:S(2)}) copy-start(s32[8]{0:T(128)} %stack.681.info) | copy-start | bytes 100
  283.7 37.7 %collective-permute-start.2 = (f32[2,32,256]{2,1,0:T(8,128)}, f32[2,32,256]{2,1,0:T(8,128)}, u32[]{:S(2)}, u32[]{:S(2)}) collective-permute-start(f32[2,32,256]{2,1,0:T(8,128)} %slice.158), channel_id=1, source_target_pairs={{0,32},{32,64},{64,96},{128,160},{160,192},{192,224},{256,288},{28... | collective-permute-start | bytes 196616 | tf_op jit(solution)/shard_map/ppermute | solution.py:285
  300.6 52.0 %collective-permute-start.3 = (f32[2,32,256]{2,1,0:T(8,128)}, f32[2,32,256]{2,1,0:T(8,128)}, u32[]{:S(2)}, u32[]{:S(2)}) collective-permute-start(f32[2,32,256]{2,1,0:T(8,128)} %slice.160), channel_id=1, source_target_pairs={{0,32},{32,64},{64,96},{128,160},{160,192},{192,224},{256,288},{28... | collective-permute-start | bytes 196616 | tf_op jit(solution)/shard_map/ppermute | solution.py:285
  328.7 23.9 %copy-start.36 = (f32[6,32,128]{2,1,0:T(8,128)S(1)}, f32[6,32,128]{2,1,0:T(8,128)}, u32[]{:S(2)}) copy-start(f32[6,32,128]{2,1,0:T(8,128)} %get-tuple-element.140.coef) | copy-start | bytes 294916
  328.7 23.9 %copy-start.51 = (s32[8]{0:T(128)S(1)}, s32[8]{0:T(128)}, u32[]{:S(2)}) copy-start(s32[8]{0:T(128)} %stack.667.info) | copy-start | bytes 100
  350.2 16.2 %collective-permute-start.4 = (f32[2,32,256]{2,1,0:T(8,128)S(1)}, f32[2,32,256]{2,1,0:T(8,128)S(1)}, u32[]{:S(2)}, u32[]{:S(2)}) collective-permute-start(f32[2,32,256]{2,1,0:T(8,128)S(1)} %slice.161), channel_id=1, source_target_pairs={{0,32},{32,64},{64,96},{128,160},{160,192},{192,224},{256,288},{28... | collective-permute-start | bytes 196616 | tf_op jit(solution)/shard_map/ppermute | solution.py:285
  352.7 13.7 %copy-start.37 = (f32[6,32,128]{2,1,0:T(8,128)S(1)}, f32[6,32,128]{2,1,0:T(8,128)}, u32[]{:S(2)}) copy-start(f32[6,32,128]{2,1,0:T(8,128)} %get-tuple-element.142.coef) | copy-start | bytes 294916
  352.7 13.7 %copy-start.50 = (s32[8]{0:T(128)S(1)}, s32[8]{0:T(128)}, u32[]{:S(2)}) copy-start(s32[8]{0:T(128)} %stack.660.info) | copy-start | bytes 100
  364.7 16.5 %collective-permute-start.5 = (f32[2,32,256]{2,1,0:T(8,128)S(1)}, f32[2,32,256]{2,1,0:T(8,128)S(1)}, u32[]{:S(2)}, u32[]{:S(2)}) collective-permute-start(f32[2,32,256]{2,1,0:T(8,128)S(1)} %slice.162), channel_id=1, source_target_pairs={{0,32},{32,64},{64,96},{128,160},{160,192},{192,224},{256,288},{28... | collective-permute-start | bytes 196616 | tf_op jit(solution)/shard_map/ppermute | solution.py:285
  366.4 14.9 %copy-start.35 = (f32[6,32,128]{2,1,0:T(8,128)S(1)}, f32[6,32,128]{2,1,0:T(8,128)}, u32[]{:S(2)}) copy-start(f32[6,32,128]{2,1,0:T(8,128)} %get-tuple-element.143.coef) | copy-start | bytes 294916
  366.4 14.8 %copy-start.49 = (s32[8]{0:T(128)S(1)}, s32[8]{0:T(128)}, u32[]{:S(2)}) copy-start(s32[8]{0:T(128)} %stack.653.info) | copy-start | bytes 100
  378.9 30.8 %collective-permute-start.6 = (f32[2,32,256]{2,1,0:T(8,128)}, f32[2,32,256]{2,1,0:T(8,128)}, u32[]{:S(2)}, u32[]{:S(2)}) collective-permute-start(f32[2,32,256]{2,1,0:T(8,128)} %slice.163), channel_id=1, source_target_pairs={{0,32},{32,64},{64,96},{128,160},{160,192},{192,224},{256,288},{28... | collective-permute-start | bytes 196616 | tf_op jit(solution)/shard_map/ppermute | solution.py:285
  396.5 47.1 %collective-permute-start.7 = (f32[2,32,256]{2,1,0:T(8,128)}, f32[2,32,256]{2,1,0:T(8,128)}, u32[]{:S(2)}, u32[]{:S(2)}) collective-permute-start(f32[2,32,256]{2,1,0:T(8,128)} %slice.165), channel_id=1, source_target_pairs={{0,32},{32,64},{64,96},{128,160},{160,192},{192,224},{256,288},{28... | collective-permute-start | bytes 196616 | tf_op jit(solution)/shard_map/ppermute | solution.py:285
  418.9 24.6 %copy-start.41 = (f32[6,32,128]{2,1,0:T(8,128)S(1)}, f32[6,32,128]{2,1,0:T(8,128)}, u32[]{:S(2)}) copy-start(f32[6,32,128]{2,1,0:T(8,128)} %get-tuple-element.145.coef) | copy-start | bytes 294916
  419.0 24.7 %copy-start.57 = (s32[8]{0:T(128)S(1)}, s32[8]{0:T(128)}, u32[]{:S(2)}) copy-start(s32[8]{0:T(128)} %stack.639.info) | copy-start | bytes 100
  440.9 16.3 %collective-permute-start.8 = (f32[2,32,256]{2,1,0:T(8,128)S(1)}, f32[2,32,256]{2,1,0:T(8,128)S(1)}, u32[]{:S(2)}, u32[]{:S(2)}) collective-permute-start(f32[2,32,256]{2,1,0:T(8,128)S(1)} %slice.166), channel_id=1, source_target_pairs={{0,32},{32,64},{64,96},{128,160},{160,192},{192,224},{256,288},{28... | collective-permute-start | bytes 196616 | tf_op jit(solution)/shard_map/ppermute | solution.py:285
  443.6 13.7 %copy-start.40 = (f32[6,32,128]{2,1,0:T(8,128)S(1)}, f32[6,32,128]{2,1,0:T(8,128)}, u32[]{:S(2)}) copy-start(f32[6,32,128]{2,1,0:T(8,128)} %get-tuple-element.146.coef) | copy-start | bytes 294916
  443.6 13.7 %copy-start.56 = (s32[8]{0:T(128)S(1)}, s32[8]{0:T(128)}, u32[]{:S(2)}) copy-start(s32[8]{0:T(128)} %stack.632.info) | copy-start | bytes 100
  455.6 16.7 %collective-permute-start.9 = (f32[2,32,256]{2,1,0:T(8,128)S(1)}, f32[2,32,256]{2,1,0:T(8,128)S(1)}, u32[]{:S(2)}, u32[]{:S(2)}) collective-permute-start(f32[2,32,256]{2,1,0:T(8,128)S(1)} %slice.167), channel_id=1, source_target_pairs={{0,32},{32,64},{64,96},{128,160},{160,192},{192,224},{256,288},{28... | collective-permute-start | bytes 196616 | tf_op jit(solution)/shard_map/ppermute | solution.py:285
  457.3 15.0 %copy-start.39 = (f32[6,32,128]{2,1,0:T(8,128)S(1)}, f32[6,32,128]{2,1,0:T(8,128)}, u32[]{:S(2)}) copy-start(f32[6,32,128]{2,1,0:T(8,128)} %get-tuple-element.148.coef) | copy-start | bytes 294916
  457.3 15.0 %copy-start.55 = (s32[8]{0:T(128)S(1)}, s32[8]{0:T(128)}, u32[]{:S(2)}) copy-start(s32[8]{0:T(128)} %stack.625.info) | copy-start | bytes 100
  470.1 29.5 %collective-permute-start.10 = (f32[2,32,256]{2,1,0:T(8,128)}, f32[2,32,256]{2,1,0:T(8,128)}, u32[]{:S(2)}, u32[]{:S(2)}) collective-permute-start(f32[2,32,256]{2,1,0:T(8,128)} %slice.168), channel_id=1, source_target_pairs={{0,32},{32,64},{64,96},{128,160},{160,192},{192,224},{256,288},{28... | collective-permute-start | bytes 196616 | tf_op jit(solution)/shard_map/ppermute | solution.py:285
  487.6 47.0 %collective-permute-start.11 = (f32[2,32,256]{2,1,0:T(8,128)}, f32[2,32,256]{2,1,0:T(8,128)}, u32[]{:S(2)}, u32[]{:S(2)}) collective-permute-start(f32[2,32,256]{2,1,0:T(8,128)} %slice.170), channel_id=1, source_target_pairs={{0,32},{32,64},{64,96},{128,160},{160,192},{192,224},{256,288},{28... | collective-permute-start | bytes 196616 | tf_op jit(solution)/shard_map/ppermute | solution.py:285
  510.6 23.9 %copy-start.33 = (f32[6,32,128]{2,1,0:T(8,128)S(1)}, f32[6,32,128]{2,1,0:T(8,128)}, u32[]{:S(2)}) copy-start(f32[6,32,128]{2,1,0:T(8,128)} %get-tuple-element.150.coef) | copy-start | bytes 294916
  510.6 23.9 %copy-start.47 = (s32[8]{0:T(128)S(1)}, s32[8]{0:T(128)}, u32[]{:S(2)}) copy-start(s32[8]{0:T(128)} %stack.611.info) | copy-start | bytes 100
  531.9 16.3 %collective-permute-start.12 = (f32[2,32,256]{2,1,0:T(8,128)S(1)}, f32[2,32,256]{2,1,0:T(8,128)S(1)}, u32[]{:S(2)}, u32[]{:S(2)}) collective-permute-start(f32[2,32,256]{2,1,0:T(8,128)S(1)} %slice.171), channel_id=1, source_target_pairs={{0,32},{32,64},{64,96},{128,160},{160,192},{192,224},{256,288},{28... | collective-permute-start | bytes 196616 | tf_op jit(solution)/shard_map/ppermute | solution.py:285
  546.6 15.6 %collective-permute-start.13 = (f32[2,32,256]{2,1,0:T(8,128)S(1)}, f32[2,32,256]{2,1,0:T(8,128)S(1)}, u32[]{:S(2)}, u32[]{:S(2)}) collective-permute-start(f32[2,32,256]{2,1,0:T(8,128)S(1)} %slice.172), channel_id=1, source_target_pairs={{0,32},{32,64},{64,96},{128,160},{160,192},{192,224},{256,288},{28... | collective-permute-start | bytes 196616 | tf_op jit(solution)/shard_map/ppermute | solution.py:285
  548.3 13.9 %copy-start.31 = (f32[6,32,128]{2,1,0:T(8,128)S(1)}, f32[6,32,128]{2,1,0:T(8,128)}, u32[]{:S(2)}) copy-start(f32[6,32,128]{2,1,0:T(8,128)} %get-tuple-element.152.coef) | copy-start | bytes 294916
  548.3 13.9 %copy-start.45 = (s32[8]{0:T(128)S(1)}, s32[8]{0:T(128)}, u32[]{:S(2)}) copy-start(s32[8]{0:T(128)} %stack.597.info) | copy-start | bytes 100
  560.6 14.9 %collective-permute-start.14 = (f32[2,32,256]{2,1,0:T(8,128)S(1)}, f32[2,32,256]{2,1,0:T(8,128)S(1)}, u32[]{:S(2)}, u32[]{:S(2)}) collective-permute-start(f32[2,32,256]{2,1,0:T(8,128)S(1)} %slice.173), channel_id=1, source_target_pairs={{0,32},{32,64},{64,96},{128,160},{160,192},{192,224},{256,288},{28... | collective-permute-start | bytes 196616 | tf_op jit(solution)/shard_map/ppermute | solution.py:285
  573.8 14.9 %collective-permute-start.15 = (f32[2,32,256]{2,1,0:T(8,128)S(1)}, f32[2,32,256]{2,1,0:T(8,128)S(1)}, u32[]{:S(2)}, u32[]{:S(2)}) collective-permute-start(f32[2,32,256]{2,1,0:T(8,128)S(1)} %slice.174), channel_id=1, source_target_pairs={{0,32},{32,64},{64,96},{128,160},{160,192},{192,224},{256,288},{28... | collective-permute-start | bytes 196616 | tf_op jit(solution)/shard_map/ppermute | solution.py:285
  578.7 23.3 %collective-permute-start.16 = (f32[2,32,256]{2,1,0:T(8,128)S(1)}, f32[2,32,256]{2,1,0:T(8,128)S(1)}, u32[]{:S(2)}, u32[]{:S(2)}) collective-permute-start(f32[2,32,256]{2,1,0:T(8,128)S(1)} %slice.175), channel_id=1, source_target_pairs={{0,32},{32,64},{64,96},{128,160},{160,192},{192,224},{256,288},{28... | collective-permute-start | bytes 196616 | tf_op jit(solution)/shard_map/ppermute | solution.py:285
  591.9 22.3 %collective-permute-start.17 = (f32[2,32,256]{2,1,0:T(8,128)S(1)}, f32[2,32,256]{2,1,0:T(8,128)S(1)}, u32[]{:S(2)}, u32[]{:S(2)}) collective-permute-start(f32[2,32,256]{2,1,0:T(8,128)S(1)} %slice.176), channel_id=1, source_target_pairs={{0,32},{32,64},{64,96},{128,160},{160,192},{192,224},{256,288},{28... | collective-permute-start | bytes 196616 | tf_op jit(solution)/shard_map/ppermute | solution.py:285
  612.6 6.6 collective-permute-start.18
  617.5 5.0 collective-permute-start.19
  664.1 14.2 %copy-start.1 = (f32[4,1,32,4,256]{4,3,2,1,0:T(4,128)S(1)}, f32[4,1,32,4,256]{4,3,2,1,0:T(4,128)}, u32[]{:S(2)}) copy-start(f32[4,1,32,4,256]{4,3,2,1,0:T(4,128)} %param.6) | copy-start | bytes 1572868
  (42 other events, 136.1 us)
Sparse Core Ops, SparseCore 0:
  41.0 115.8 all-gather.33
  159.0 72.2 all-gather.35
  233.4 88.0 all-gather.37
  323.3 86.3 all-gather.39
  411.7 87.8 all-gather.41
  625.8 38.2 all-gather.43

commit v2 on v1

v2 whole, which is shorter than its diff:
```python
import jax
import jax.numpy as jnp
from jax import lax
from jax.experimental import pallas as pl
from jax.experimental.pallas import tpu as pltpu
from jax.sharding import PartitionSpec as P

STEPS = 2
loss_rate = 0.2
recovery = 0.8
F32 = jnp.float32
BF16 = jnp.bfloat16

ROWS = 16
GROUP = 4
HALF = 384
PAY = 288 + HALF
LAG = 2


def section_kernel(info, e_in, halo, msg, here, taps_in, e_out, pay, taps_out, mid, w_hi, w_lo):
    active, first, core, keep, keep_row, slot = (info[k] for k in range(6))
    lane = lax.broadcasted_iota(jnp.int32, (32, 128), 1)
    other = 1 - core
    coefs = [here[HALF + 16 * k : HALF + 16 * k + 16, :] for k in range(6)]
    coefs = [jnp.concatenate([v[:, 0:128], v[:, 128:256]], axis=0) for v in coefs]
    pay[288:, :] = here[0:HALF, :]

    @pl.when(active == 0)
    def _():
        e_out[...] = e_in[...]
        pay[0:128, :] = e_in[ROWS - 1].reshape(128, 256)
        pay[128:256, :] = e_in[ROWS - 2].reshape(128, 256)
        pay[256:288, :] = jnp.zeros((32, 256), F32)

    @pl.when(active == 1)
    def _():
        for k in range(2):
            w = halo[k, 288 : 288 + HALF, :]
            hi = w.astype(BF16)
            w_hi[k * HALF : (k + 1) * HALF, :] = hi
            w_lo[k * HALF : (k + 1) * HALF, :] = (w - hi.astype(F32)).astype(BF16)

        theirs = pltpu.roll(msg[other, :, 0:128], 1, 1)
        received = jnp.where(lane == ROWS, theirs, msg[core, :, 0:128])
        n = jnp.where(first == 1, coefs[0], received)
        gain_n = coefs[1] * n

        def products(x):
            rows = x.shape[0]
            flat = x.reshape(rows * 4, 32, 256)
            hi = flat.astype(BF16)
            lo = (flat - hi.astype(F32)).astype(BF16)
            zero = jnp.zeros((32, 256), BF16)

            def wide(v):
                parts = []
                for i in range(rows * 4):
                    b = i % 4
                    before = v[i - 1] if b > 0 else zero
                    after = v[i + 1] if b < 3 else zero
                    parts.append(jnp.concatenate([before, v[i], after], axis=1))
                return jnp.concatenate(parts, axis=0)

            hi, lo = wide(hi), wide(lo)
            y = jnp.dot(hi, w_hi[...], preferred_element_type=F32)
            y += jnp.dot(lo, w_hi[...], preferred_element_type=F32)
            y += jnp.dot(hi, w_lo[...], preferred_element_type=F32)
            return y.reshape(rows, 4, 32, 256)

        def rows_step(get, row_before, row_after, dst, base, count, last_n):
            turn_by = (128 - base) % 128 if isinstance(base, int) else lax.rem(128 - base, 128)
            gn, n_here, c_prev, c_next, c_left, c_right = (
                pltpu.roll(v, turn_by, 1) for v in (gain_n, n, *coefs[2:])
            )
            x = get(base, count)
            y = products(x)
            for r in range(count):
                before = row_before if r == 0 else x[r - 1]
                after = row_after if r == count - 1 else x[r + 1]
                cp, cn = c_prev[:, r : r + 1], c_next[:, r : r + 1]
                cl, cr = c_left[:, r : r + 1], c_right[:, r : r + 1]
                linear = []
                power = jnp.zeros((32, 128), F32)
                for b in range(4):
                    own = x[r, b]
                    spread = (
                        cp * before[b]
                        + cn * after[b]
                        + cl * pltpu.roll(own, 1, 0)
                        + cr * pltpu.roll(own, 31, 0)
                    )
                    re = y[r, b, :, 0:128] - spread[:, 128:256]
                    im = y[r, b, :, 128:256] + spread[:, 0:128]
                    power += re * re + im * im
                    linear.append((re, im))
                mean = jnp.sum(power, axis=1, keepdims=True) * (1.0 / 512.0)
                factor = jnp.exp(0.5 * (gn[:, r : r + 1] / (1.0 + mean) - loss_rate))
                for b in range(4):
                    dst[base + r, b, :, 0:128] = factor * linear[b][0]
                    dst[base + r, b, :, 128:256] = factor * linear[b][1]
                if last_n is not None:
                    leaving = factor * factor * mean
                    updated = 1.0 - recovery * (1.0 - n_here[:, r : r + 1] / (1.0 + leaving))
                    last_n = jnp.where(lane == base + r, updated, last_n)
            return last_n

        near = halo[other, 0:128, :].reshape(4, 32, 256)
        far = halo[other, 128:256, :].reshape(4, 32, 256)

        def get_e(base, count):
            return e_in[pl.ds(base, count)]

        def get_mid(base, count):
            return mid[pl.ds(base, count)]

        def one(g, carry):
            base = g * GROUP
            rows_step(get_e, e_in[jnp.maximum(base - 1, 0)], e_in[base + GROUP], mid, base, GROUP, None)
            return carry

        def two(g, last_n):
            base = g * GROUP
            before = mid[jnp.maximum(base - 1, 0)]
            return rows_step(get_mid, before, mid[base + GROUP], e_out, base, GROUP, last_n)

        last = ROWS - GROUP
        lax.fori_loop(0, ROWS // GROUP - 1, one, 0)
        rows_step(get_e, e_in[last - 1], near, mid, last, GROUP, None)
        rows_step(lambda *_: near[None], e_in[ROWS - 1], far, mid, ROWS, 1, None)
        last_n = lax.fori_loop(0, ROWS // GROUP, two, jnp.zeros((32, 128), F32))

        @pl.when(keep == 1)
        def _():
            taps_out[slot] = e_out[pl.ds(keep_row, 2)]

        pay[0:128, :] = e_out[ROWS - 1].reshape(128, 256)
        pay[128:256, :] = e_out[ROWS - 2].reshape(128, 256)
        pay[256:288, 0:128] = last_n
        pay[256:288, 128:256] = last_n


def section_call(info, e, halo, msg, here, taps):
    vmem = pl.BlockSpec(memory_space=pltpu.VMEM)
    return pl.pallas_call(
        section_kernel,
        out_shape=(
            jax.ShapeDtypeStruct((ROWS, 4, 32, 256), F32),
            jax.ShapeDtypeStruct((PAY, 256), F32),
            jax.ShapeDtypeStruct(taps.shape, F32),
        ),
        in_specs=[pl.BlockSpec(memory_space=pltpu.SMEM)] + [vmem] * 5,
        out_specs=(vmem, vmem, vmem),
        scratch_shapes=[
            pltpu.VMEM((ROWS + 1, 4, 32, 256), F32),
            pltpu.VMEM((768, 256), BF16),
            pltpu.VMEM((768, 256), BF16),
        ],
        input_output_aliases={5: 2},
        compiler_params=pltpu.CompilerParams(vmem_limit_bytes=40 * 1024 * 1024),
        name="section",
    )(info, e, halo, msg, here, taps)


def local(input_fields, injection_order, dispersion, coupling, amplifier_gain, inversion):
    seg, row = lax.axis_index("segment"), lax.axis_index("row")
    x, z_lo = seg % 4, seg // 4
    core, y, z_hi = row % 2, (row // 2) % 8, row // 16
    chips = [[2 * k, 2 * k + 1] for k in range(16)]
    rings = [[4 * k + i for i in range(4)] for k in range(4)]
    columns = [[16 * h + 2 * k + c for k in range(8)] for h in range(2) for c in range(2)]
    across = [(17 * h + 2 * k, 16 * (1 - h) + 2 * k + h) for h in range(2) for k in range(8)]
    ahead = [(g, g + 1) for g in range(16) if g % 4 < 3]

    half = lax.dynamic_slice_in_dim(dispersion[0], HALF * core, HALF, 0)
    w_all = lax.all_gather(half, "segment")

    own = jnp.concatenate([inversion[0], amplifier_gain[0], coupling[0, :, 0]], axis=0)
    own = jnp.pad(own.reshape(1, 192), ((0, 0), (0, 64)))
    row_coefs = lax.all_to_all(jnp.broadcast_to(own[None], (16, 1, 256)), "segment", 0, 0)[:, 0]

    field = lax.dynamic_index_in_dim(input_fields, injection_order[x], 0, keepdims=False)[0]
    field = field.transpose(1, 0, 2).reshape(128, 256)
    pair = lax.all_gather(
        jnp.concatenate([field, row_coefs], axis=0), "row", axis_index_groups=chips
    )
    pair = jnp.where(core == z_hi, pair, lax.ppermute(pair, "row", across))
    rows = lax.all_to_all(
        jnp.broadcast_to(pair[None], (8, 2, 144, 256)), "row", 0, 0, axis_index_groups=columns
    ).reshape(ROWS, 144, 256)
    rows = jnp.where(core == 0, rows, jnp.flip(rows, 0))
    e = rows[:, :128].reshape(ROWS, 4, 32, 256)
    sibling = lax.all_gather(rows[ROWS - 1, 128:], "row", axis_index_groups=chips)
    sibling = lax.dynamic_index_in_dim(sibling, 1 - core, 0)
    table = jnp.concatenate([rows[:, 128:], sibling], axis=0)[:, :, :192]
    table = table.reshape(ROWS + 1, 16, 6, 32).transpose(1, 2, 3, 0)
    n0, gain, up, down, left, right = (table[:, k] for k in range(6))
    before = jnp.where(core == 0, up, down)
    after = jnp.where(core == 0, down, up)
    at_row = jnp.arange(ROWS + 1)[None, None, :]
    at_col = jnp.arange(32)[None, :, None]
    before = jnp.where(at_row == 0, 0.0, before)
    left = jnp.where(at_col == 0, 0.0, left)
    right = jnp.where(at_col == 31, 0.0, right)
    table = jnp.stack([n0, gain, before, after, left, right], axis=1)
    table = jnp.pad(table, ((0, 0), (0, 0), (0, 0), (0, 128 - ROWS - 1)))
    table = jnp.concatenate([table[:, :, :16], table[:, :, 16:]], axis=3).reshape(16, 96, 256)

    turns = 16 + 3 * LAG

    def section_at(turn):
        return jnp.clip(turn - LAG * x, 0, 15)

    def here_at(turn):
        w = lax.dynamic_index_in_dim(w_all, section_at(turn + 1), 0, keepdims=False)
        coef = lax.dynamic_index_in_dim(table, section_at(turn), 0, keepdims=False)
        return jnp.concatenate([w, coef], axis=0)

    first_pay = jnp.concatenate(
        [e[ROWS - 1].reshape(128, 256), e[ROWS - 2].reshape(128, 256), jnp.zeros((32, 256), F32), w_all[0]],
        axis=0,
    )
    halo = lax.all_gather(first_pay, "row", axis_index_groups=chips)
    taps = jnp.zeros((4, 2, 4, 32, 256), F32)
    keep_row = jnp.where(core == 0, 2 * y, 14 - 2 * y)
    msgs = {}
    for turn in range(turns):
        section = turn - LAG * x
        active = jnp.logical_and(section >= 0, section < 16)
        at = section_at(turn)
        keep = active & (at // 4 == z_lo) & (core == z_hi)
        info = jnp.stack([active, x == 0, core, keep, keep_row, at % 4]).astype(jnp.int32)
        msg = msgs.pop(turn - LAG, None)
        if msg is None:
            msg = jnp.zeros((2, 32, 256), F32)
        e, pay, taps = section_call(info, e, halo, msg, here_at(turn), taps)
        if turn + 1 < turns:
            halo = lax.all_gather(pay, "row", axis_index_groups=chips)
        if turn + LAG < turns:
            msgs[turn] = lax.ppermute(halo[:, 256:288], "segment", ahead)

    taps = jnp.where(z_hi == 0, taps, jnp.flip(taps, 1)).swapaxes(0, 1)
    both = lax.all_to_all(taps, "row", 0, 0, axis_index_groups=chips)
    mine = lax.dynamic_index_in_dim(both, z_hi, 0, keepdims=False)
    out = lax.all_to_all(mine, "segment", 0, 0, axis_index_groups=rings)
    return out.transpose(0, 2, 1, 3)[None, :, None]


def solution(mesh):
    return jax.shard_map(
        local,
        mesh=mesh,
        in_specs=(
            P(None, "row", None, None, None),
            P(),
            P("segment", None, None),
            P("segment", None, "row", None),
            P("segment", "row", None),
            P("segment", "row", None),
        ),
        out_specs=P("segment", None, "row", None, None, None),
        check_vma=False,
    )
```

time: 695 us -> 894 us (1.29)
  the two profiles are of different devices: /device:TPU:1 before, /device:TPU:8 now
where the time goes in v2:
time: 894 us; the launch traced here: 882 us
  waiting for transfers between devices  356 us (40%)
  local copies, waits for them, and re-layouts  168 us (19%)
  Pallas kernels  162 us (18%)
  starting transfers between devices  103 us (12%)
  other arithmetic  45.9 us (5%)
  blocking collectives  29.2 us (3%)
  between operations  17 us (2%)
    all_gather x21, waiting for transfers between devices, local(): halo = lax.all_gather(pay, 'row', axis_index_groups=chips)  286 us
    pallas_call x22, Pallas kernels, section_call(): pl.pallas_call(section_kernel, out_shape=(jax.ShapeDtypeStruct((ROWS, 4,...  162 us
    unnamed x183, local copies, waits for them, and re-layouts  104 us
    ppermute x20, starting transfers between devices, local(): msgs[turn] = lax.ppermute(halo[:, 256:288], 'segment', ahead)  75.7 us
    all_to_all x1, waiting for transfers between devices, local(): lax.all_to_all(jnp.broadcast_to(pair[None], (8, 2, 144, 256)), 'row', 0,...  51.7 us
    concatenate x22, other arithmetic, here_at(): return jnp.concatenate([w, coef], axis=0)  36.8 us
    all_to_all x1, blocking collectives, local(): out = lax.all_to_all(mine, 'segment', 0, 0, axis_index_groups=rings)  20.6 us
  transfers between devices with their start and end apart: 46, of which 30 were waited for; matrix products, arithmetic and copies ran while one was open for 12% of the time, Pallas kernels for 0%

profile of v2, /device:TPU:8, one launch (start us, length us, event | category | flops | bytes accessed | tf_op | source)
XLA Modules:
  0.0 881.6 jit_solution(2852327848522514547)
XLA Ops:
  9.9 9.8 %all-to-all-start = ((f32[16,1,256]{2,1,0:T(1,128)}), f32[16,1,256]{2,1,0:T(1,128)S(1)}, u32[]{:S(2)}, u32[]{:S(2)}) async-start(f32[16,1,256]{2,1,0:T(1,128)} %broadcast_in_dim.54), calls=%async_computation | async-start | bytes 32768 | tf_op jit(solution)/shard_map/all_to_all | solution.py:180
  29.7 8.2 collective-permute-start
  38.0 10.7 %collective-permute-done = f32[2,144,256]{2,1,0:T(8,128)S(1)} collective-permute-done((f32[2,144,256]{2,1,0:T(8,128)S(1)}, f32[2,144,256]{2,1,0:T(8,128)S(1)}, u32[]{:S(2)}, u32[]{:S(2)}) %collective-permute-start) | collective-permute-done | bytes 294944 | tf_op jit(solution)/shard_map/ppermute | solution.py:187
  50.4 8.0 all-to-all-start.1
  58.6 51.7 %all-to-all-done.1 = f32[8,2,144,256]{3,2,1,0:T(8,128)} async-done(((f32[8,2,144,256]{3,2,1,0:T(8,128)}), f32[8,2,144,256]{3,2,1,0:T(8,128)}, u32[]{:S(2)}, u32[]{:S(2)}) %all-to-all-start.1) | async-done | bytes 2359328 | tf_op jit(solution)/shard_map/all_to_all | solution.py:188
  128.1 8.2 pad_slice_fusion.1
  136.4 6.0 copy.58
  142.3 6.6 copy.59
  154.7 9.0 %section.22 = (f32[16,4,32,256]{3,2,1,0:T(8,128)S(1)}, f32[672,256]{1,0:T(8,128)S(1)}, f32[4,2,4,32,256]{4,3,2,1,0:T(8,128)S(1)}) custom-call(s32[6]{0:T(128)S(1)} %stack.614.info, f32[16,4,32,256]{3,2,1,0:T(8,128)S(1)} %bitcast.210, f32[2,672,256]{2,1,0:T(8,128)S(1)} %bitcast.252, ...), custom_call_target="tpu_custom_call", output_to_operand_aliasing={{2}: (5, {})} | custom-call | tf_op jit(solution)/shard_map/section/pallas_call | solution.py:145
  168.1 16.7 %all-gather.51.cloned.1.call-done = f32[1344,256]{1,0:T(8,128)} async-done(((f32[672,256]{1,0:T(8,128)}), f32[1344,256]{1,0:T(8,128)}) %all-gather.51.cloned.1.call-update) | async-done | bytes 1376272 | tf_op jit(solution)/shard_map/all_gather | solution.py:238
  188.7 9.8 %section.23 = (f32[16,4,32,256]{3,2,1,0:T(8,128)S(1)}, f32[672,256]{1,0:T(8,128)S(1)}, f32[4,2,4,32,256]{4,3,2,1,0:T(8,128)S(1)}) custom-call(s32[6]{0:T(128)S(1)} %stack.608.info, f32[16,4,32,256]{3,2,1,0:T(8,128)S(1)} %copy-done.23, f32[2,672,256]{2,1,0:T(8,128)S(1)} %bitcast.250, ...), custom_call_target="tpu_custom_call", output_to_operand_aliasing={{2}: (5, {})} | custom-call | tf_op jit(solution)/shard_map/section/pallas_call | solution.py:145
  204.9 12.8 %all-gather.53.cloned.1.call-done = f32[1344,256]{1,0:T(8,128)} async-done(((f32[672,256]{1,0:T(8,128)}), f32[1344,256]{1,0:T(8,128)}) %all-gather.53.cloned.1.call-update) | async-done | bytes 1376272 | tf_op jit(solution)/shard_map/all_gather | solution.py:238
  220.1 9.0 %section.24 = (f32[16,4,32,256]{3,2,1,0:T(8,128)S(1)}, f32[672,256]{1,0:T(8,128)S(1)}, f32[4,2,4,32,256]{4,3,2,1,0:T(8,128)S(1)}) custom-call(s32[6]{0:T(128)S(1)} %stack.602.info, f32[16,4,32,256]{3,2,1,0:T(8,128)S(1)} %get-tuple-element.72.e_in, f32[2,672,256]{2,1,0:T(8,128)S(1)} %bitcast.218, ...), custom_call_target="tpu_custom_call", output_to_operand_aliasing={{2}: (5, {})} | custom-call | tf_op jit(solution)/shard_map/section/pallas_call | solution.py:145
  237.7 11.3 %all-gather.55.cloned.1.call-done = f32[1344,256]{1,0:T(8,128)} async-done(((f32[672,256]{1,0:T(8,128)}), f32[1344,256]{1,0:T(8,128)}) %all-gather.55.cloned.1.call-update) | async-done | bytes 1376272 | tf_op jit(solution)/shard_map/all_gather | solution.py:238
  253.0 9.0 %section.25 = (f32[16,4,32,256]{3,2,1,0:T(8,128)S(1)}, f32[672,256]{1,0:T(8,128)S(1)}, f32[4,2,4,32,256]{4,3,2,1,0:T(8,128)S(1)}) custom-call(s32[6]{0:T(128)S(1)} %stack.596.info, f32[16,4,32,256]{3,2,1,0:T(8,128)S(1)} %copy-done.3, f32[2,672,256]{2,1,0:T(8,128)S(1)} %bitcast.212, ...), custom_call_target="tpu_custom_call", output_to_operand_aliasing={{2}: (5, {})} | custom-call | tf_op jit(solution)/shard_map/section/pallas_call | solution.py:145
  266.2 6.5 dynamic-slice_bitcast_fusion.1
  282.8 9.0 %section.26 = (f32[16,4,32,256]{3,2,1,0:T(8,128)S(1)}, f32[672,256]{1,0:T(8,128)S(1)}, f32[4,2,4,32,256]{4,3,2,1,0:T(8,128)S(1)}) custom-call(s32[6]{0:T(128)S(1)} %stack.590.info, f32[16,4,32,256]{3,2,1,0:T(8,128)S(1)} %get-tuple-element.78.e_in, f32[2,672,256]{2,1,0:T(8,128)S(1)} %bitcast.214, ...), custom_call_target="tpu_custom_call", output_to_operand_aliasing={{2}: (5, {})} | custom-call | tf_op jit(solution)/shard_map/section/pallas_call | solution.py:145
  300.4 12.8 %all-gather.59.cloned.1.call-done = f32[1344,256]{1,0:T(8,128)} async-done(((f32[672,256]{1,0:T(8,128)}), f32[1344,256]{1,0:T(8,128)}) %all-gather.59.cloned.1.call-update) | async-done | bytes 1376272 | tf_op jit(solution)/shard_map/all_gather | solution.py:238
  317.2 9.5 %section.27 = (f32[16,4,32,256]{3,2,1,0:T(8,128)S(1)}, f32[672,256]{1,0:T(8,128)S(1)}, f32[4,2,4,32,256]{4,3,2,1,0:T(8,128)S(1)}) custom-call(s32[6]{0:T(128)S(1)} %stack.584.info, f32[16,4,32,256]{3,2,1,0:T(8,128)S(1)} %copy-done.5, f32[2,672,256]{2,1,0:T(8,128)S(1)} %bitcast.220, ...), custom_call_target="tpu_custom_call", output_to_operand_aliasing={{2}: (5, {})} | custom-call | tf_op jit(solution)/shard_map/section/pallas_call | solution.py:145
  333.8 12.8 %all-gather.61.cloned.1.call-done = f32[1344,256]{1,0:T(8,128)} async-done(((f32[672,256]{1,0:T(8,128)}), f32[1344,256]{1,0:T(8,128)}) %all-gather.61.cloned.1.call-update) | async-done | bytes 1376272 | tf_op jit(solution)/shard_map/all_gather | solution.py:238
  349.0 9.0 %section.28 = (f32[16,4,32,256]{3,2,1,0:T(8,128)S(1)}, f32[672,256]{1,0:T(8,128)S(1)}, f32[4,2,4,32,256]{4,3,2,1,0:T(8,128)S(1)}) custom-call(s32[6]{0:T(128)S(1)} %stack.578.info, f32[16,4,32,256]{3,2,1,0:T(8,128)S(1)} %get-tuple-element.84.e_in, f32[2,672,256]{2,1,0:T(8,128)S(1)} %bitcast.222, ...), custom_call_target="tpu_custom_call", output_to_operand_aliasing={{2}: (5, {})} | custom-call | tf_op jit(solution)/shard_map/section/pallas_call | solution.py:145
  366.6 12.9 %all-gather.63.cloned.1.call-done = f32[1344,256]{1,0:T(8,128)} async-done(((f32[672,256]{1,0:T(8,128)}), f32[1344,256]{1,0:T(8,128)}) %all-gather.63.cloned.1.call-update) | async-done | bytes 1376272 | tf_op jit(solution)/shard_map/all_gather | solution.py:238
  383.4 9.0 %section.29 = (f32[16,4,32,256]{3,2,1,0:T(8,128)S(1)}, f32[672,256]{1,0:T(8,128)S(1)}, f32[4,2,4,32,256]{4,3,2,1,0:T(8,128)S(1)}) custom-call(s32[6]{0:T(128)S(1)} %stack.572.info, f32[16,4,32,256]{3,2,1,0:T(8,128)S(1)} %copy-done.7, f32[2,672,256]{2,1,0:T(8,128)S(1)} %bitcast.224, ...), custom_call_target="tpu_custom_call", output_to_operand_aliasing={{2}: (5, {})} | custom-call | tf_op jit(solution)/shard_map/section/pallas_call | solution.py:145
  399.6 12.9 %all-gather.65.cloned.1.call-done = f32[1344,256]{1,0:T(8,128)} async-done(((f32[672,256]{1,0:T(8,128)}), f32[1344,256]{1,0:T(8,128)}) %all-gather.65.cloned.1.call-update) | async-done | bytes 1376272 | tf_op jit(solution)/shard_map/all_gather | solution.py:238
  414.8 9.0 %section.30 = (f32[16,4,32,256]{3,2,1,0:T(8,128)S(1)}, f32[672,256]{1,0:T(8,128)S(1)}, f32[4,2,4,32,256]{4,3,2,1,0:T(8,128)S(1)}) custom-call(s32[6]{0:T(128)S(1)} %stack.566.info, f32[16,4,32,256]{3,2,1,0:T(8,128)S(1)} %get-tuple-element.90.e_in, f32[2,672,256]{2,1,0:T(8,128)S(1)} %bitcast.226, ...), custom_call_target="tpu_custom_call", output_to_operand_aliasing={{2}: (5, {})} | custom-call | tf_op jit(solution)/shard_map/section/pallas_call | solution.py:145
  432.4 12.8 %all-gather.67.cloned.1.call-done = f32[1344,256]{1,0:T(8,128)} async-done(((f32[672,256]{1,0:T(8,128)}), f32[1344,256]{1,0:T(8,128)}) %all-gather.67.cloned.1.call-update) | async-done | bytes 1376272 | tf_op jit(solution)/shard_map/all_gather | solution.py:238
  449.2 9.6 %section.31 = (f32[16,4,32,256]{3,2,1,0:T(8,128)S(1)}, f32[672,256]{1,0:T(8,128)S(1)}, f32[4,2,4,32,256]{4,3,2,1,0:T(8,128)S(1)}) custom-call(s32[6]{0:T(128)S(1)} %stack.560.info, f32[16,4,32,256]{3,2,1,0:T(8,128)S(1)} %copy-done.9, f32[2,672,256]{2,1,0:T(8,128)S(1)} %bitcast.228, ...), custom_call_target="tpu_custom_call", output_to_operand_aliasing={{2}: (5, {})} | custom-call | tf_op jit(solution)/shard_map/section/pallas_call | solution.py:145
  466.0 12.8 %all-gather.69.cloned.1.call-done = f32[1344,256]{1,0:T(8,128)} async-done(((f32[672,256]{1,0:T(8,128)}), f32[1344,256]{1,0:T(8,128)}) %all-gather.69.cloned.1.call-update) | async-done | bytes 1376272 | tf_op jit(solution)/shard_map/all_gather | solution.py:238
  481.2 9.0 %section.32 = (f32[16,4,32,256]{3,2,1,0:T(8,128)S(1)}, f32[672,256]{1,0:T(8,128)S(1)}, f32[4,2,4,32,256]{4,3,2,1,0:T(8,128)S(1)}) custom-call(s32[6]{0:T(128)S(1)} %stack.554.info, f32[16,4,32,256]{3,2,1,0:T(8,128)S(1)} %get-tuple-element.96.e_in, f32[2,672,256]{2,1,0:T(8,128)S(1)} %bitcast.230, ...), custom_call_target="tpu_custom_call", output_to_operand_aliasing={{2}: (5, {})} | custom-call | tf_op jit(solution)/shard_map/section/pallas_call | solution.py:145
  498.8 12.8 %all-gather.71.cloned.1.call-done = f32[1344,256]{1,0:T(8,128)} async-done(((f32[672,256]{1,0:T(8,128)}), f32[1344,256]{1,0:T(8,128)}) %all-gather.71.cloned.1.call-update) | async-done | bytes 1376272 | tf_op jit(solution)/shard_map/all_gather | solution.py:238
  515.6 9.0 %section.33 = (f32[16,4,32,256]{3,2,1,0:T(8,128)S(1)}, f32[672,256]{1,0:T(8,128)S(1)}, f32[4,2,4,32,256]{4,3,2,1,0:T(8,128)S(1)}) custom-call(s32[6]{0:T(128)S(1)} %stack.548.info, f32[16,4,32,256]{3,2,1,0:T(8,128)S(1)} %copy-done.11, f32[2,672,256]{2,1,0:T(8,128)S(1)} %bitcast.232, ...), custom_call_target="tpu_custom_call", output_to_operand_aliasing={{2}: (5, {})} | custom-call | tf_op jit(solution)/shard_map/section/pallas_call | solution.py:145
  531.8 12.8 %all-gather.73.cloned.1.call-done = f32[1344,256]{1,0:T(8,128)} async-done(((f32[672,256]{1,0:T(8,128)}), f32[1344,256]{1,0:T(8,128)}) %all-gather.73.cloned.1.call-update) | async-done | bytes 1376272 | tf_op jit(solution)/shard_map/all_gather | solution.py:238
  547.0 9.0 %section.34 = (f32[16,4,32,256]{3,2,1,0:T(8,128)S(1)}, f32[672,256]{1,0:T(8,128)S(1)}, f32[4,2,4,32,256]{4,3,2,1,0:T(8,128)S(1)}) custom-call(s32[6]{0:T(128)S(1)} %stack.542.info, f32[16,4,32,256]{3,2,1,0:T(8,128)S(1)} %get-tuple-element.102.e_in, f32[2,672,256]{2,1,0:T(8,128)S(1)} %bitcast.234, ...), custom_call_target="tpu_custom_call", output_to_operand_aliasing={{2}: (5, {})} | custom-call | tf_op jit(solution)/shard_map/section/pallas_call | solution.py:145
  564.6 12.8 %all-gather.75.cloned.1.call-done = f32[1344,256]{1,0:T(8,128)} async-done(((f32[672,256]{1,0:T(8,128)}), f32[1344,256]{1,0:T(8,128)}) %all-gather.75.cloned.1.call-update) | async-done | bytes 1376272 | tf_op jit(solution)/shard_map/all_gather | solution.py:238
  581.4 9.5 %section.35 = (f32[16,4,32,256]{3,2,1,0:T(8,128)S(1)}, f32[672,256]{1,0:T(8,128)S(1)}, f32[4,2,4,32,256]{4,3,2,1,0:T(8,128)S(1)}) custom-call(s32[6]{0:T(128)S(1)} %stack.536.info, f32[16,4,32,256]{3,2,1,0:T(8,128)S(1)} %copy-done.13, f32[2,672,256]{2,1,0:T(8,128)S(1)} %bitcast.236, ...), custom_call_target="tpu_custom_call", output_to_operand_aliasing={{2}: (5, {})} | custom-call | tf_op jit(solution)/shard_map/section/pallas_call | solution.py:145
  598.0 12.8 %all-gather.77.cloned.1.call-done = f32[1344,256]{1,0:T(8,128)} async-done(((f32[672,256]{1,0:T(8,128)}), f32[1344,256]{1,0:T(8,128)}) %all-gather.77.cloned.1.call-update) | async-done | bytes 1376272 | tf_op jit(solution)/shard_map/all_gather | solution.py:238
  613.2 9.0 %section.36 = (f32[16,4,32,256]{3,2,1,0:T(8,128)S(1)}, f32[672,256]{1,0:T(8,128)S(1)}, f32[4,2,4,32,256]{4,3,2,1,0:T(8,128)S(1)}) custom-call(s32[6]{0:T(128)S(1)} %stack.530.info, f32[16,4,32,256]{3,2,1,0:T(8,128)S(1)} %get-tuple-element.108.e_in, f32[2,672,256]{2,1,0:T(8,128)S(1)} %bitcast.238, ...), custom_call_target="tpu_custom_call", output_to_operand_aliasing={{2}: (5, {})} | custom-call | tf_op jit(solution)/shard_map/section/pallas_call | solution.py:145
  630.8 12.8 %all-gather.79.cloned.1.call-done = f32[1344,256]{1,0:T(8,128)} async-done(((f32[672,256]{1,0:T(8,128)}), f32[1344,256]{1,0:T(8,128)}) %all-gather.79.cloned.1.call-update) | async-done | bytes 1376272 | tf_op jit(solution)/shard_map/all_gather | solution.py:238
  647.6 9.0 %section.37 = (f32[16,4,32,256]{3,2,1,0:T(8,128)S(1)}, f32[672,256]{1,0:T(8,128)S(1)}, f32[4,2,4,32,256]{4,3,2,1,0:T(8,128)S(1)}) custom-call(s32[6]{0:T(128)S(1)} %stack.524.info, f32[16,4,32,256]{3,2,1,0:T(8,128)S(1)} %copy-done.15, f32[2,672,256]{2,1,0:T(8,128)S(1)} %bitcast.240, ...), custom_call_target="tpu_custom_call", output_to_operand_aliasing={{2}: (5, {})} | custom-call | tf_op jit(solution)/shard_map/section/pallas_call | solution.py:145
  663.7 12.8 %all-gather.81.cloned.1.call-done = f32[1344,256]{1,0:T(8,128)} async-done(((f32[672,256]{1,0:T(8,128)}), f32[1344,256]{1,0:T(8,128)}) %all-gather.81.cloned.1.call-update) | async-done | bytes 1376272 | tf_op jit(solution)/shard_map/all_gather | solution.py:238
  683.0 11.6 %collective-permute-start.16 = (f32[2,32,256]{2,1,0:T(8,128)S(1)}, f32[2,32,256]{2,1,0:T(8,128)S(1)}, u32[]{:S(2)}, u32[]{:S(2)}) collective-permute-start(f32[2,32,256]{2,1,0:T(8,128)S(1)} %slice.168), channel_id=1, source_target_pairs={{0,32},{32,64},{64,96},{128,160},{160,192},{192,224},{256,288},{28... | collective-permute-start | bytes 196616 | tf_op jit(solution)/shard_map/ppermute | solution.py:240
  696.6 12.8 %all-gather.83.cloned.1.call-done = f32[1344,256]{1,0:T(8,128)} async-done(((f32[672,256]{1,0:T(8,128)}), f32[1344,256]{1,0:T(8,128)}) %all-gather.83.cloned.1.call-update) | async-done | bytes 1376272 | tf_op jit(solution)/shard_map/all_gather | solution.py:238
  713.4 8.4 section.39
  730.3 12.8 %all-gather.85.cloned.1.call-done = f32[1344,256]{1,0:T(8,128)} async-done(((f32[672,256]{1,0:T(8,128)}), f32[1344,256]{1,0:T(8,128)}) %all-gather.85.cloned.1.call-update) | async-done | bytes 1376272 | tf_op jit(solution)/shard_map/all_gather | solution.py:238
  754.8 21.1 %all-gather.87.cloned.1.call-done = f32[1344,256]{1,0:T(8,128)} async-done(((f32[672,256]{1,0:T(8,128)}), f32[1344,256]{1,0:T(8,128)}) %all-gather.87.cloned.1.call-update) | async-done | bytes 1376272 | tf_op jit(solution)/shard_map/all_gather | solution.py:238
  788.1 21.1 %all-gather.89.cloned.1.call-done = f32[1344,256]{1,0:T(8,128)} async-done(((f32[672,256]{1,0:T(8,128)}), f32[1344,256]{1,0:T(8,128)}) %all-gather.89.cloned.1.call-update) | async-done | bytes 1376272 | tf_op jit(solution)/shard_map/all_gather | solution.py:238
  821.0 20.8 %all-gather.91.cloned.1.call-done = f32[1344,256]{1,0:T(8,128)} async-done(((f32[672,256]{1,0:T(8,128)}), f32[1344,256]{1,0:T(8,128)}) %all-gather.91.cloned.1.call-update) | async-done | bytes 1376272 | tf_op jit(solution)/shard_map/all_gather | solution.py:238
  853.1 20.6 %all_to_all.21 = f32[4,4,32,256]{3,2,1,0:T(8,128)S(1)} all-to-all(f32[4,4,32,256]{3,2,1,0:T(8,128)S(1)} %dynamic-slice_bitcast_fusion), channel_id=1, replica_groups={{0,32,64,96},{128,160,192,224},{256,288,320,352},{384,416,448,480},{1,3..., dimensions={0} | all-to-all | bytes 1048576 | tf_op jit(solution)/shard_map/all_to_all | solution.py:245
  (382 shorter events, 278.3 us)
Async XLA Ops:
  6.5 108.5 %all-gather.47.cloned.1.call-start = ((), (), s32[]{:S(2)}) async-start(), calls=%async_computation.4 | async-start | bytes 6684672 | tf_op jit(solution)/shard_map/all_gather | solution.py:176
  9.9 17.8 %all-to-all-start = ((f32[16,1,256]{2,1,0:T(1,128)}), f32[16,1,256]{2,1,0:T(1,128)S(1)}, u32[]{:S(2)}, u32[]{:S(2)}) async-start(f32[16,1,256]{2,1,0:T(1,128)} %broadcast_in_dim.54), calls=%async_computation | async-start | bytes 32768 | tf_op jit(solution)/shard_map/all_to_all | solution.py:180
  29.7 19.0 %collective-permute-start = (f32[2,144,256]{2,1,0:T(8,128)S(1)}, f32[2,144,256]{2,1,0:T(8,128)S(1)}, u32[]{:S(2)}, u32[]{:S(2)}) collective-permute-start(f32[2,144,256]{2,1,0:T(8,128)S(1)} %bitcast.258), channel_id=1, source_target_pairs={{0,16},{2,18},{4,20},{6,22},{8,24},{10,26},{12,28},{14,30},{17,1},... | collective-permute-start | bytes 884744 | tf_op jit(solution)/shard_map/ppermute | solution.py:187
  50.4 59.9 %all-to-all-start.1 = ((f32[8,2,144,256]{3,2,1,0:T(8,128)}), f32[8,2,144,256]{3,2,1,0:T(8,128)}, u32[]{:S(2)}, u32[]{:S(2)}) async-start(f32[8,2,144,256]{3,2,1,0:T(8,128)} %broadcast_in_dim.55), calls=%async_computation.1 | async-start | bytes 4718592 | tf_op jit(solution)/shard_map/all_to_all | solution.py:188
  58.4 93.8 %all-gather.49.cloned.1.call-start = ((), (), s32[]{:S(2)}) async-start(), calls=%async_computation.5 | async-start | bytes 2064384 | tf_op jit(solution)/shard_map/all_gather | solution.py:223
  118.7 66.0 %all-gather.51.cloned.1.call-start = ((), (), s32[]{:S(2)}) async-start(), calls=%async_computation.6 | async-start | bytes 2064384 | tf_op jit(solution)/shard_map/all_gather | solution.py:238
  166.1 51.7 %all-gather.53.cloned.1.call-start = ((), (), s32[]{:S(2)}) async-start(), calls=%async_computation.7 | async-start | bytes 2064384 | tf_op jit(solution)/shard_map/all_gather | solution.py:238
  199.4 49.6 %all-gather.55.cloned.1.call-start = ((), (), s32[]{:S(2)}) async-start(), calls=%async_computation.8 | async-start | bytes 2064384 | tf_op jit(solution)/shard_map/all_gather | solution.py:238
  200.4 4.5 collective-permute-start.1
  231.4 49.1 %all-gather.57.cloned.1.call-start = ((), (), s32[]{:S(2)}) async-start(), calls=%async_computation.9 | async-start | bytes 2064384 | tf_op jit(solution)/shard_map/all_gather | solution.py:238
  232.4 5.3 collective-permute-start.2
  262.9 50.4 %all-gather.59.cloned.1.call-start = ((), (), s32[]{:S(2)}) async-start(), calls=%async_computation.10 | async-start | bytes 2064384 | tf_op jit(solution)/shard_map/all_gather | solution.py:238
  273.5 4.7 collective-permute-start.3
  294.1 52.6 %all-gather.61.cloned.1.call-start = ((), (), s32[]{:S(2)}) async-start(), calls=%async_computation.11 | async-start | bytes 2064384 | tf_op jit(solution)/shard_map/all_gather | solution.py:238
  295.1 5.3 collective-permute-start.4
  327.5 52.0 %all-gather.63.cloned.1.call-start = ((), (), s32[]{:S(2)}) async-start(), calls=%async_computation.12 | async-start | bytes 2064384 | tf_op jit(solution)/shard_map/all_gather | solution.py:238
  328.5 5.3 collective-permute-start.5
  360.3 52.1 %all-gather.65.cloned.1.call-start = ((), (), s32[]{:S(2)}) async-start(), calls=%async_computation.13 | async-start | bytes 2064384 | tf_op jit(solution)/shard_map/all_gather | solution.py:238
  361.4 5.3 collective-permute-start.6
  393.3 51.9 %all-gather.67.cloned.1.call-start = ((), (), s32[]{:S(2)}) async-start(), calls=%async_computation.14 | async-start | bytes 2064384 | tf_op jit(solution)/shard_map/all_gather | solution.py:238
  394.3 5.3 collective-permute-start.7
  426.1 52.7 %all-gather.69.cloned.1.call-start = ((), (), s32[]{:S(2)}) async-start(), calls=%async_computation.15 | async-start | bytes 2064384 | tf_op jit(solution)/shard_map/all_gather | solution.py:238
  427.1 5.3 collective-permute-start.8
  459.7 51.9 %all-gather.71.cloned.1.call-start = ((), (), s32[]{:S(2)}) async-start(), calls=%async_computation.16 | async-start | bytes 2064384 | tf_op jit(solution)/shard_map/all_gather | solution.py:238
  460.7 5.3 collective-permute-start.9
  492.5 52.1 %all-gather.73.cloned.1.call-start = ((), (), s32[]{:S(2)}) async-start(), calls=%async_computation.17 | async-start | bytes 2064384 | tf_op jit(solution)/shard_map/all_gather | solution.py:238
  493.5 5.3 collective-permute-start.10
  525.5 51.9 %all-gather.75.cloned.1.call-start = ((), (), s32[]{:S(2)}) async-start(), calls=%async_computation.18 | async-start | bytes 2064384 | tf_op jit(solution)/shard_map/all_gather | solution.py:238
  526.5 5.3 collective-permute-start.11
  558.3 52.5 %all-gather.77.cloned.1.call-start = ((), (), s32[]{:S(2)}) async-start(), calls=%async_computation.19 | async-start | bytes 2064384 | tf_op jit(solution)/shard_map/all_gather | solution.py:238
  559.3 5.3 collective-permute-start.12
  591.7 51.9 %all-gather.79.cloned.1.call-start = ((), (), s32[]{:S(2)}) async-start(), calls=%async_computation.20 | async-start | bytes 2064384 | tf_op jit(solution)/shard_map/all_gather | solution.py:238
  592.7 5.3 collective-permute-start.13
  624.5 52.1 %all-gather.81.cloned.1.call-start = ((), (), s32[]{:S(2)}) async-start(), calls=%async_computation.21 | async-start | bytes 2064384 | tf_op jit(solution)/shard_map/all_gather | solution.py:238
  625.5 5.3 collective-permute-start.14
  657.5 51.9 %all-gather.83.cloned.1.call-start = ((), (), s32[]{:S(2)}) async-start(), calls=%async_computation.22 | async-start | bytes 2064384 | tf_op jit(solution)/shard_map/all_gather | solution.py:238
  658.5 5.3 collective-permute-start.15
  682.0 61.1 %all-gather.85.cloned.1.call-start = ((), (), s32[]{:S(2)}) async-start(), calls=%async_computation.23 | async-start | bytes 2064384 | tf_op jit(solution)/shard_map/all_gather | solution.py:238
  683.0 13.5 %collective-permute-start.16 = (f32[2,32,256]{2,1,0:T(8,128)S(1)}, f32[2,32,256]{2,1,0:T(8,128)S(1)}, u32[]{:S(2)}, u32[]{:S(2)}) collective-permute-start(f32[2,32,256]{2,1,0:T(8,128)S(1)} %slice.168), channel_id=1, source_target_pairs={{0,32},{32,64},{64,96},{128,160},{160,192},{192,224},{256,288},{28... | collective-permute-start | bytes 196616 | tf_op jit(solution)/shard_map/ppermute | solution.py:240
  722.6 53.3 %all-gather.87.cloned.1.call-start = ((), (), s32[]{:S(2)}) async-start(), calls=%async_computation.24 | async-start | bytes 2064384 | tf_op jit(solution)/shard_map/all_gather | solution.py:238
  723.7 6.7 collective-permute-start.17
  748.5 60.7 %all-gather.89.cloned.1.call-start = ((), (), s32[]{:S(2)}) async-start(), calls=%async_computation.25 | async-start | bytes 2064384 | tf_op jit(solution)/shard_map/all_gather | solution.py:238
  749.6 5.3 collective-permute-start.18
  778.8 7.4 copy-start.89
  781.8 60.0 %all-gather.91.cloned.1.call-start = ((), (), s32[]{:S(2)}) async-start(), calls=%async_computation.26 | async-start | bytes 2064384 | tf_op jit(solution)/shard_map/all_gather | solution.py:238
  782.9 5.3 collective-permute-start.19
  815.8 5.3 collective-permute-start.20
  848.3 26.5 %copy-start.1 = (f32[1,768,256]{2,1,0:T(8,128)S(1)}, f32[1,768,256]{2,1,0:T(8,128)}, u32[]{:S(2)}) copy-start(f32[1,768,256]{2,1,0:T(8,128)} %param.8) | copy-start | bytes 2359300
  (90 other events, 112.0 us)
Sparse Core Ops, SparseCore 0:
  9.4 105.3 all-gather.46
  118.9 21.6 all-gather.48
  166.2 18.4 all-gather.50
  199.5 18.1 all-gather.52
  231.5 17.4 all-gather.54
  263.0 17.4 all-gather.56
  294.2 18.9 all-gather.58
  327.6 18.9 all-gather.60
  360.5 18.9 all-gather.62
  393.4 18.9 all-gather.64
  426.3 18.9 all-gather.66
  459.8 18.9 all-gather.68
  492.7 18.9 all-gather.70
  525.6 18.9 all-gather.72
  558.4 18.9 all-gather.74
  591.8 18.9 all-gather.76
  624.6 18.9 all-gather.78
  657.6 18.9 all-gather.80
  682.1 27.2 all-gather.82
  722.8 20.3 all-gather.84
  748.7 27.2 all-gather.86
  782.0 27.2 all-gather.88
  814.9 26.9 all-gather.90

commit v3 on v2

--- a/solution.py
+++ b/solution.py
@@ -12,38 +12,51 @@
 BF16 = jnp.bfloat16
 
 ROWS = 16
-GROUP = 4
-HALF = 384
-PAY = 288 + HALF
+GROUP = 8
+PAY = 288
 LAG = 2
 
 
-def section_kernel(info, e_in, halo, msg, here, taps_in, e_out, pay, taps_out, mid, w_hi, w_lo):
-    active, first, core, keep, keep_row, slot = (info[k] for k in range(6))
+def section_kernel(
+    count, ids, e_in, halo, msg, table, w_all, taps_in,
+    count_out, e_out, pay, taps_out,
+    mid, w_f32, w_hi, w_lo, coef, w_sem, c_sem, t_sem,
+):
+    turn = count[0]
+    field, z_lo, core, half_here, keep_row = (ids[k] for k in range(5))
+    section = turn - LAG * field
+    active = jnp.logical_and(section >= 0, section < 16)
+    at = jnp.clip(section, 0, 15)
+    keep = jnp.logical_and(active, jnp.logical_and(at // 4 == z_lo, half_here == core))
+    slot = lax.rem(at, 4)
+    count_out[0] = turn + 1
     lane = lax.broadcasted_iota(jnp.int32, (32, 128), 1)
     other = 1 - core
-    coefs = [here[HALF + 16 * k : HALF + 16 * k + 16, :] for k in range(6)]
-    coefs = [jnp.concatenate([v[:, 0:128], v[:, 128:256]], axis=0) for v in coefs]
-    pay[288:, :] = here[0:HALF, :]
-
-    @pl.when(active == 0)
+
+    @pl.when(jnp.logical_not(active))
     def _():
         e_out[...] = e_in[...]
         pay[0:128, :] = e_in[ROWS - 1].reshape(128, 256)
         pay[128:256, :] = e_in[ROWS - 2].reshape(128, 256)
         pay[256:288, :] = jnp.zeros((32, 256), F32)
 
-    @pl.when(active == 1)
+    @pl.when(active)
     def _():
-        for k in range(2):
-            w = halo[k, 288 : 288 + HALF, :]
-            hi = w.astype(BF16)
-            w_hi[k * HALF : (k + 1) * HALF, :] = hi
-            w_lo[k * HALF : (k + 1) * HALF, :] = (w - hi.astype(F32)).astype(BF16)
+        w_copy = pltpu.make_async_copy(w_all.at[at], w_f32, w_sem)
+        c_copy = pltpu.make_async_copy(table.at[at], coef, c_sem)
+        w_copy.start()
+        c_copy.start()
+        w_copy.wait()
+        c_copy.wait()
+        w = w_f32[...]
+        hi = w.astype(BF16)
+        w_hi[...] = hi
+        w_lo[...] = (w - hi.astype(F32)).astype(BF16)
+        coefs = [coef[k] for k in range(6)]
 
         theirs = pltpu.roll(msg[other, :, 0:128], 1, 1)
         received = jnp.where(lane == ROWS, theirs, msg[core, :, 0:128])
-        n = jnp.where(first == 1, coefs[0], received)
+        n = jnp.where(field == 0, coefs[0], received)
         gain_n = coefs[1] * n
 
         def products(x):
@@ -130,9 +143,11 @@
         rows_step(lambda *_: near[None], e_in[ROWS - 1], far, mid, ROWS, 1, None)
         last_n = lax.fori_loop(0, ROWS // GROUP, two, jnp.zeros((32, 128), F32))
 
-        @pl.when(keep == 1)
+        @pl.when(keep)
         def _():
-            taps_out[slot] = e_out[pl.ds(keep_row, 2)]
+            t_copy = pltpu.make_async_copy(e_out.at[pl.ds(keep_row, 2)], taps_out.at[slot], t_sem)
+            t_copy.start()
+            t_copy.wait()
 
         pay[0:128, :] = e_out[ROWS - 1].reshape(128, 256)
         pay[128:256, :] = e_out[ROWS - 2].reshape(128, 256)
@@ -140,26 +155,37 @@
         pay[256:288, 128:256] = last_n
 
 
-def section_call(info, e, halo, msg, here, taps):
+def section_call(count, ids, e, halo, msg, table, w_all, taps):
     vmem = pl.BlockSpec(memory_space=pltpu.VMEM)
+    smem = pl.BlockSpec(memory_space=pltpu.SMEM)
+    hbm = pl.BlockSpec(memory_space=pl.ANY)
     return pl.pallas_call(
         section_kernel,
         out_shape=(
+            jax.ShapeDtypeStruct((1,), jnp.int32),
             jax.ShapeDtypeStruct((ROWS, 4, 32, 256), F32),
             jax.ShapeDtypeStruct((PAY, 256), F32),
             jax.ShapeDtypeStruct(taps.shape, F32),
         ),
-        in_specs=[pl.BlockSpec(memory_space=pltpu.SMEM)] + [vmem] * 5,
-        out_specs=(vmem, vmem, vmem),
+        in_specs=[smem, smem, vmem, vmem, vmem, hbm, hbm, hbm],
+        out_specs=(smem, vmem, vmem, hbm),
         scratch_shapes=[
             pltpu.VMEM((ROWS + 1, 4, 32, 256), F32),
+            pltpu.VMEM((768, 256), F32),
             pltpu.VMEM((768, 256), BF16),
             pltpu.VMEM((768, 256), BF16),
+            pltpu.VMEM((6, 32, 128), F32),
+            pltpu.SemaphoreType.DMA,
+            pltpu.SemaphoreType.DMA,
+            pltpu.SemaphoreType.DMA,
         ],
-        input_output_aliases={5: 2},
-        compiler_params=pltpu.CompilerParams(vmem_limit_bytes=40 * 1024 * 1024),
+        input_output_aliases={7: 3},
+        compiler_params=pltpu.CompilerParams(vmem_limit_bytes=32 * 1024 * 1024),
+        cost_estimate=pl.CostEstimate(
+            flops=33 * 3 * 2 * 128 * 768 * 256, bytes_accessed=8 << 20, transcendentals=0
+        ),
         name="section",
-    )(info, e, halo, msg, here, taps)
+    )(count, ids, e, halo, msg, table, w_all, taps)
 
 
 def local(input_fields, injection_order, dispersion, coupling, amplifier_gain, inversion):
@@ -172,8 +198,7 @@
     across = [(17 * h + 2 * k, 16 * (1 - h) + 2 * k + h) for h in range(2) for k in range(8)]
     ahead = [(g, g + 1) for g in range(16) if g % 4 < 3]
 
-    half = lax.dynamic_slice_in_dim(dispersion[0], HALF * core, HALF, 0)
-    w_all = lax.all_gather(half, "segment")
+    w_all = lax.all_gather(dispersion[0], "segment")
 
     own = jnp.concatenate([inversion[0], amplifier_gain[0], coupling[0, :, 0]], axis=0)
     own = jnp.pad(own.reshape(1, 192), ((0, 0), (0, 64)))
@@ -204,40 +229,26 @@
     right = jnp.where(at_col == 31, 0.0, right)
     table = jnp.stack([n0, gain, before, after, left, right], axis=1)
     table = jnp.pad(table, ((0, 0), (0, 0), (0, 0), (0, 128 - ROWS - 1)))
-    table = jnp.concatenate([table[:, :, :16], table[:, :, 16:]], axis=3).reshape(16, 96, 256)
-
-    turns = 16 + 3 * LAG
-
-    def section_at(turn):
-        return jnp.clip(turn - LAG * x, 0, 15)
-
-    def here_at(turn):
-        w = lax.dynamic_index_in_dim(w_all, section_at(turn + 1), 0, keepdims=False)
-        coef = lax.dynamic_index_in_dim(table, section_at(turn), 0, keepdims=False)
-        return jnp.concatenate([w, coef], axis=0)
-
-    first_pay = jnp.concatenate(
-        [e[ROWS - 1].reshape(128, 256), e[ROWS - 2].reshape(128, 256), jnp.zeros((32, 256), F32), w_all[0]],
-        axis=0,
+
+    pay = jnp.concatenate(
+        [e[ROWS - 1].reshape(128, 256), e[ROWS - 2].reshape(128, 256), jnp.zeros((32, 256), F32)], axis=0
     )
-    halo = lax.all_gather(first_pay, "row", axis_index_groups=chips)
+    halo = lax.all_gather(pay, "row", axis_index_groups=chips)
     taps = jnp.zeros((4, 2, 4, 32, 256), F32)
     keep_row = jnp.where(core == 0, 2 * y, 14 - 2 * y)
-    msgs = {}
-    for turn in range(turns):
-        section = turn - LAG * x
-        active = jnp.logical_and(section >= 0, section < 16)
-        at = section_at(turn)
-        keep = active & (at // 4 == z_lo) & (core == z_hi)
-        info = jnp.stack([active, x == 0, core, keep, keep_row, at % 4]).astype(jnp.int32)
-        msg = msgs.pop(turn - LAG, None)
-        if msg is None:
-            msg = jnp.zeros((2, 32, 256), F32)
-        e, pay, taps = section_call(info, e, halo, msg, here_at(turn), taps)
-        if turn + 1 < turns:
+    ids = jnp.stack([x, z_lo, core, z_hi, keep_row]).astype(jnp.int32)
+
+    def two_turns(_, carry):
+        count, e, halo, msg, taps = carry
+        for _ in range(2):
+            coming = lax.ppermute(halo[:, 256:], "segment", ahead)
+            count, e, pay, taps = section_call(count, ids, e, halo, msg, table, w_all, taps)
             halo = lax.all_gather(pay, "row", axis_index_groups=chips)
-        if turn + LAG < turns:
-            msgs[turn] = lax.ppermute(halo[:, 256:288], "segment", ahead)
+            msg = coming
+        return count, e, halo, msg, taps
+
+    start = (jnp.zeros((1,), jnp.int32), e, halo, jnp.zeros((2, 32, 256), F32), taps)
+    taps = lax.fori_loop(0, (16 + 3 * LAG) // 2, two_turns, start)[4]
 
     taps = jnp.where(z_hi == 0, taps, jnp.flip(taps, 1)).swapaxes(0, 1)
     both = lax.all_to_all(taps, "row", 0, 0, axis_index_groups=chips)

time: 894 us -> 583 us (0.65)
  the two profiles are of different devices: /device:TPU:8 before, /device:TPU:64 now
where the time goes in v3:
time: 583 us; the launch traced here: 580 us
  Pallas kernels  183 us (31%)
  starting transfers between devices  170 us (29%)
  waiting for transfers between devices  97.5 us (17%)
  blocking collectives  75.2 us (13%)
  local copies, waits for them, and re-layouts  22.7 us (4%)
  between operations  15.6 us (3%)
  loops' own time  8.14 us (1%)
  other arithmetic  7.83 us (1%)
    pallas_call x22, Pallas kernels, section_call(): pl.pallas_call(section_kernel, out_shape=(jax.ShapeDtypeStruct((1,), jnp....  183 us
    ppermute x22, starting transfers between devices, two_turns(): coming = lax.ppermute(halo[:, 256:], 'segment', ahead)  145 us
    all_to_all x1, waiting for transfers between devices, local(): lax.all_to_all(jnp.broadcast_to(pair[None], (8, 2, 144, 256)), 'row', 0,...  56.5 us
    all_gather x22, blocking collectives, two_turns(): halo = lax.all_gather(pay, 'row', axis_index_groups=chips)  49 us
    all_gather x1, waiting for transfers between devices, local(): w_all = lax.all_gather(dispersion[0], 'segment')  24 us
    all_to_all x1, blocking collectives, local(): out = lax.all_to_all(mine, 'segment', 0, 0, axis_index_groups=rings)  15.4 us
    ppermute x1, waiting for transfers between devices, local(): pair = jnp.where(core == z_hi, pair, lax.ppermute(pair, 'row', across))  13.2 us
  transfers between devices with their start and end apart: 26, of which 4 were waited for; matrix products, arithmetic and copies ran while one was open for 4% of the time, Pallas kernels for 32%

profile of v3, /device:TPU:64, one launch (start us, length us, event | category | flops | bytes accessed | tf_op | source)
XLA Modules:
  0.0 580.0 jit_solution(16508499199160784196)
XLA Ops:
  8.7 9.4 %all-to-all-start = ((f32[16,1,256]{2,1,0:T(1,128)}), f32[16,1,256]{2,1,0:T(1,128)S(1)}, u32[]{:S(2)}, u32[]{:S(2)}) async-start(f32[16,1,256]{2,1,0:T(1,128)} %broadcast_in_dim.57), calls=%async_computation | async-start | bytes 32768 | tf_op jit(solution)/shard_map/all_to_all | solution.py:205
  21.5 3.1 all-to-all-done
  26.6 8.2 %collective-permute-start.2 = (f32[2,144,256]{2,1,0:T(8,128)S(1)}, f32[2,144,256]{2,1,0:T(8,128)S(1)}, u32[]{:S(2)}, u32[]{:S(2)}) collective-permute-start(f32[2,144,256]{2,1,0:T(8,128)S(1)} %bitcast.49), channel_id=1, source_target_pairs={{0,16},{2,18},{4,20},{6,22},{8,24},{10,26},{12,28},{14,30},{17,1},... | collective-permute-start | bytes 884744 | tf_op jit(solution)/shard_map/ppermute | solution.py:212
  34.9 13.2 %collective-permute-done.2 = f32[2,144,256]{2,1,0:T(8,128)S(1)} collective-permute-done((f32[2,144,256]{2,1,0:T(8,128)S(1)}, f32[2,144,256]{2,1,0:T(8,128)S(1)}, u32[]{:S(2)}, u32[]{:S(2)}) %collective-permute-start.2) | collective-permute-done | bytes 294944 | tf_op jit(solution)/shard_map/ppermute | solution.py:212
  49.8 7.1 %all-to-all-start.1 = ((f32[8,2,144,256]{3,2,1,0:T(8,128)}), f32[8,2,144,256]{3,2,1,0:T(8,128)S(1)}, u32[]{:S(2)}, u32[]{:S(2)}) async-start(f32[8,2,144,256]{3,2,1,0:T(8,128)} %broadcast_in_dim.58), calls=%async_computation.1 | async-start | bytes 4718592 | tf_op jit(solution)/shard_map/all_to_all | solution.py:213
  57.0 56.5 %all-to-all-done.1 = f32[8,2,144,256]{3,2,1,0:T(8,128)S(1)} async-done(((f32[8,2,144,256]{3,2,1,0:T(8,128)}), f32[8,2,144,256]{3,2,1,0:T(8,128)S(1)}, u32[]{:S(2)}, u32[]{:S(2)}) %all-to-all-start.1) | async-done | bytes 2359328 | tf_op jit(solution)/shard_map/all_to_all | solution.py:213
  114.9 2.7 reverse_select_fusion
  123.6 4.1 broadcast_select_fusion.1
  127.7 3.8 stack.32
  131.5 3.0 copy.28
  134.6 2.8 pad.9.clone
  137.5 2.4 all-gather.3
  139.9 24.0 %all-gather.10.cloned.1.call-done = f32[16,768,256]{2,1,0:T(8,128)} async-done(((f32[1,768,256]{2,1,0:T(8,128)}), f32[16,768,256]{2,1,0:T(8,128)}) %all-gather.10.cloned.1.call-update) | async-done | bytes 12582928 | tf_op jit(solution)/shard_map/all_gather | solution.py:201
  165.0 385.5 %while.18 = (s32[]{:T(128)}, s32[1]{0:T(128)}, f32[16,4,32,256]{3,2,1,0:T(8,128)}, f32[2,288,256]{2,1,0:T(8,128)S(1)}, f32[2,32,256]{2,1,0:T(8,128)S(1)}, /*inde...) while((s32[]{:T(128)}, s32[1]{0:T(128)}, ...), condition=%wide.region_1.2_spmd, body=%wide.region_0.1_spmd.sunk | while | flops 9965666304 | bytes 19333300 | solution.py:251
  166.3 10.1 %section.2 = (s32[1]{0:T(128)}, f32[16,4,32,256]{3,2,1,0:T(8,128)S(1)}, f32[288,256]{1,0:T(8,128)S(1)}, f32[4,2,4,32,256]{4,3,2,1,0:T(8,128)}) custom-call(s32[1]{0:T(128)} %get-tuple-element.196.count, s32[5]{0:T(128)S(1)} %get-tuple-element.211.ids, f32[16,4,32,256]{3,2,1,0:T(8,128)} %get-tuple-element.197.e_in, ...), custom_call_target="tpu_custom_call", output_to_operand_aliasing={{3}: (7, {})} | custom-call | flops 4982833152 | bytes 8388608 | tf_op jit(solution)/shard_map/while/body/eval_jaxpr/section/pallas_call | solution.py:162
  176.5 2.2 all-gather.6
  180.0 10.5 %section.3 = (s32[1]{0:T(128)}, f32[16,4,32,256]{3,2,1,0:T(8,128)}, f32[288,256]{1,0:T(8,128)S(1)}, f32[4,2,4,32,256]{4,3,2,1,0:T(8,128)}) custom-call(s32[1]{0:T(128)} %get-tuple-element.177.count, s32[5]{0:T(128)S(1)} %get-tuple-element.211.ids, f32[16,4,32,256]{3,2,1,0:T(8,128)S(1)} %get-tuple-element.178.e_in, ...), custom_call_target="tpu_custom_call", output_to_operand_aliasing={{3}: (7, {})} | custom-call | flops 4982833152 | bytes 8388608 | tf_op jit(solution)/shard_map/while/body/eval_jaxpr/section/pallas_call | solution.py:162
  190.5 2.2 all-gather.7
  193.5 82.9 %collective-permute-start = (f32[2,32,256]{2,1,0:T(8,128)S(1)}, f32[2,32,256]{2,1,0:T(8,128)S(1)}, u32[]{:S(2)}, u32[]{:S(2)}) collective-permute-start(f32[2,32,256]{2,1,0:T(8,128)S(1)} %slice.77), channel_id=1, source_target_pairs={{0,32},{32,64},{64,96},{128,160},{160,192},{192,224},{256,288},{28... | collective-permute-start | bytes 196616 | tf_op jit(solution)/shard_map/while/body/eval_jaxpr/ppermute | solution.py:244
  276.4 10.1 %section.2 = (s32[1]{0:T(128)}, f32[16,4,32,256]{3,2,1,0:T(8,128)S(1)}, f32[288,256]{1,0:T(8,128)S(1)}, f32[4,2,4,32,256]{4,3,2,1,0:T(8,128)}) custom-call(s32[1]{0:T(128)} %get-tuple-element.196.count, s32[5]{0:T(128)S(1)} %get-tuple-element.211.ids, f32[16,4,32,256]{3,2,1,0:T(8,128)} %get-tuple-element.197.e_in, ...), custom_call_target="tpu_custom_call", output_to_operand_aliasing={{3}: (7, {})} | custom-call | flops 4982833152 | bytes 8388608 | tf_op jit(solution)/shard_map/while/body/eval_jaxpr/section/pallas_call | solution.py:162
  290.7 10.5 %section.3 = (s32[1]{0:T(128)}, f32[16,4,32,256]{3,2,1,0:T(8,128)}, f32[288,256]{1,0:T(8,128)S(1)}, f32[4,2,4,32,256]{4,3,2,1,0:T(8,128)}) custom-call(s32[1]{0:T(128)} %get-tuple-element.177.count, s32[5]{0:T(128)S(1)} %get-tuple-element.211.ids, f32[16,4,32,256]{3,2,1,0:T(8,128)S(1)} %get-tuple-element.178.e_in, ...), custom_call_target="tpu_custom_call", output_to_operand_aliasing={{3}: (7, {})} | custom-call | flops 4982833152 | bytes 8388608 | tf_op jit(solution)/shard_map/while/body/eval_jaxpr/section/pallas_call | solution.py:162
  306.0 10.8 %section.2 = (s32[1]{0:T(128)}, f32[16,4,32,256]{3,2,1,0:T(8,128)S(1)}, f32[288,256]{1,0:T(8,128)S(1)}, f32[4,2,4,32,256]{4,3,2,1,0:T(8,128)}) custom-call(s32[1]{0:T(128)} %get-tuple-element.196.count, s32[5]{0:T(128)S(1)} %get-tuple-element.211.ids, f32[16,4,32,256]{3,2,1,0:T(8,128)} %get-tuple-element.197.e_in, ...), custom_call_target="tpu_custom_call", output_to_operand_aliasing={{3}: (7, {})} | custom-call | flops 4982833152 | bytes 8388608 | tf_op jit(solution)/shard_map/while/body/eval_jaxpr/section/pallas_call | solution.py:162
  320.4 11.2 %section.3 = (s32[1]{0:T(128)}, f32[16,4,32,256]{3,2,1,0:T(8,128)}, f32[288,256]{1,0:T(8,128)S(1)}, f32[4,2,4,32,256]{4,3,2,1,0:T(8,128)}) custom-call(s32[1]{0:T(128)} %get-tuple-element.177.count, s32[5]{0:T(128)S(1)} %get-tuple-element.211.ids, f32[16,4,32,256]{3,2,1,0:T(8,128)S(1)} %get-tuple-element.178.e_in, ...), custom_call_target="tpu_custom_call", output_to_operand_aliasing={{3}: (7, {})} | custom-call | flops 4982833152 | bytes 8388608 | tf_op jit(solution)/shard_map/while/body/eval_jaxpr/section/pallas_call | solution.py:162
  335.9 10.8 %section.2 = (s32[1]{0:T(128)}, f32[16,4,32,256]{3,2,1,0:T(8,128)S(1)}, f32[288,256]{1,0:T(8,128)S(1)}, f32[4,2,4,32,256]{4,3,2,1,0:T(8,128)}) custom-call(s32[1]{0:T(128)} %get-tuple-element.196.count, s32[5]{0:T(128)S(1)} %get-tuple-element.211.ids, f32[16,4,32,256]{3,2,1,0:T(8,128)} %get-tuple-element.197.e_in, ...), custom_call_target="tpu_custom_call", output_to_operand_aliasing={{3}: (7, {})} | custom-call | flops 4982833152 | bytes 8388608 | tf_op jit(solution)/shard_map/while/body/eval_jaxpr/section/pallas_call | solution.py:162
  346.6 2.2 all-gather.6
  350.7 11.2 %section.3 = (s32[1]{0:T(128)}, f32[16,4,32,256]{3,2,1,0:T(8,128)}, f32[288,256]{1,0:T(8,128)S(1)}, f32[4,2,4,32,256]{4,3,2,1,0:T(8,128)}) custom-call(s32[1]{0:T(128)} %get-tuple-element.177.count, s32[5]{0:T(128)S(1)} %get-tuple-element.211.ids, f32[16,4,32,256]{3,2,1,0:T(8,128)S(1)} %get-tuple-element.178.e_in, ...), custom_call_target="tpu_custom_call", output_to_operand_aliasing={{3}: (7, {})} | custom-call | flops 4982833152 | bytes 8388608 | tf_op jit(solution)/shard_map/while/body/eval_jaxpr/section/pallas_call | solution.py:162
  366.8 10.1 %section.2 = (s32[1]{0:T(128)}, f32[16,4,32,256]{3,2,1,0:T(8,128)S(1)}, f32[288,256]{1,0:T(8,128)S(1)}, f32[4,2,4,32,256]{4,3,2,1,0:T(8,128)}) custom-call(s32[1]{0:T(128)} %get-tuple-element.196.count, s32[5]{0:T(128)S(1)} %get-tuple-element.211.ids, f32[16,4,32,256]{3,2,1,0:T(8,128)} %get-tuple-element.197.e_in, ...), custom_call_target="tpu_custom_call", output_to_operand_aliasing={{3}: (7, {})} | custom-call | flops 4982833152 | bytes 8388608 | tf_op jit(solution)/shard_map/while/body/eval_jaxpr/section/pallas_call | solution.py:162
  379.1 2.6 collective-permute-start.1
  381.7 10.5 %section.3 = (s32[1]{0:T(128)}, f32[16,4,32,256]{3,2,1,0:T(8,128)}, f32[288,256]{1,0:T(8,128)S(1)}, f32[4,2,4,32,256]{4,3,2,1,0:T(8,128)}) custom-call(s32[1]{0:T(128)} %get-tuple-element.177.count, s32[5]{0:T(128)S(1)} %get-tuple-element.211.ids, f32[16,4,32,256]{3,2,1,0:T(8,128)S(1)} %get-tuple-element.178.e_in, ...), custom_call_target="tpu_custom_call", output_to_operand_aliasing={{3}: (7, {})} | custom-call | flops 4982833152 | bytes 8388608 | tf_op jit(solution)/shard_map/while/body/eval_jaxpr/section/pallas_call | solution.py:162
  395.2 2.6 collective-permute-start
  397.8 10.1 %section.2 = (s32[1]{0:T(128)}, f32[16,4,32,256]{3,2,1,0:T(8,128)S(1)}, f32[288,256]{1,0:T(8,128)S(1)}, f32[4,2,4,32,256]{4,3,2,1,0:T(8,128)}) custom-call(s32[1]{0:T(128)} %get-tuple-element.196.count, s32[5]{0:T(128)S(1)} %get-tuple-element.211.ids, f32[16,4,32,256]{3,2,1,0:T(8,128)} %get-tuple-element.197.e_in, ...), custom_call_target="tpu_custom_call", output_to_operand_aliasing={{3}: (7, {})} | custom-call | flops 4982833152 | bytes 8388608 | tf_op jit(solution)/shard_map/while/body/eval_jaxpr/section/pallas_call | solution.py:162
  412.1 10.5 %section.3 = (s32[1]{0:T(128)}, f32[16,4,32,256]{3,2,1,0:T(8,128)}, f32[288,256]{1,0:T(8,128)S(1)}, f32[4,2,4,32,256]{4,3,2,1,0:T(8,128)}) custom-call(s32[1]{0:T(128)} %get-tuple-element.177.count, s32[5]{0:T(128)S(1)} %get-tuple-element.211.ids, f32[16,4,32,256]{3,2,1,0:T(8,128)S(1)} %get-tuple-element.178.e_in, ...), custom_call_target="tpu_custom_call", output_to_operand_aliasing={{3}: (7, {})} | custom-call | flops 4982833152 | bytes 8388608 | tf_op jit(solution)/shard_map/while/body/eval_jaxpr/section/pallas_call | solution.py:162
  427.5 10.1 %section.2 = (s32[1]{0:T(128)}, f32[16,4,32,256]{3,2,1,0:T(8,128)S(1)}, f32[288,256]{1,0:T(8,128)S(1)}, f32[4,2,4,32,256]{4,3,2,1,0:T(8,128)}) custom-call(s32[1]{0:T(128)} %get-tuple-element.196.count, s32[5]{0:T(128)S(1)} %get-tuple-element.211.ids, f32[16,4,32,256]{3,2,1,0:T(8,128)} %get-tuple-element.197.e_in, ...), custom_call_target="tpu_custom_call", output_to_operand_aliasing={{3}: (7, {})} | custom-call | flops 4982833152 | bytes 8388608 | tf_op jit(solution)/shard_map/while/body/eval_jaxpr/section/pallas_call | solution.py:162
  441.7 10.5 %section.3 = (s32[1]{0:T(128)}, f32[16,4,32,256]{3,2,1,0:T(8,128)}, f32[288,256]{1,0:T(8,128)S(1)}, f32[4,2,4,32,256]{4,3,2,1,0:T(8,128)}) custom-call(s32[1]{0:T(128)} %get-tuple-element.177.count, s32[5]{0:T(128)S(1)} %get-tuple-element.211.ids, f32[16,4,32,256]{3,2,1,0:T(8,128)S(1)} %get-tuple-element.178.e_in, ...), custom_call_target="tpu_custom_call", output_to_operand_aliasing={{3}: (7, {})} | custom-call | flops 4982833152 | bytes 8388608 | tf_op jit(solution)/shard_map/while/body/eval_jaxpr/section/pallas_call | solution.py:162
  457.1 10.1 %section.2 = (s32[1]{0:T(128)}, f32[16,4,32,256]{3,2,1,0:T(8,128)S(1)}, f32[288,256]{1,0:T(8,128)S(1)}, f32[4,2,4,32,256]{4,3,2,1,0:T(8,128)}) custom-call(s32[1]{0:T(128)} %get-tuple-element.196.count, s32[5]{0:T(128)S(1)} %get-tuple-element.211.ids, f32[16,4,32,256]{3,2,1,0:T(8,128)} %get-tuple-element.197.e_in, ...), custom_call_target="tpu_custom_call", output_to_operand_aliasing={{3}: (7, {})} | custom-call | flops 4982833152 | bytes 8388608 | tf_op jit(solution)/shard_map/while/body/eval_jaxpr/section/pallas_call | solution.py:162
  471.4 10.5 %section.3 = (s32[1]{0:T(128)}, f32[16,4,32,256]{3,2,1,0:T(8,128)}, f32[288,256]{1,0:T(8,128)S(1)}, f32[4,2,4,32,256]{4,3,2,1,0:T(8,128)}) custom-call(s32[1]{0:T(128)} %get-tuple-element.177.count, s32[5]{0:T(128)S(1)} %get-tuple-element.211.ids, f32[16,4,32,256]{3,2,1,0:T(8,128)S(1)} %get-tuple-element.178.e_in, ...), custom_call_target="tpu_custom_call", output_to_operand_aliasing={{3}: (7, {})} | custom-call | flops 4982833152 | bytes 8388608 | tf_op jit(solution)/shard_map/while/body/eval_jaxpr/section/pallas_call | solution.py:162
  486.8 2.3 section.2
  491.3 9.7 %collective-permute-start.1 = (f32[2,32,256]{2,1,0:T(8,128)S(1)}, f32[2,32,256]{2,1,0:T(8,128)S(1)}, u32[]{:S(2)}, u32[]{:S(2)}) collective-permute-start(f32[2,32,256]{2,1,0:T(8,128)S(1)} %slice.78), channel_id=1, source_target_pairs={{0,32},{32,64},{64,96},{128,160},{160,192},{192,224},{256,288},{28... | collective-permute-start | bytes 196616 | tf_op jit(solution)/shard_map/while/body/eval_jaxpr/ppermute | solution.py:244
  501.1 2.7 section.3
  506.7 9.7 %collective-permute-start = (f32[2,32,256]{2,1,0:T(8,128)S(1)}, f32[2,32,256]{2,1,0:T(8,128)S(1)}, u32[]{:S(2)}, u32[]{:S(2)}) collective-permute-start(f32[2,32,256]{2,1,0:T(8,128)S(1)} %slice.77), channel_id=1, source_target_pairs={{0,32},{32,64},{64,96},{128,160},{160,192},{192,224},{256,288},{28... | collective-permute-start | bytes 196616 | tf_op jit(solution)/shard_map/while/body/eval_jaxpr/ppermute | solution.py:244
  516.4 2.3 section.2
  518.8 2.2 all-gather.6
  522.9 2.7 section.3
  530.7 2.3 section.2
  535.2 9.7 %collective-permute-start.1 = (f32[2,32,256]{2,1,0:T(8,128)S(1)}, f32[2,32,256]{2,1,0:T(8,128)S(1)}, u32[]{:S(2)}, u32[]{:S(2)}) collective-permute-start(f32[2,32,256]{2,1,0:T(8,128)S(1)} %slice.78), channel_id=1, source_target_pairs={{0,32},{32,64},{64,96},{128,160},{160,192},{192,224},{256,288},{28... | collective-permute-start | bytes 196616 | tf_op jit(solution)/shard_map/while/body/eval_jaxpr/ppermute | solution.py:244
  544.9 2.7 section.3
  552.0 4.6 all_to_all.20
  556.7 15.4 %all_to_all.21 = f32[4,4,32,256]{3,2,1,0:T(8,128)S(1)} all-to-all(f32[4,4,32,256]{3,2,1,0:T(8,128)S(1)} %dynamic-slice_bitcast_fusion), channel_id=1, replica_groups={{0,32,64,96},{128,160,192,224},{256,288,320,352},{384,416,448,480},{1,3..., dimensions={0} | all-to-all | bytes 1048576 | tf_op jit(solution)/shard_map/all_to_all | solution.py:256
  (117 shorter events, 86.9 us)
Async XLA Ops:
  6.5 14.9 %copy-start = (f32[4,1,32,4,256]{4,3,2,1,0:T(4,128)S(1)}, f32[4,1,32,4,256]{4,3,2,1,0:T(4,128)}, u32[]{:S(2)}) copy-start(f32[4,1,32,4,256]{4,3,2,1,0:T(4,128)} %param.8) | copy-start | bytes 1572868
  6.5 157.4 %all-gather.10.cloned.1.call-start = ((), (), s32[]{:S(2)}) async-start(), calls=%async_computation.4 | async-start | bytes 13369344 | tf_op jit(solution)/shard_map/all_gather | solution.py:201
  8.7 15.9 %all-to-all-start = ((f32[16,1,256]{2,1,0:T(1,128)}), f32[16,1,256]{2,1,0:T(1,128)S(1)}, u32[]{:S(2)}, u32[]{:S(2)}) async-start(f32[16,1,256]{2,1,0:T(1,128)} %broadcast_in_dim.57), calls=%async_computation | async-start | bytes 32768 | tf_op jit(solution)/shard_map/all_to_all | solution.py:205
  26.6 21.5 %collective-permute-start.2 = (f32[2,144,256]{2,1,0:T(8,128)S(1)}, f32[2,144,256]{2,1,0:T(8,128)S(1)}, u32[]{:S(2)}, u32[]{:S(2)}) collective-permute-start(f32[2,144,256]{2,1,0:T(8,128)S(1)} %bitcast.49), channel_id=1, source_target_pairs={{0,16},{2,18},{4,20},{6,22},{8,24},{10,26},{12,28},{14,30},{17,1},... | collective-permute-start | bytes 884744 | tf_op jit(solution)/shard_map/ppermute | solution.py:212
  49.8 63.7 %all-to-all-start.1 = ((f32[8,2,144,256]{3,2,1,0:T(8,128)}), f32[8,2,144,256]{3,2,1,0:T(8,128)S(1)}, u32[]{:S(2)}, u32[]{:S(2)}) async-start(f32[8,2,144,256]{3,2,1,0:T(8,128)} %broadcast_in_dim.58), calls=%async_computation.1 | async-start | bytes 4718592 | tf_op jit(solution)/shard_map/all_to_all | solution.py:213
  113.5 1.4 copy-start.1
  165.0 14.9 %collective-permute-start = (f32[2,32,256]{2,1,0:T(8,128)S(1)}, f32[2,32,256]{2,1,0:T(8,128)S(1)}, u32[]{:S(2)}, u32[]{:S(2)}) collective-permute-start(f32[2,32,256]{2,1,0:T(8,128)S(1)} %slice.77), channel_id=1, source_target_pairs={{0,32},{32,64},{64,96},{128,160},{160,192},{192,224},{256,288},{28... | collective-permute-start | bytes 196616 | tf_op jit(solution)/shard_map/while/body/eval_jaxpr/ppermute | solution.py:244
  178.7 14.1 %collective-permute-start.1 = (f32[2,32,256]{2,1,0:T(8,128)S(1)}, f32[2,32,256]{2,1,0:T(8,128)S(1)}, u32[]{:S(2)}, u32[]{:S(2)}) collective-permute-start(f32[2,32,256]{2,1,0:T(8,128)S(1)} %slice.78), channel_id=1, source_target_pairs={{0,32},{32,64},{64,96},{128,160},{160,192},{192,224},{256,288},{28... | collective-permute-start | bytes 196616 | tf_op jit(solution)/shard_map/while/body/eval_jaxpr/ppermute | solution.py:244
  193.5 97.2 %collective-permute-start = (f32[2,32,256]{2,1,0:T(8,128)S(1)}, f32[2,32,256]{2,1,0:T(8,128)S(1)}, u32[]{:S(2)}, u32[]{:S(2)}) collective-permute-start(f32[2,32,256]{2,1,0:T(8,128)S(1)} %slice.77), channel_id=1, source_target_pairs={{0,32},{32,64},{64,96},{128,160},{160,192},{192,224},{256,288},{28... | collective-permute-start | bytes 196616 | tf_op jit(solution)/shard_map/while/body/eval_jaxpr/ppermute | solution.py:244
  288.7 14.7 %collective-permute-start.1 = (f32[2,32,256]{2,1,0:T(8,128)S(1)}, f32[2,32,256]{2,1,0:T(8,128)S(1)}, u32[]{:S(2)}, u32[]{:S(2)}) collective-permute-start(f32[2,32,256]{2,1,0:T(8,128)S(1)} %slice.78), channel_id=1, source_target_pairs={{0,32},{32,64},{64,96},{128,160},{160,192},{192,224},{256,288},{28... | collective-permute-start | bytes 196616 | tf_op jit(solution)/shard_map/while/body/eval_jaxpr/ppermute | solution.py:244
  304.1 16.3 %collective-permute-start = (f32[2,32,256]{2,1,0:T(8,128)S(1)}, f32[2,32,256]{2,1,0:T(8,128)S(1)}, u32[]{:S(2)}, u32[]{:S(2)}) collective-permute-start(f32[2,32,256]{2,1,0:T(8,128)S(1)} %slice.77), channel_id=1, source_target_pairs={{0,32},{32,64},{64,96},{128,160},{160,192},{192,224},{256,288},{28... | collective-permute-start | bytes 196616 | tf_op jit(solution)/shard_map/while/body/eval_jaxpr/ppermute | solution.py:244
  319.1 14.8 %collective-permute-start.1 = (f32[2,32,256]{2,1,0:T(8,128)S(1)}, f32[2,32,256]{2,1,0:T(8,128)S(1)}, u32[]{:S(2)}, u32[]{:S(2)}) collective-permute-start(f32[2,32,256]{2,1,0:T(8,128)S(1)} %slice.78), channel_id=1, source_target_pairs={{0,32},{32,64},{64,96},{128,160},{160,192},{192,224},{256,288},{28... | collective-permute-start | bytes 196616 | tf_op jit(solution)/shard_map/while/body/eval_jaxpr/ppermute | solution.py:244
  334.6 16.1 %collective-permute-start = (f32[2,32,256]{2,1,0:T(8,128)S(1)}, f32[2,32,256]{2,1,0:T(8,128)S(1)}, u32[]{:S(2)}, u32[]{:S(2)}) collective-permute-start(f32[2,32,256]{2,1,0:T(8,128)S(1)} %slice.77), channel_id=1, source_target_pairs={{0,32},{32,64},{64,96},{128,160},{160,192},{192,224},{256,288},{28... | collective-permute-start | bytes 196616 | tf_op jit(solution)/shard_map/while/body/eval_jaxpr/ppermute | solution.py:244
  348.9 15.3 %collective-permute-start.1 = (f32[2,32,256]{2,1,0:T(8,128)S(1)}, f32[2,32,256]{2,1,0:T(8,128)S(1)}, u32[]{:S(2)}, u32[]{:S(2)}) collective-permute-start(f32[2,32,256]{2,1,0:T(8,128)S(1)} %slice.78), channel_id=1, source_target_pairs={{0,32},{32,64},{64,96},{128,160},{160,192},{192,224},{256,288},{28... | collective-permute-start | bytes 196616 | tf_op jit(solution)/shard_map/while/body/eval_jaxpr/ppermute | solution.py:244
  364.8 16.9 %collective-permute-start = (f32[2,32,256]{2,1,0:T(8,128)S(1)}, f32[2,32,256]{2,1,0:T(8,128)S(1)}, u32[]{:S(2)}, u32[]{:S(2)}) collective-permute-start(f32[2,32,256]{2,1,0:T(8,128)S(1)} %slice.77), channel_id=1, source_target_pairs={{0,32},{32,64},{64,96},{128,160},{160,192},{192,224},{256,288},{28... | collective-permute-start | bytes 196616 | tf_op jit(solution)/shard_map/while/body/eval_jaxpr/ppermute | solution.py:244
  379.1 15.4 %collective-permute-start.1 = (f32[2,32,256]{2,1,0:T(8,128)S(1)}, f32[2,32,256]{2,1,0:T(8,128)S(1)}, u32[]{:S(2)}, u32[]{:S(2)}) collective-permute-start(f32[2,32,256]{2,1,0:T(8,128)S(1)} %slice.78), channel_id=1, source_target_pairs={{0,32},{32,64},{64,96},{128,160},{160,192},{192,224},{256,288},{28... | collective-permute-start | bytes 196616 | tf_op jit(solution)/shard_map/while/body/eval_jaxpr/ppermute | solution.py:244
  395.2 16.9 %collective-permute-start = (f32[2,32,256]{2,1,0:T(8,128)S(1)}, f32[2,32,256]{2,1,0:T(8,128)S(1)}, u32[]{:S(2)}, u32[]{:S(2)}) collective-permute-start(f32[2,32,256]{2,1,0:T(8,128)S(1)} %slice.77), channel_id=1, source_target_pairs={{0,32},{32,64},{64,96},{128,160},{160,192},{192,224},{256,288},{28... | collective-permute-start | bytes 196616 | tf_op jit(solution)/shard_map/while/body/eval_jaxpr/ppermute | solution.py:244
  410.1 14.7 %collective-permute-start.1 = (f32[2,32,256]{2,1,0:T(8,128)S(1)}, f32[2,32,256]{2,1,0:T(8,128)S(1)}, u32[]{:S(2)}, u32[]{:S(2)}) collective-permute-start(f32[2,32,256]{2,1,0:T(8,128)S(1)} %slice.78), channel_id=1, source_target_pairs={{0,32},{32,64},{64,96},{128,160},{160,192},{192,224},{256,288},{28... | collective-permute-start | bytes 196616 | tf_op jit(solution)/shard_map/while/body/eval_jaxpr/ppermute | solution.py:244
  425.5 16.2 %collective-permute-start = (f32[2,32,256]{2,1,0:T(8,128)S(1)}, f32[2,32,256]{2,1,0:T(8,128)S(1)}, u32[]{:S(2)}, u32[]{:S(2)}) collective-permute-start(f32[2,32,256]{2,1,0:T(8,128)S(1)} %slice.77), channel_id=1, source_target_pairs={{0,32},{32,64},{64,96},{128,160},{160,192},{192,224},{256,288},{28... | collective-permute-start | bytes 196616 | tf_op jit(solution)/shard_map/while/body/eval_jaxpr/ppermute | solution.py:244
  439.8 14.7 %collective-permute-start.1 = (f32[2,32,256]{2,1,0:T(8,128)S(1)}, f32[2,32,256]{2,1,0:T(8,128)S(1)}, u32[]{:S(2)}, u32[]{:S(2)}) collective-permute-start(f32[2,32,256]{2,1,0:T(8,128)S(1)} %slice.78), channel_id=1, source_target_pairs={{0,32},{32,64},{64,96},{128,160},{160,192},{192,224},{256,288},{28... | collective-permute-start | bytes 196616 | tf_op jit(solution)/shard_map/while/body/eval_jaxpr/ppermute | solution.py:244
  455.2 16.2 %collective-permute-start = (f32[2,32,256]{2,1,0:T(8,128)S(1)}, f32[2,32,256]{2,1,0:T(8,128)S(1)}, u32[]{:S(2)}, u32[]{:S(2)}) collective-permute-start(f32[2,32,256]{2,1,0:T(8,128)S(1)} %slice.77), channel_id=1, source_target_pairs={{0,32},{32,64},{64,96},{128,160},{160,192},{192,224},{256,288},{28... | collective-permute-start | bytes 196616 | tf_op jit(solution)/shard_map/while/body/eval_jaxpr/ppermute | solution.py:244
  469.5 14.7 %collective-permute-start.1 = (f32[2,32,256]{2,1,0:T(8,128)S(1)}, f32[2,32,256]{2,1,0:T(8,128)S(1)}, u32[]{:S(2)}, u32[]{:S(2)}) collective-permute-start(f32[2,32,256]{2,1,0:T(8,128)S(1)} %slice.78), channel_id=1, source_target_pairs={{0,32},{32,64},{64,96},{128,160},{160,192},{192,224},{256,288},{28... | collective-permute-start | bytes 196616 | tf_op jit(solution)/shard_map/while/body/eval_jaxpr/ppermute | solution.py:244
  484.9 16.2 %collective-permute-start = (f32[2,32,256]{2,1,0:T(8,128)S(1)}, f32[2,32,256]{2,1,0:T(8,128)S(1)}, u32[]{:S(2)}, u32[]{:S(2)}) collective-permute-start(f32[2,32,256]{2,1,0:T(8,128)S(1)} %slice.77), channel_id=1, source_target_pairs={{0,32},{32,64},{64,96},{128,160},{160,192},{192,224},{256,288},{28... | collective-permute-start | bytes 196616 | tf_op jit(solution)/shard_map/while/body/eval_jaxpr/ppermute | solution.py:244
  491.3 14.7 %collective-permute-start.1 = (f32[2,32,256]{2,1,0:T(8,128)S(1)}, f32[2,32,256]{2,1,0:T(8,128)S(1)}, u32[]{:S(2)}, u32[]{:S(2)}) collective-permute-start(f32[2,32,256]{2,1,0:T(8,128)S(1)} %slice.78), channel_id=1, source_target_pairs={{0,32},{32,64},{64,96},{128,160},{160,192},{192,224},{256,288},{28... | collective-permute-start | bytes 196616 | tf_op jit(solution)/shard_map/while/body/eval_jaxpr/ppermute | solution.py:244
  506.7 16.2 %collective-permute-start = (f32[2,32,256]{2,1,0:T(8,128)S(1)}, f32[2,32,256]{2,1,0:T(8,128)S(1)}, u32[]{:S(2)}, u32[]{:S(2)}) collective-permute-start(f32[2,32,256]{2,1,0:T(8,128)S(1)} %slice.77), channel_id=1, source_target_pairs={{0,32},{32,64},{64,96},{128,160},{160,192},{192,224},{256,288},{28... | collective-permute-start | bytes 196616 | tf_op jit(solution)/shard_map/while/body/eval_jaxpr/ppermute | solution.py:244
  521.0 6.9 %collective-permute-start.1 = (f32[2,32,256]{2,1,0:T(8,128)S(1)}, f32[2,32,256]{2,1,0:T(8,128)S(1)}, u32[]{:S(2)}, u32[]{:S(2)}) collective-permute-start(f32[2,32,256]{2,1,0:T(8,128)S(1)} %slice.78), channel_id=1, source_target_pairs={{0,32},{32,64},{64,96},{128,160},{160,192},{192,224},{256,288},{28... | collective-permute-start | bytes 196616 | tf_op jit(solution)/shard_map/while/body/eval_jaxpr/ppermute | solution.py:244
  528.6 16.3 %collective-permute-start = (f32[2,32,256]{2,1,0:T(8,128)S(1)}, f32[2,32,256]{2,1,0:T(8,128)S(1)}, u32[]{:S(2)}, u32[]{:S(2)}) collective-permute-start(f32[2,32,256]{2,1,0:T(8,128)S(1)} %slice.77), channel_id=1, source_target_pairs={{0,32},{32,64},{64,96},{128,160},{160,192},{192,224},{256,288},{28... | collective-permute-start | bytes 196616 | tf_op jit(solution)/shard_map/while/body/eval_jaxpr/ppermute | solution.py:244
  535.2 14.7 %collective-permute-start.1 = (f32[2,32,256]{2,1,0:T(8,128)S(1)}, f32[2,32,256]{2,1,0:T(8,128)S(1)}, u32[]{:S(2)}, u32[]{:S(2)}) collective-permute-start(f32[2,32,256]{2,1,0:T(8,128)S(1)} %slice.78), channel_id=1, source_target_pairs={{0,32},{32,64},{64,96},{128,160},{160,192},{192,224},{256,288},{28... | collective-permute-start | bytes 196616 | tf_op jit(solution)/shard_map/while/body/eval_jaxpr/ppermute | solution.py:244
Sparse Core Ops, SparseCore 0:
  9.4 154.4 all-gather.9

commit v4 on v3

--- a/solution.py
+++ b/solution.py
@@ -12,7 +12,7 @@
 BF16 = jnp.bfloat16
 
 ROWS = 16
-GROUP = 8
+GROUP = 16
 PAY = 288
 LAG = 2
 
@@ -138,8 +138,9 @@
             return rows_step(get_mid, before, mid[base + GROUP], e_out, base, GROUP, last_n)
 
         last = ROWS - GROUP
-        lax.fori_loop(0, ROWS // GROUP - 1, one, 0)
-        rows_step(get_e, e_in[last - 1], near, mid, last, GROUP, None)
+        if last:
+            lax.fori_loop(0, ROWS // GROUP - 1, one, 0)
+        rows_step(get_e, e_in[max(last - 1, 0)], near, mid, last, GROUP, None)
         rows_step(lambda *_: near[None], e_in[ROWS - 1], far, mid, ROWS, 1, None)
         last_n = lax.fori_loop(0, ROWS // GROUP, two, jnp.zeros((32, 128), F32))
 

time: 583 us -> 660 us (1.13)
  Pallas kernels: 183 us -> 252 us
    pallas_call x22, Pallas kernels: 183 us -> 252 us  [section_call(): pl.pallas_call(section_kernel, out_shape=(jax.ShapeDtypeStruct((1,), jnp....]
  transfers between devices with their start and end apart: 26 -> 26, of which waited for: 4 -> 4; matrix products, arithmetic and copies ran while one was open for 4% -> 4% of each run, Pallas kernels for 32% -> 38%
where the time goes in v4:
time: 660 us; the launch traced here: 658 us
  Pallas kernels  252 us (38%)
  starting transfers between devices  174 us (26%)
  waiting for transfers between devices  97.7 us (15%)
  blocking collectives  79.4 us (12%)
  local copies, waits for them, and re-layouts  22.7 us (3%)
  between operations  15.6 us (2%)
  loops' own time  8.15 us (1%)
  other arithmetic  7.83 us (1%)
    pallas_call x22, Pallas kernels, section_call(): pl.pallas_call(section_kernel, out_shape=(jax.ShapeDtypeStruct((1,), jnp....  252 us
    ppermute x22, starting transfers between devices, two_turns(): coming = lax.ppermute(halo[:, 256:], 'segment', ahead)  149 us
    all_to_all x1, waiting for transfers between devices, local(): lax.all_to_all(jnp.broadcast_to(pair[None], (8, 2, 144, 256)), 'row', 0,...  56.5 us
    all_gather x22, blocking collectives, two_turns(): halo = lax.all_gather(pay, 'row', axis_index_groups=chips)  49 us
    all_gather x1, waiting for transfers between devices, local(): w_all = lax.all_gather(dispersion[0], 'segment')  24.2 us
    all_to_all x1, blocking collectives, local(): out = lax.all_to_all(mine, 'segment', 0, 0, axis_index_groups=rings)  19.7 us
    ppermute x1, waiting for transfers between devices, local(): pair = jnp.where(core == z_hi, pair, lax.ppermute(pair, 'row', across))  13.2 us
  transfers between devices with their start and end apart: 26, of which 4 were waited for; matrix products, arithmetic and copies ran while one was open for 4% of the time, Pallas kernels for 38%

profile of v4, /device:TPU:64, one launch (start us, length us, event | category | flops | bytes accessed | tf_op | source)
XLA Modules:
  0.0 657.9 jit_solution(5756230473816084333)
XLA Ops:
  8.7 9.4 %all-to-all-start = ((f32[16,1,256]{2,1,0:T(1,128)}), f32[16,1,256]{2,1,0:T(1,128)S(1)}, u32[]{:S(2)}, u32[]{:S(2)}) async-start(f32[16,1,256]{2,1,0:T(1,128)} %broadcast_in_dim.57), calls=%async_computation | async-start | bytes 32768 | tf_op jit(solution)/shard_map/all_to_all | solution.py:206
  21.5 3.1 all-to-all-done
  26.6 8.2 %collective-permute-start.2 = (f32[2,144,256]{2,1,0:T(8,128)S(1)}, f32[2,144,256]{2,1,0:T(8,128)S(1)}, u32[]{:S(2)}, u32[]{:S(2)}) collective-permute-start(f32[2,144,256]{2,1,0:T(8,128)S(1)} %bitcast.49), channel_id=1, source_target_pairs={{0,16},{2,18},{4,20},{6,22},{8,24},{10,26},{12,28},{14,30},{17,1},... | collective-permute-start | bytes 884744 | tf_op jit(solution)/shard_map/ppermute | solution.py:213
  34.9 13.2 %collective-permute-done.2 = f32[2,144,256]{2,1,0:T(8,128)S(1)} collective-permute-done((f32[2,144,256]{2,1,0:T(8,128)S(1)}, f32[2,144,256]{2,1,0:T(8,128)S(1)}, u32[]{:S(2)}, u32[]{:S(2)}) %collective-permute-start.2) | collective-permute-done | bytes 294944 | tf_op jit(solution)/shard_map/ppermute | solution.py:213
  49.8 7.1 %all-to-all-start.1 = ((f32[8,2,144,256]{3,2,1,0:T(8,128)}), f32[8,2,144,256]{3,2,1,0:T(8,128)S(1)}, u32[]{:S(2)}, u32[]{:S(2)}) async-start(f32[8,2,144,256]{3,2,1,0:T(8,128)} %broadcast_in_dim.58), calls=%async_computation.1 | async-start | bytes 4718592 | tf_op jit(solution)/shard_map/all_to_all | solution.py:214
  57.0 56.5 %all-to-all-done.1 = f32[8,2,144,256]{3,2,1,0:T(8,128)S(1)} async-done(((f32[8,2,144,256]{3,2,1,0:T(8,128)}), f32[8,2,144,256]{3,2,1,0:T(8,128)S(1)}, u32[]{:S(2)}, u32[]{:S(2)}) %all-to-all-start.1) | async-done | bytes 2359328 | tf_op jit(solution)/shard_map/all_to_all | solution.py:214
  114.9 2.7 reverse_select_fusion
  123.6 4.1 broadcast_select_fusion.1
  127.7 3.8 stack.32
  131.5 3.0 copy.28
  134.6 2.8 pad.9.clone
  137.5 2.2 all-gather.3
  139.7 24.2 %all-gather.10.cloned.1.call-done = f32[16,768,256]{2,1,0:T(8,128)} async-done(((f32[1,768,256]{2,1,0:T(8,128)}), f32[16,768,256]{2,1,0:T(8,128)}) %all-gather.10.cloned.1.call-update) | async-done | bytes 12582928 | tf_op jit(solution)/shard_map/all_gather | solution.py:202
  165.0 459.1 %while.18 = (s32[]{:T(128)}, s32[1]{0:T(128)}, f32[16,4,32,256]{3,2,1,0:T(8,128)}, f32[2,288,256]{2,1,0:T(8,128)S(1)}, f32[2,32,256]{2,1,0:T(8,128)S(1)}, /*inde...) while((s32[]{:T(128)}, s32[1]{0:T(128)}, ...), condition=%wide.region_1.2_spmd, body=%wide.region_0.1_spmd.sunk | while | flops 9965666304 | bytes 19333300 | solution.py:252
  166.3 14.4 %section.2 = (s32[1]{0:T(128)}, f32[16,4,32,256]{3,2,1,0:T(8,128)S(1)}, f32[288,256]{1,0:T(8,128)S(1)}, f32[4,2,4,32,256]{4,3,2,1,0:T(8,128)}) custom-call(s32[1]{0:T(128)} %get-tuple-element.196.count, s32[5]{0:T(128)S(1)} %get-tuple-element.211.ids, f32[16,4,32,256]{3,2,1,0:T(8,128)} %get-tuple-element.197.e_in, ...), custom_call_target="tpu_custom_call", output_to_operand_aliasing={{3}: (7, {})} | custom-call | flops 4982833152 | bytes 8388608 | tf_op jit(solution)/shard_map/while/body/eval_jaxpr/section/pallas_call | solution.py:163
  180.8 2.2 all-gather.6
  184.3 14.9 %section.3 = (s32[1]{0:T(128)}, f32[16,4,32,256]{3,2,1,0:T(8,128)}, f32[288,256]{1,0:T(8,128)S(1)}, f32[4,2,4,32,256]{4,3,2,1,0:T(8,128)}) custom-call(s32[1]{0:T(128)} %get-tuple-element.177.count, s32[5]{0:T(128)S(1)} %get-tuple-element.211.ids, f32[16,4,32,256]{3,2,1,0:T(8,128)S(1)} %get-tuple-element.178.e_in, ...), custom_call_target="tpu_custom_call", output_to_operand_aliasing={{3}: (7, {})} | custom-call | flops 4982833152 | bytes 8388608 | tf_op jit(solution)/shard_map/while/body/eval_jaxpr/section/pallas_call | solution.py:163
  202.1 74.1 %collective-permute-start = (f32[2,32,256]{2,1,0:T(8,128)S(1)}, f32[2,32,256]{2,1,0:T(8,128)S(1)}, u32[]{:S(2)}, u32[]{:S(2)}) collective-permute-start(f32[2,32,256]{2,1,0:T(8,128)S(1)} %slice.77), channel_id=1, source_target_pairs={{0,32},{32,64},{64,96},{128,160},{160,192},{192,224},{256,288},{28... | collective-permute-start | bytes 196616 | tf_op jit(solution)/shard_map/while/body/eval_jaxpr/ppermute | solution.py:245
  276.2 14.4 %section.2 = (s32[1]{0:T(128)}, f32[16,4,32,256]{3,2,1,0:T(8,128)S(1)}, f32[288,256]{1,0:T(8,128)S(1)}, f32[4,2,4,32,256]{4,3,2,1,0:T(8,128)}) custom-call(s32[1]{0:T(128)} %get-tuple-element.196.count, s32[5]{0:T(128)S(1)} %get-tuple-element.211.ids, f32[16,4,32,256]{3,2,1,0:T(8,128)} %get-tuple-element.197.e_in, ...), custom_call_target="tpu_custom_call", output_to_operand_aliasing={{3}: (7, {})} | custom-call | flops 4982833152 | bytes 8388608 | tf_op jit(solution)/shard_map/while/body/eval_jaxpr/section/pallas_call | solution.py:163
  294.8 14.9 %section.3 = (s32[1]{0:T(128)}, f32[16,4,32,256]{3,2,1,0:T(8,128)}, f32[288,256]{1,0:T(8,128)S(1)}, f32[4,2,4,32,256]{4,3,2,1,0:T(8,128)}) custom-call(s32[1]{0:T(128)} %get-tuple-element.177.count, s32[5]{0:T(128)S(1)} %get-tuple-element.211.ids, f32[16,4,32,256]{3,2,1,0:T(8,128)S(1)} %get-tuple-element.178.e_in, ...), custom_call_target="tpu_custom_call", output_to_operand_aliasing={{3}: (7, {})} | custom-call | flops 4982833152 | bytes 8388608 | tf_op jit(solution)/shard_map/while/body/eval_jaxpr/section/pallas_call | solution.py:163
  314.6 15.1 %section.2 = (s32[1]{0:T(128)}, f32[16,4,32,256]{3,2,1,0:T(8,128)S(1)}, f32[288,256]{1,0:T(8,128)S(1)}, f32[4,2,4,32,256]{4,3,2,1,0:T(8,128)}) custom-call(s32[1]{0:T(128)} %get-tuple-element.196.count, s32[5]{0:T(128)S(1)} %get-tuple-element.211.ids, f32[16,4,32,256]{3,2,1,0:T(8,128)} %get-tuple-element.197.e_in, ...), custom_call_target="tpu_custom_call", output_to_operand_aliasing={{3}: (7, {})} | custom-call | flops 4982833152 | bytes 8388608 | tf_op jit(solution)/shard_map/while/body/eval_jaxpr/section/pallas_call | solution.py:163
  329.7 2.2 all-gather.6
  333.2 15.6 %section.3 = (s32[1]{0:T(128)}, f32[16,4,32,256]{3,2,1,0:T(8,128)}, f32[288,256]{1,0:T(8,128)S(1)}, f32[4,2,4,32,256]{4,3,2,1,0:T(8,128)}) custom-call(s32[1]{0:T(128)} %get-tuple-element.177.count, s32[5]{0:T(128)S(1)} %get-tuple-element.211.ids, f32[16,4,32,256]{3,2,1,0:T(8,128)S(1)} %get-tuple-element.178.e_in, ...), custom_call_target="tpu_custom_call", output_to_operand_aliasing={{3}: (7, {})} | custom-call | flops 4982833152 | bytes 8388608 | tf_op jit(solution)/shard_map/while/body/eval_jaxpr/section/pallas_call | solution.py:163
  353.0 15.1 %section.2 = (s32[1]{0:T(128)}, f32[16,4,32,256]{3,2,1,0:T(8,128)S(1)}, f32[288,256]{1,0:T(8,128)S(1)}, f32[4,2,4,32,256]{4,3,2,1,0:T(8,128)}) custom-call(s32[1]{0:T(128)} %get-tuple-element.196.count, s32[5]{0:T(128)S(1)} %get-tuple-element.211.ids, f32[16,4,32,256]{3,2,1,0:T(8,128)} %get-tuple-element.197.e_in, ...), custom_call_target="tpu_custom_call", output_to_operand_aliasing={{3}: (7, {})} | custom-call | flops 4982833152 | bytes 8388608 | tf_op jit(solution)/shard_map/while/body/eval_jaxpr/section/pallas_call | solution.py:163
  372.2 15.5 %section.3 = (s32[1]{0:T(128)}, f32[16,4,32,256]{3,2,1,0:T(8,128)}, f32[288,256]{1,0:T(8,128)S(1)}, f32[4,2,4,32,256]{4,3,2,1,0:T(8,128)}) custom-call(s32[1]{0:T(128)} %get-tuple-element.177.count, s32[5]{0:T(128)S(1)} %get-tuple-element.211.ids, f32[16,4,32,256]{3,2,1,0:T(8,128)S(1)} %get-tuple-element.178.e_in, ...), custom_call_target="tpu_custom_call", output_to_operand_aliasing={{3}: (7, {})} | custom-call | flops 4982833152 | bytes 8388608 | tf_op jit(solution)/shard_map/while/body/eval_jaxpr/section/pallas_call | solution.py:163
  387.8 2.2 all-gather.7
  392.6 14.4 %section.2 = (s32[1]{0:T(128)}, f32[16,4,32,256]{3,2,1,0:T(8,128)S(1)}, f32[288,256]{1,0:T(8,128)S(1)}, f32[4,2,4,32,256]{4,3,2,1,0:T(8,128)}) custom-call(s32[1]{0:T(128)} %get-tuple-element.196.count, s32[5]{0:T(128)S(1)} %get-tuple-element.211.ids, f32[16,4,32,256]{3,2,1,0:T(8,128)} %get-tuple-element.197.e_in, ...), custom_call_target="tpu_custom_call", output_to_operand_aliasing={{3}: (7, {})} | custom-call | flops 4982833152 | bytes 8388608 | tf_op jit(solution)/shard_map/while/body/eval_jaxpr/section/pallas_call | solution.py:163
  409.3 2.6 collective-permute-start.1
  411.9 14.9 %section.3 = (s32[1]{0:T(128)}, f32[16,4,32,256]{3,2,1,0:T(8,128)}, f32[288,256]{1,0:T(8,128)S(1)}, f32[4,2,4,32,256]{4,3,2,1,0:T(8,128)}) custom-call(s32[1]{0:T(128)} %get-tuple-element.177.count, s32[5]{0:T(128)S(1)} %get-tuple-element.211.ids, f32[16,4,32,256]{3,2,1,0:T(8,128)S(1)} %get-tuple-element.178.e_in, ...), custom_call_target="tpu_custom_call", output_to_operand_aliasing={{3}: (7, {})} | custom-call | flops 4982833152 | bytes 8388608 | tf_op jit(solution)/shard_map/while/body/eval_jaxpr/section/pallas_call | solution.py:163
  429.7 2.6 collective-permute-start
  432.3 14.4 %section.2 = (s32[1]{0:T(128)}, f32[16,4,32,256]{3,2,1,0:T(8,128)S(1)}, f32[288,256]{1,0:T(8,128)S(1)}, f32[4,2,4,32,256]{4,3,2,1,0:T(8,128)}) custom-call(s32[1]{0:T(128)} %get-tuple-element.196.count, s32[5]{0:T(128)S(1)} %get-tuple-element.211.ids, f32[16,4,32,256]{3,2,1,0:T(8,128)} %get-tuple-element.197.e_in, ...), custom_call_target="tpu_custom_call", output_to_operand_aliasing={{3}: (7, {})} | custom-call | flops 4982833152 | bytes 8388608 | tf_op jit(solution)/shard_map/while/body/eval_jaxpr/section/pallas_call | solution.py:163
  450.9 14.9 %section.3 = (s32[1]{0:T(128)}, f32[16,4,32,256]{3,2,1,0:T(8,128)}, f32[288,256]{1,0:T(8,128)S(1)}, f32[4,2,4,32,256]{4,3,2,1,0:T(8,128)}) custom-call(s32[1]{0:T(128)} %get-tuple-element.177.count, s32[5]{0:T(128)S(1)} %get-tuple-element.211.ids, f32[16,4,32,256]{3,2,1,0:T(8,128)S(1)} %get-tuple-element.178.e_in, ...), custom_call_target="tpu_custom_call", output_to_operand_aliasing={{3}: (7, {})} | custom-call | flops 4982833152 | bytes 8388608 | tf_op jit(solution)/shard_map/while/body/eval_jaxpr/section/pallas_call | solution.py:163
  470.7 14.4 %section.2 = (s32[1]{0:T(128)}, f32[16,4,32,256]{3,2,1,0:T(8,128)S(1)}, f32[288,256]{1,0:T(8,128)S(1)}, f32[4,2,4,32,256]{4,3,2,1,0:T(8,128)}) custom-call(s32[1]{0:T(128)} %get-tuple-element.196.count, s32[5]{0:T(128)S(1)} %get-tuple-element.211.ids, f32[16,4,32,256]{3,2,1,0:T(8,128)} %get-tuple-element.197.e_in, ...), custom_call_target="tpu_custom_call", output_to_operand_aliasing={{3}: (7, {})} | custom-call | flops 4982833152 | bytes 8388608 | tf_op jit(solution)/shard_map/while/body/eval_jaxpr/section/pallas_call | solution.py:163
  489.3 14.9 %section.3 = (s32[1]{0:T(128)}, f32[16,4,32,256]{3,2,1,0:T(8,128)}, f32[288,256]{1,0:T(8,128)S(1)}, f32[4,2,4,32,256]{4,3,2,1,0:T(8,128)}) custom-call(s32[1]{0:T(128)} %get-tuple-element.177.count, s32[5]{0:T(128)S(1)} %get-tuple-element.211.ids, f32[16,4,32,256]{3,2,1,0:T(8,128)S(1)} %get-tuple-element.178.e_in, ...), custom_call_target="tpu_custom_call", output_to_operand_aliasing={{3}: (7, {})} | custom-call | flops 4982833152 | bytes 8388608 | tf_op jit(solution)/shard_map/while/body/eval_jaxpr/section/pallas_call | solution.py:163
  509.0 14.4 %section.2 = (s32[1]{0:T(128)}, f32[16,4,32,256]{3,2,1,0:T(8,128)S(1)}, f32[288,256]{1,0:T(8,128)S(1)}, f32[4,2,4,32,256]{4,3,2,1,0:T(8,128)}) custom-call(s32[1]{0:T(128)} %get-tuple-element.196.count, s32[5]{0:T(128)S(1)} %get-tuple-element.211.ids, f32[16,4,32,256]{3,2,1,0:T(8,128)} %get-tuple-element.197.e_in, ...), custom_call_target="tpu_custom_call", output_to_operand_aliasing={{3}: (7, {})} | custom-call | flops 4982833152 | bytes 8388608 | tf_op jit(solution)/shard_map/while/body/eval_jaxpr/section/pallas_call | solution.py:163
  527.6 14.9 %section.3 = (s32[1]{0:T(128)}, f32[16,4,32,256]{3,2,1,0:T(8,128)}, f32[288,256]{1,0:T(8,128)S(1)}, f32[4,2,4,32,256]{4,3,2,1,0:T(8,128)}) custom-call(s32[1]{0:T(128)} %get-tuple-element.177.count, s32[5]{0:T(128)S(1)} %get-tuple-element.211.ids, f32[16,4,32,256]{3,2,1,0:T(8,128)S(1)} %get-tuple-element.178.e_in, ...), custom_call_target="tpu_custom_call", output_to_operand_aliasing={{3}: (7, {})} | custom-call | flops 4982833152 | bytes 8388608 | tf_op jit(solution)/shard_map/while/body/eval_jaxpr/section/pallas_call | solution.py:163
  547.4 2.3 section.2
  551.9 14.0 %collective-permute-start.1 = (f32[2,32,256]{2,1,0:T(8,128)S(1)}, f32[2,32,256]{2,1,0:T(8,128)S(1)}, u32[]{:S(2)}, u32[]{:S(2)}) collective-permute-start(f32[2,32,256]{2,1,0:T(8,128)S(1)} %slice.78), channel_id=1, source_target_pairs={{0,32},{32,64},{64,96},{128,160},{160,192},{192,224},{256,288},{28... | collective-permute-start | bytes 196616 | tf_op jit(solution)/shard_map/while/body/eval_jaxpr/ppermute | solution.py:245
  566.0 2.7 section.3
  571.6 14.1 %collective-permute-start = (f32[2,32,256]{2,1,0:T(8,128)S(1)}, f32[2,32,256]{2,1,0:T(8,128)S(1)}, u32[]{:S(2)}, u32[]{:S(2)}) collective-permute-start(f32[2,32,256]{2,1,0:T(8,128)S(1)} %slice.77), channel_id=1, source_target_pairs={{0,32},{32,64},{64,96},{128,160},{160,192},{192,224},{256,288},{28... | collective-permute-start | bytes 196616 | tf_op jit(solution)/shard_map/while/body/eval_jaxpr/ppermute | solution.py:245
  585.7 2.3 section.2
  592.2 2.7 section.3
  594.9 2.2 all-gather.7
  599.9 2.3 section.2
  604.4 14.0 %collective-permute-start.1 = (f32[2,32,256]{2,1,0:T(8,128)S(1)}, f32[2,32,256]{2,1,0:T(8,128)S(1)}, u32[]{:S(2)}, u32[]{:S(2)}) collective-permute-start(f32[2,32,256]{2,1,0:T(8,128)S(1)} %slice.78), channel_id=1, source_target_pairs={{0,32},{32,64},{64,96},{128,160},{160,192},{192,224},{256,288},{28... | collective-permute-start | bytes 196616 | tf_op jit(solution)/shard_map/while/body/eval_jaxpr/ppermute | solution.py:245
  618.5 2.7 section.3
  625.6 4.6 all_to_all.20
  630.2 19.7 %all_to_all.21 = f32[4,4,32,256]{3,2,1,0:T(8,128)S(1)} all-to-all(f32[4,4,32,256]{3,2,1,0:T(8,128)S(1)} %dynamic-slice_bitcast_fusion), channel_id=1, replica_groups={{0,32,64,96},{128,160,192,224},{256,288,320,352},{384,416,448,480},{1,3..., dimensions={0} | all-to-all | bytes 1048576 | tf_op jit(solution)/shard_map/all_to_all | solution.py:257
  (117 shorter events, 86.9 us)
Async XLA Ops:
  6.5 14.9 %copy-start = (f32[4,1,32,4,256]{4,3,2,1,0:T(4,128)S(1)}, f32[4,1,32,4,256]{4,3,2,1,0:T(4,128)}, u32[]{:S(2)}) copy-start(f32[4,1,32,4,256]{4,3,2,1,0:T(4,128)} %param.8) | copy-start | bytes 1572868
  6.5 157.4 %all-gather.10.cloned.1.call-start = ((), (), s32[]{:S(2)}) async-start(), calls=%async_computation.4 | async-start | bytes 13369344 | tf_op jit(solution)/shard_map/all_gather | solution.py:202
  8.7 15.9 %all-to-all-start = ((f32[16,1,256]{2,1,0:T(1,128)}), f32[16,1,256]{2,1,0:T(1,128)S(1)}, u32[]{:S(2)}, u32[]{:S(2)}) async-start(f32[16,1,256]{2,1,0:T(1,128)} %broadcast_in_dim.57), calls=%async_computation | async-start | bytes 32768 | tf_op jit(solution)/shard_map/all_to_all | solution.py:206
  26.6 21.5 %collective-permute-start.2 = (f32[2,144,256]{2,1,0:T(8,128)S(1)}, f32[2,144,256]{2,1,0:T(8,128)S(1)}, u32[]{:S(2)}, u32[]{:S(2)}) collective-permute-start(f32[2,144,256]{2,1,0:T(8,128)S(1)} %bitcast.49), channel_id=1, source_target_pairs={{0,16},{2,18},{4,20},{6,22},{8,24},{10,26},{12,28},{14,30},{17,1},... | collective-permute-start | bytes 884744 | tf_op jit(solution)/shard_map/ppermute | solution.py:213
  49.8 63.7 %all-to-all-start.1 = ((f32[8,2,144,256]{3,2,1,0:T(8,128)}), f32[8,2,144,256]{3,2,1,0:T(8,128)S(1)}, u32[]{:S(2)}, u32[]{:S(2)}) async-start(f32[8,2,144,256]{3,2,1,0:T(8,128)} %broadcast_in_dim.58), calls=%async_computation.1 | async-start | bytes 4718592 | tf_op jit(solution)/shard_map/all_to_all | solution.py:214
  113.5 1.4 copy-start.1
  165.0 19.3 %collective-permute-start = (f32[2,32,256]{2,1,0:T(8,128)S(1)}, f32[2,32,256]{2,1,0:T(8,128)S(1)}, u32[]{:S(2)}, u32[]{:S(2)}) collective-permute-start(f32[2,32,256]{2,1,0:T(8,128)S(1)} %slice.77), channel_id=1, source_target_pairs={{0,32},{32,64},{64,96},{128,160},{160,192},{192,224},{256,288},{28... | collective-permute-start | bytes 196616 | tf_op jit(solution)/shard_map/while/body/eval_jaxpr/ppermute | solution.py:245
  183.0 18.4 %collective-permute-start.1 = (f32[2,32,256]{2,1,0:T(8,128)S(1)}, f32[2,32,256]{2,1,0:T(8,128)S(1)}, u32[]{:S(2)}, u32[]{:S(2)}) collective-permute-start(f32[2,32,256]{2,1,0:T(8,128)S(1)} %slice.78), channel_id=1, source_target_pairs={{0,32},{32,64},{64,96},{128,160},{160,192},{192,224},{256,288},{28... | collective-permute-start | bytes 196616 | tf_op jit(solution)/shard_map/while/body/eval_jaxpr/ppermute | solution.py:245
  202.1 92.7 %collective-permute-start = (f32[2,32,256]{2,1,0:T(8,128)S(1)}, f32[2,32,256]{2,1,0:T(8,128)S(1)}, u32[]{:S(2)}, u32[]{:S(2)}) collective-permute-start(f32[2,32,256]{2,1,0:T(8,128)S(1)} %slice.77), channel_id=1, source_target_pairs={{0,32},{32,64},{64,96},{128,160},{160,192},{192,224},{256,288},{28... | collective-permute-start | bytes 196616 | tf_op jit(solution)/shard_map/while/body/eval_jaxpr/ppermute | solution.py:245
  292.9 19.0 %collective-permute-start.1 = (f32[2,32,256]{2,1,0:T(8,128)S(1)}, f32[2,32,256]{2,1,0:T(8,128)S(1)}, u32[]{:S(2)}, u32[]{:S(2)}) collective-permute-start(f32[2,32,256]{2,1,0:T(8,128)S(1)} %slice.78), channel_id=1, source_target_pairs={{0,32},{32,64},{64,96},{128,160},{160,192},{192,224},{256,288},{28... | collective-permute-start | bytes 196616 | tf_op jit(solution)/shard_map/while/body/eval_jaxpr/ppermute | solution.py:245
  312.6 20.6 %collective-permute-start = (f32[2,32,256]{2,1,0:T(8,128)S(1)}, f32[2,32,256]{2,1,0:T(8,128)S(1)}, u32[]{:S(2)}, u32[]{:S(2)}) collective-permute-start(f32[2,32,256]{2,1,0:T(8,128)S(1)} %slice.77), channel_id=1, source_target_pairs={{0,32},{32,64},{64,96},{128,160},{160,192},{192,224},{256,288},{28... | collective-permute-start | bytes 196616 | tf_op jit(solution)/shard_map/while/body/eval_jaxpr/ppermute | solution.py:245
  331.9 19.1 %collective-permute-start.1 = (f32[2,32,256]{2,1,0:T(8,128)S(1)}, f32[2,32,256]{2,1,0:T(8,128)S(1)}, u32[]{:S(2)}, u32[]{:S(2)}) collective-permute-start(f32[2,32,256]{2,1,0:T(8,128)S(1)} %slice.78), channel_id=1, source_target_pairs={{0,32},{32,64},{64,96},{128,160},{160,192},{192,224},{256,288},{28... | collective-permute-start | bytes 196616 | tf_op jit(solution)/shard_map/while/body/eval_jaxpr/ppermute | solution.py:245
  351.7 20.5 %collective-permute-start = (f32[2,32,256]{2,1,0:T(8,128)S(1)}, f32[2,32,256]{2,1,0:T(8,128)S(1)}, u32[]{:S(2)}, u32[]{:S(2)}) collective-permute-start(f32[2,32,256]{2,1,0:T(8,128)S(1)} %slice.77), channel_id=1, source_target_pairs={{0,32},{32,64},{64,96},{128,160},{160,192},{192,224},{256,288},{28... | collective-permute-start | bytes 196616 | tf_op jit(solution)/shard_map/while/body/eval_jaxpr/ppermute | solution.py:245
  370.4 19.6 %collective-permute-start.1 = (f32[2,32,256]{2,1,0:T(8,128)S(1)}, f32[2,32,256]{2,1,0:T(8,128)S(1)}, u32[]{:S(2)}, u32[]{:S(2)}) collective-permute-start(f32[2,32,256]{2,1,0:T(8,128)S(1)} %slice.78), channel_id=1, source_target_pairs={{0,32},{32,64},{64,96},{128,160},{160,192},{192,224},{256,288},{28... | collective-permute-start | bytes 196616 | tf_op jit(solution)/shard_map/while/body/eval_jaxpr/ppermute | solution.py:245
  390.7 21.2 %collective-permute-start = (f32[2,32,256]{2,1,0:T(8,128)S(1)}, f32[2,32,256]{2,1,0:T(8,128)S(1)}, u32[]{:S(2)}, u32[]{:S(2)}) collective-permute-start(f32[2,32,256]{2,1,0:T(8,128)S(1)} %slice.77), channel_id=1, source_target_pairs={{0,32},{32,64},{64,96},{128,160},{160,192},{192,224},{256,288},{28... | collective-permute-start | bytes 196616 | tf_op jit(solution)/shard_map/while/body/eval_jaxpr/ppermute | solution.py:245
  409.3 19.7 %collective-permute-start.1 = (f32[2,32,256]{2,1,0:T(8,128)S(1)}, f32[2,32,256]{2,1,0:T(8,128)S(1)}, u32[]{:S(2)}, u32[]{:S(2)}) collective-permute-start(f32[2,32,256]{2,1,0:T(8,128)S(1)} %slice.78), channel_id=1, source_target_pairs={{0,32},{32,64},{64,96},{128,160},{160,192},{192,224},{256,288},{28... | collective-permute-start | bytes 196616 | tf_op jit(solution)/shard_map/while/body/eval_jaxpr/ppermute | solution.py:245
  429.7 21.2 %collective-permute-start = (f32[2,32,256]{2,1,0:T(8,128)S(1)}, f32[2,32,256]{2,1,0:T(8,128)S(1)}, u32[]{:S(2)}, u32[]{:S(2)}) collective-permute-start(f32[2,32,256]{2,1,0:T(8,128)S(1)} %slice.77), channel_id=1, source_target_pairs={{0,32},{32,64},{64,96},{128,160},{160,192},{192,224},{256,288},{28... | collective-permute-start | bytes 196616 | tf_op jit(solution)/shard_map/while/body/eval_jaxpr/ppermute | solution.py:245
  449.0 19.0 %collective-permute-start.1 = (f32[2,32,256]{2,1,0:T(8,128)S(1)}, f32[2,32,256]{2,1,0:T(8,128)S(1)}, u32[]{:S(2)}, u32[]{:S(2)}) collective-permute-start(f32[2,32,256]{2,1,0:T(8,128)S(1)} %slice.78), channel_id=1, source_target_pairs={{0,32},{32,64},{64,96},{128,160},{160,192},{192,224},{256,288},{28... | collective-permute-start | bytes 196616 | tf_op jit(solution)/shard_map/while/body/eval_jaxpr/ppermute | solution.py:245
  468.7 20.5 %collective-permute-start = (f32[2,32,256]{2,1,0:T(8,128)S(1)}, f32[2,32,256]{2,1,0:T(8,128)S(1)}, u32[]{:S(2)}, u32[]{:S(2)}) collective-permute-start(f32[2,32,256]{2,1,0:T(8,128)S(1)} %slice.77), channel_id=1, source_target_pairs={{0,32},{32,64},{64,96},{128,160},{160,192},{192,224},{256,288},{28... | collective-permute-start | bytes 196616 | tf_op jit(solution)/shard_map/while/body/eval_jaxpr/ppermute | solution.py:245
  487.3 19.0 %collective-permute-start.1 = (f32[2,32,256]{2,1,0:T(8,128)S(1)}, f32[2,32,256]{2,1,0:T(8,128)S(1)}, u32[]{:S(2)}, u32[]{:S(2)}) collective-permute-start(f32[2,32,256]{2,1,0:T(8,128)S(1)} %slice.78), channel_id=1, source_target_pairs={{0,32},{32,64},{64,96},{128,160},{160,192},{192,224},{256,288},{28... | collective-permute-start | bytes 196616 | tf_op jit(solution)/shard_map/while/body/eval_jaxpr/ppermute | solution.py:245
  507.1 20.5 %collective-permute-start = (f32[2,32,256]{2,1,0:T(8,128)S(1)}, f32[2,32,256]{2,1,0:T(8,128)S(1)}, u32[]{:S(2)}, u32[]{:S(2)}) collective-permute-start(f32[2,32,256]{2,1,0:T(8,128)S(1)} %slice.77), channel_id=1, source_target_pairs={{0,32},{32,64},{64,96},{128,160},{160,192},{192,224},{256,288},{28... | collective-permute-start | bytes 196616 | tf_op jit(solution)/shard_map/while/body/eval_jaxpr/ppermute | solution.py:245
  525.7 19.0 %collective-permute-start.1 = (f32[2,32,256]{2,1,0:T(8,128)S(1)}, f32[2,32,256]{2,1,0:T(8,128)S(1)}, u32[]{:S(2)}, u32[]{:S(2)}) collective-permute-start(f32[2,32,256]{2,1,0:T(8,128)S(1)} %slice.78), channel_id=1, source_target_pairs={{0,32},{32,64},{64,96},{128,160},{160,192},{192,224},{256,288},{28... | collective-permute-start | bytes 196616 | tf_op jit(solution)/shard_map/while/body/eval_jaxpr/ppermute | solution.py:245
  545.4 20.5 %collective-permute-start = (f32[2,32,256]{2,1,0:T(8,128)S(1)}, f32[2,32,256]{2,1,0:T(8,128)S(1)}, u32[]{:S(2)}, u32[]{:S(2)}) collective-permute-start(f32[2,32,256]{2,1,0:T(8,128)S(1)} %slice.77), channel_id=1, source_target_pairs={{0,32},{32,64},{64,96},{128,160},{160,192},{192,224},{256,288},{28... | collective-permute-start | bytes 196616 | tf_op jit(solution)/shard_map/while/body/eval_jaxpr/ppermute | solution.py:245
  551.9 19.0 %collective-permute-start.1 = (f32[2,32,256]{2,1,0:T(8,128)S(1)}, f32[2,32,256]{2,1,0:T(8,128)S(1)}, u32[]{:S(2)}, u32[]{:S(2)}) collective-permute-start(f32[2,32,256]{2,1,0:T(8,128)S(1)} %slice.78), channel_id=1, source_target_pairs={{0,32},{32,64},{64,96},{128,160},{160,192},{192,224},{256,288},{28... | collective-permute-start | bytes 196616 | tf_op jit(solution)/shard_map/while/body/eval_jaxpr/ppermute | solution.py:245
  571.6 20.5 %collective-permute-start = (f32[2,32,256]{2,1,0:T(8,128)S(1)}, f32[2,32,256]{2,1,0:T(8,128)S(1)}, u32[]{:S(2)}, u32[]{:S(2)}) collective-permute-start(f32[2,32,256]{2,1,0:T(8,128)S(1)} %slice.77), channel_id=1, source_target_pairs={{0,32},{32,64},{64,96},{128,160},{160,192},{192,224},{256,288},{28... | collective-permute-start | bytes 196616 | tf_op jit(solution)/shard_map/while/body/eval_jaxpr/ppermute | solution.py:245
  590.3 6.9 %collective-permute-start.1 = (f32[2,32,256]{2,1,0:T(8,128)S(1)}, f32[2,32,256]{2,1,0:T(8,128)S(1)}, u32[]{:S(2)}, u32[]{:S(2)}) collective-permute-start(f32[2,32,256]{2,1,0:T(8,128)S(1)} %slice.78), channel_id=1, source_target_pairs={{0,32},{32,64},{64,96},{128,160},{160,192},{192,224},{256,288},{28... | collective-permute-start | bytes 196616 | tf_op jit(solution)/shard_map/while/body/eval_jaxpr/ppermute | solution.py:245
  597.9 20.6 %collective-permute-start = (f32[2,32,256]{2,1,0:T(8,128)S(1)}, f32[2,32,256]{2,1,0:T(8,128)S(1)}, u32[]{:S(2)}, u32[]{:S(2)}) collective-permute-start(f32[2,32,256]{2,1,0:T(8,128)S(1)} %slice.77), channel_id=1, source_target_pairs={{0,32},{32,64},{64,96},{128,160},{160,192},{192,224},{256,288},{28... | collective-permute-start | bytes 196616 | tf_op jit(solution)/shard_map/while/body/eval_jaxpr/ppermute | solution.py:245
  604.4 19.0 %collective-permute-start.1 = (f32[2,32,256]{2,1,0:T(8,128)S(1)}, f32[2,32,256]{2,1,0:T(8,128)S(1)}, u32[]{:S(2)}, u32[]{:S(2)}) collective-permute-start(f32[2,32,256]{2,1,0:T(8,128)S(1)} %slice.78), channel_id=1, source_target_pairs={{0,32},{32,64},{64,96},{128,160},{160,192},{192,224},{256,288},{28... | collective-permute-start | bytes 196616 | tf_op jit(solution)/shard_map/while/body/eval_jaxpr/ppermute | solution.py:245
Sparse Core Ops, SparseCore 0:
  9.4 154.4 all-gather.9
